TPU v7x, 512 devices: a whole 4x8x8 slice. The times are simulated.
512 devices in a mesh: inst: 64 (over z_lo, y, core), tensor: 8 (over z_hi, x).
Axes of the slice: x: 4, y: 8, z: 8 (z_hi: 2, z_lo: 4; z = z_hi * 4 + z_lo), core: 2. Of those that a mesh axis runs over, the one named last changes fastest.
Arguments:
- query_first: bfloat16 [64, 8, 8192], P('inst', None, 'tensor')
- query_second: bfloat16 [64, 8, 8192], P('inst', None, 'tensor')
- hidden_first: bfloat16 [64, 8, 8192], P('inst', None, 'tensor'), may hold values from -6 to 6
- hidden_second: bfloat16 [64, 8, 8192], P('inst', None, 'tensor'), may hold values from -6 to 6
- fresh_first: bfloat16 [64, 8, 2, 1024], P('inst', None, None, 'tensor')
- fresh_second: bfloat16 [64, 8, 2, 1024], P('inst', None, None, 'tensor')
- kv_cache: bfloat16 [64, 8, 2, 1024, 1024], P('inst', None, None, None, 'tensor')
- adapters: bfloat16 [64, 4, 4, 16, 8192], P('inst', None, None, None, 'tensor')
- lengths: int32 [64, 8], replicated, may hold values from 1 to 1022, as said below
- adapter_ids: int32 [64, 8], replicated, may hold values from 0 to 3
- move_counts: int32 [64], replicated, may hold values from 0 to 4, as said below
- move_from: int32 [64, 4], replicated, may hold values from 0 to 7, as said below
- move_to: int32 [64, 4], replicated, may hold values from 0 to 7, as said below
Outputs:
- attn_first: bfloat16 [64, 8, 8192], P('inst', None, 'tensor')
- delta_first: bfloat16 [64, 8, 8192], P('inst', None, 'tensor')
- attn_second: bfloat16 [64, 8, 8192], P('inst', None, 'tensor')
- delta_second: bfloat16 [64, 8, 8192], P('inst', None, 'tensor')
Inputs may be any that keep to these rules, and one draw needn't show every extreme that they name: `move_counts`: of two partners i and i xor 64/2 at most one has a nonzero count; some instance hands over 4. `move_from`: the entries of one row are distinct slots. `move_to`: the entries of one row are distinct slots. `lengths`: some slot holds 1022 tokens.
All inputs are finite; a program needn't handle non-finite values.
Results may differ from a plain program's by a relative error of at most 0.013.
Values may be sent and summed in bfloat16 or wider, within the bound.
No kernel may reach another device: no remote copies, remote signals or barrier semaphores. Data moves between devices by JAX's collectives and lax.ppermute only.
A program may use at most 64 MiB of HBM per device.

v0:
```python
import math

import jax
import jax.numpy as jnp
from jax import lax
from jax.sharding import PartitionSpec as P

HEAD = 128


masked_score = -1e30


def swapped(block, axis, stride):
    count = lax.axis_size(axis)
    route = []
    for low in range(count):
        high = low | 1 << stride
        if high != low and high < count:
            route += [(low, high), (high, low)]
    return lax.ppermute(block, axis, route)


def attend(queries, stored_keys, stored_values, visible, extra_keys, extra_values, extra_visible):
    row_count = queries.shape[0]
    kv_heads = stored_keys.shape[-1] // HEAD
    group_size = queries.shape[-1] // stored_keys.shape[-1]
    scaling = 1.0 / math.sqrt(HEAD)
    grouped = queries.reshape(row_count, kv_heads, group_size, HEAD)
    keys_main = stored_keys.reshape(row_count, -1, kv_heads, HEAD)
    values_main = stored_values.reshape(row_count, -1, kv_heads, HEAD)
    keys_more = extra_keys.reshape(row_count, -1, kv_heads, HEAD)
    values_more = extra_values.reshape(row_count, -1, kv_heads, HEAD)
    scores_main = (
        jnp.einsum("rkgd,rckd->rkgc", grouped, keys_main, preferred_element_type=jnp.float32)
        * scaling
    )
    scores_more = (
        jnp.einsum("rkgd,rekd->rkge", grouped, keys_more, preferred_element_type=jnp.float32)
        * scaling
    )
    scores_main = jnp.where(visible[:, None, None, :], scores_main, masked_score)
    scores_more = jnp.where(extra_visible[:, None, None, :], scores_more, masked_score)
    largest = jnp.maximum(jnp.max(scores_main, -1), jnp.max(scores_more, -1))[..., None]
    weights_main = jnp.exp(scores_main - largest)
    weights_more = jnp.exp(scores_more - largest)
    denominator = jnp.sum(weights_main, -1, keepdims=True) + jnp.sum(
        weights_more, -1, keepdims=True
    )
    probs_main = (weights_main / denominator).astype(jnp.bfloat16)
    probs_more = (weights_more / denominator).astype(jnp.bfloat16)
    mixed = jnp.einsum(
        "rkgc,rckd->rkgd", probs_main, values_main, preferred_element_type=jnp.float32
    )
    mixed = mixed + jnp.einsum(
        "rkge,rekd->rkgd", probs_more, values_more, preferred_element_type=jnp.float32
    )
    return mixed.reshape(row_count, -1).astype(jnp.bfloat16)


def query_section(query_base, hidden, selector, tables):
    rank_part = jnp.einsum("rd,akd->rak", hidden, tables[:, 0], preferred_element_type=jnp.float32)
    rank_part = jnp.sum(rank_part * selector[:, :, None], 1)
    rank_value = lax.psum(rank_part, "tensor").astype(jnp.bfloat16)
    update = jnp.einsum("rk,akd->rad", rank_value, tables[:, 1], preferred_element_type=jnp.float32)
    update = jnp.sum(update * selector[:, :, None], 1)
    return (query_base.astype(jnp.float32) + update).astype(jnp.bfloat16)


def output_section(attended, selector, tables):
    rank_part = jnp.einsum(
        "rd,akd->rak", attended, tables[:, 2], preferred_element_type=jnp.float32
    )
    rank_part = jnp.sum(rank_part * selector[:, :, None], 1)
    rank_value = lax.psum(rank_part, "tensor").astype(jnp.bfloat16)
    update = jnp.einsum("rk,akd->rad", rank_value, tables[:, 3], preferred_element_type=jnp.float32)
    return jnp.sum(update * selector[:, :, None], 1).astype(jnp.bfloat16)


def per_device(
    query_first,
    query_second,
    hidden_first,
    hidden_second,
    fresh_first,
    fresh_second,
    kv_cache,
    adapters,
    lengths,
    adapter_ids,
    move_counts,
    move_from,
    move_to,
):
    inst_count = lax.axis_size("inst")
    own_index = lax.axis_index("inst")
    partner = jnp.bitwise_xor(own_index, inst_count // 2)
    swap_bit = inst_count.bit_length() - 2
    stored = kv_cache[0]
    tables = adapters[0]
    fresh_one = fresh_first[0]
    fresh_two = fresh_second[0]
    slot_total = stored.shape[0]
    pool_size = tables.shape[0]
    move_most = move_from.shape[1]
    slot_iota = jnp.arange(slot_total, dtype=jnp.int32)
    pool_iota = jnp.arange(pool_size, dtype=jnp.int32)
    positions = jnp.arange(stored.shape[2], dtype=jnp.int32)
    move_iota = jnp.arange(move_most, dtype=jnp.int32)
    own_length = lengths[own_index]
    own_ids = adapter_ids[own_index]
    selector_one = (own_ids[:, None] == pool_iota[None, :]).astype(jnp.float32)
    queries_one = query_section(query_first[0], hidden_first[0], selector_one, tables)
    attended_one = attend(
        queries_one,
        stored[:, 0],
        stored[:, 1],
        positions[None, :] < own_length[:, None],
        fresh_one[:, 0:1],
        fresh_one[:, 1:2],
        jnp.ones((slot_total, 1), bool),
    )
    update_one = output_section(attended_one, selector_one, tables)
    leaving = move_from[own_index]
    leaving_live = move_iota < move_counts[own_index]
    vacated = jnp.any((leaving[None, :] == slot_iota[:, None]) & leaving_live[None, :], 1)
    arriving_from = move_from[partner]
    arriving_live = move_iota < move_counts[partner]
    arrive = (move_to[partner][None, :] == slot_iota[:, None]) & arriving_live[None, :]
    incoming = jnp.any(arrive, 1)
    staying = jnp.logical_not(incoming)[:, None].astype(jnp.float32)
    arrive_float = arrive.astype(jnp.float32)
    arrive_half = arrive.astype(jnp.bfloat16)
    arriving_length = lengths[partner][arriving_from]
    out_stored = stored[leaving]
    out_fresh = fresh_one[leaving]
    keys_own = jnp.concatenate([fresh_one[:, 0:1], fresh_two[:, 0:1]], 1)
    values_own = jnp.concatenate([fresh_one[:, 1:2], fresh_two[:, 1:2]], 1)
    own_more_visible = jnp.stack([jnp.logical_not(vacated), jnp.ones((slot_total,), bool)], 1)
    own_visible = (positions[None, :] < own_length[:, None]) & jnp.logical_not(vacated)[:, None]
    moved_visible = jnp.ones((move_most, 2), bool)
    selector_two = jnp.concatenate([selector_one * staying, arrive_float], 1)
    out_tables = tables[own_ids[leaving]]
    got_stored, got_fresh, got_tables = swapped(
        (out_stored, out_fresh, out_tables), "inst", swap_bit
    )
    tables_two = jnp.concatenate([tables, got_tables], 0)
    queries_two = query_section(query_second[0], hidden_second[0], selector_two, tables_two)
    queries_moved = jnp.dot(arrive_half.T, queries_two, preferred_element_type=jnp.float32).astype(
        jnp.bfloat16
    )
    fresh_moved = jnp.einsum(
        "sm,sed->med", arrive_half, fresh_two, preferred_element_type=jnp.float32
    ).astype(jnp.bfloat16)
    keys_more = jnp.concatenate([got_fresh[:, 0:1], fresh_moved[:, 0:1]], 1)
    values_more = jnp.concatenate([got_fresh[:, 1:2], fresh_moved[:, 1:2]], 1)
    attended_moved = attend(
        queries_moved,
        got_stored[:, 0],
        got_stored[:, 1],
        positions[None, :] < arriving_length[:, None],
        keys_more,
        values_more,
        moved_visible,
    )
    attended_own = attend(
        queries_two, stored[:, 0], stored[:, 1], own_visible, keys_own, values_own, own_more_visible
    )
    placed = jnp.dot(arrive_half, attended_moved, preferred_element_type=jnp.float32).astype(
        jnp.bfloat16
    )
    attended_two = jnp.where(incoming[:, None], placed, attended_own)
    update_two = output_section(attended_two, selector_two, tables_two)
    return (attended_one[None], update_one[None], attended_two[None], update_two[None])


def solution(mesh):
    in_specs = (
        P("inst", None, "tensor"),
        P("inst", None, "tensor"),
        P("inst", None, "tensor"),
        P("inst", None, "tensor"),
        P("inst", None, None, "tensor"),
        P("inst", None, None, "tensor"),
        P("inst", None, None, None, "tensor"),
        P("inst", None, None, None, "tensor"),
        P(),
        P(),
        P(),
        P(),
        P(),
    )
    out_specs = (
        P("inst", None, "tensor"),
        P("inst", None, "tensor"),
        P("inst", None, "tensor"),
        P("inst", None, "tensor"),
    )
    return jax.shard_map(
        per_device, mesh=mesh, in_specs=in_specs, out_specs=out_specs, check_vma=False
    )
```

profile of v0, /device:TPU:66, one launch (start us, length us, event | category | flops | bytes accessed | tf_op | source)
XLA Modules:
  0.0 190.5 jit_solution(713164331809090948)
XLA Ops:
  0.7 1.0 dynamic-slice_reduce_fusion.4
  1.7 1.3 gather_fusion.4
  2.9 6.1 %collective-permute-start.2 = (bf16[4,2,128]{2,0,1:T(4,128)(2,1)S(1)}, bf16[4,2,128]{2,0,1:T(4,128)(2,1)S(1)}, u32[]{:S(2)}, u32[]{:S(2)}) collective-permute-start(bf16[4,2,128]{2,0,1:T(4,128)(2,1)S(1)} %copy.46), channel_id=1, source_target_pairs={{0,256},{256,0},{8,264},{264,8},{16,272},{272,16},{24,280},{280,24... | collective-permute-start | bytes 6152 | tf_op jit(solution)/shard_map/ppermute | solution.py:21
  9.0 1.0 dynamic-slice_reduce_fusion
  10.0 0.6 gather_fusion.1
  10.7 1.6 gather_fusion.2
  12.3 0.9 copy.44
  13.2 1.9 %collective-permute-start = (bf16[4,4,16,1024]{3,2,0,1:T(8,128)(2,1)}, bf16[4,4,16,1024]{3,2,0,1:T(8,128)(2,1)S(1)}, u32[]{:S(2)}, u32[]{:S(2)}) collective-permute-start(bf16[4,4,16,1024]{3,2,0,1:T(8,128)(2,1)} %copy.44), channel_id=1, source_target_pairs={{0,256},{256,0},{8,264},{264,8},{16,272},{272,16},{24,280},{280,24... | collective-permute-start | bytes 1572872 | tf_op jit(solution)/shard_map/ppermute | solution.py:21
  15.1 4.5 %copy.97 = bf16[1,8,2,1024,128]{4,3,1,2,0:T(8,128)(2,1)} copy(bf16[1,8,2,1024,128]{4,3,2,1,0:T(8,128)(2,1)} %param.19) | data formatting | bytes 8388608 | tf_op args[6]
  19.6 3.2 %gather_fusion.3 = bf16[4,2,1024,128]{3,2,1,0:T(8,128)(2,1)S(1)} fusion(bf16[8,2,1024,128]{3,2,0,1:T(8,128)(2,1)} %bitcast.177, s32[1024]{0:T(1024)S(1)} %pad_clamp_fusion.1), kind=kCustom, calls=%fused_computation.3 | custom fusion | bytes 4194320 | tf_op jit(solution)/shard_map/gather | solution.py:135
  22.8 4.8 %collective-permute-start.1 = (bf16[4,2,1024,128]{3,2,1,0:T(8,128)(2,1)S(1)}, bf16[4,2,1024,128]{3,2,1,0:T(8,128)(2,1)}, u32[]{:S(2)}, u32[]{:S(2)}) collective-permute-start(bf16[4,2,1024,128]{3,2,1,0:T(8,128)(2,1)S(1)} %gather_fusion.3), channel_id=1, source_target_pairs={{0,256},{256,0},{8,264},{264,8},{16,272},{272,16},{24,280},{280,24... | collective-permute-start | bytes 6291464 | tf_op jit(solution)/shard_map/ppermute | solution.py:21
  28.5 0.6 iota_compare_fusion.6
  29.4 1.1 copy.98
  30.5 0.7 iota_compare_fusion.5
  32.6 49.3 %collective-permute-done = bf16[4,4,16,1024]{3,2,0,1:T(8,128)(2,1)S(1)} collective-permute-done((bf16[4,4,16,1024]{3,2,0,1:T(8,128)(2,1)}, bf16[4,4,16,1024]{3,2,0,1:T(8,128)(2,1)S(1)}, u32[]{:S(2)}, u32[]{:S(2)}) %collective-permute-start) | collective-permute-done | bytes 524320 | tf_op jit(solution)/shard_map/ppermute | solution.py:21
  82.3 60.2 %all-reduce.2 = (bf16[8,16]{1,0:T(8,128)(2,1)S(1)}, bf16[8,16]{1,0:T(8,128)(2,1)S(1)}) all-reduce(f32[8,16]{1,0:T(8,128)S(1)} %fusion.23, f32[8,16]{1,0:T(8,128)S(1)} %fusion.18), channel_id=1, replica_groups=mesh['inst'=64,'tensor'=8] {'tensor'}, use_global_device_ids=true, to_apply=%region_1.0 | all-reduce | flops 256 | bytes 1536 | tf_op jit(solution)/shard_map/psum | solution.py:64
  142.9 2.3 %fusion.116 = (f32[8,8]{1,0:T(8,128)S(1)}, f32[8,8,1024]{2,1,0:T(8,128)S(1)}) fusion(bf16[8,8,128]{2,1,0:T(8,128)(2,1)S(1)} %fusion.51, bf16[8,2,1024,128]{3,2,0,1:T(8,128)(2,1)} %bitcast.178, pred[8,1024]{1,0:T(8,128)(4,1)S(1)} %get-tuple-element.26), kind=kOutput, calls=%fused_computation.193 | convolution fusion | flops 16973760 | bytes 2384128 | tf_op jit(solution)/shard_map/rkgd,rckd->rkgc/dot_general | solution.py:35
  145.4 2.0 %fusion.17 = bf16[8,8,128]{2,1,0:T(8,128)(2,1)S(1)} fusion(bf16[8,2,1024,128]{3,2,0,1:T(8,128)(2,1)} %bitcast.179, f32[8,8,1024]{2,1,0:T(8,128)S(1)} %get-tuple-element.32, f32[8,8]{1,0:T(8,128)S(1)} %get-tuple-element.15, f32[8,8]{1,0:T(8,128)S(1)} %multiply_maximum_fusion, f32[8,128]{1,0:T(8,128)S(1)} %bitcast.202, f32[8,8]{1,0:T(8,128)S(1)} %get-tuple-element.14), kind=kOutput, calls=%fused_computation.38 | convolution fusion | flops 16998400 | bytes 2380544 | tf_op jit(solution)/shard_map/rkgc,rckd->rkgd/dot_general | solution.py:52
  148.4 2.5 %fusion.117 = (f32[8,8]{1,0:T(8,128)S(1)}, f32[8,8,1024]{2,1,0:T(8,128)S(1)}) fusion(bf16[8,8,128]{2,1,0:T(8,128)(2,1)S(1)} %fusion.52, bf16[8,2,1024,128]{3,2,0,1:T(8,128)(2,1)} %bitcast.180, pred[8,1024]{1,0:T(8,128)(4,1)S(1)} %get-tuple-element.25), kind=kOutput, calls=%fused_computation.194 | convolution fusion | flops 16973760 | bytes 2384128 | tf_op jit(solution)/shard_map/rkgd,rckd->rkgc/dot_general | solution.py:35
  152.4 1.7 fusion.119
  154.5 1.5 fusion.26
  156.6 32.4 %all-reduce.1 = (bf16[8,16]{1,0:T(8,128)(2,1)S(1)}, bf16[8,16]{1,0:T(8,128)(2,1)S(1)}) all-reduce(f32[8,16]{1,0:T(8,128)S(1)} %fusion.24, f32[8,16]{1,0:T(8,128)S(1)} %fusion.19), channel_id=1, replica_groups=mesh['inst'=64,'tensor'=8] {'tensor'}, use_global_device_ids=true, to_apply=%region_6.7 | all-reduce | flops 256 | bytes 1536 | tf_op jit(solution)/shard_map/psum | solution.py:75
  189.0 0.8 fusion.12
  189.8 0.8 fusion.9
  (81 shorter events, 6.8 us)
Async XLA Ops:
  0.6 31.5 %copy-start = (bf16[1,8,1024]{2,1,0:T(8,128)(2,1)S(1)}, bf16[1,8,1024]{2,1,0:T(8,128)(2,1)}, u32[]{:S(2)}) copy-start(bf16[1,8,1024]{2,1,0:T(8,128)(2,1)} %param.15) | copy-start | bytes 49156
  2.9 29.6 %collective-permute-start.2 = (bf16[4,2,128]{2,0,1:T(4,128)(2,1)S(1)}, bf16[4,2,128]{2,0,1:T(4,128)(2,1)S(1)}, u32[]{:S(2)}, u32[]{:S(2)}) collective-permute-start(bf16[4,2,128]{2,0,1:T(4,128)(2,1)S(1)} %copy.46), channel_id=1, source_target_pairs={{0,256},{256,0},{8,264},{264,8},{16,272},{272,16},{24,280},{280,24... | collective-permute-start | bytes 6152 | tf_op jit(solution)/shard_map/ppermute | solution.py:21
  13.2 68.8 %collective-permute-start = (bf16[4,4,16,1024]{3,2,0,1:T(8,128)(2,1)}, bf16[4,4,16,1024]{3,2,0,1:T(8,128)(2,1)S(1)}, u32[]{:S(2)}, u32[]{:S(2)}) collective-permute-start(bf16[4,4,16,1024]{3,2,0,1:T(8,128)(2,1)} %copy.44), channel_id=1, source_target_pairs={{0,256},{256,0},{8,264},{264,8},{16,272},{272,16},{24,280},{280,24... | collective-permute-start | bytes 1572872 | tf_op jit(solution)/shard_map/ppermute | solution.py:21
  19.6 8.1 %copy-start.9 = (s32[64,4]{0,1:T(4,128)S(1)}, s32[64,4]{0,1:T(4,128)}, u32[]{:S(2)}) copy-start(s32[64,4]{0,1:T(4,128)} %param.25) | copy-start | bytes 3076
  19.6 8.3 %copy-start.8 = (s32[64]{0:T(128)S(1)}, s32[64]{0:T(128)}, u32[]{:S(2)}) copy-start(s32[64]{0:T(128)} %param.23) | copy-start | bytes 772
  19.6 9.6 %copy-start.7 = (bf16[1,8,2,128]{3,2,1,0:T(2,128)(2,1)S(1)}, bf16[1,8,2,128]{3,2,1,0:T(2,128)(2,1)}, u32[]{:S(2)}) copy-start(bf16[1,8,2,128]{3,2,1,0:T(2,128)(2,1)} %param.18) | copy-start | bytes 12292
  19.6 9.8 %copy-start.3 = (bf16[1,8,2,128]{3,2,1,0:T(2,128)(2,1)S(1)}, bf16[1,8,2,128]{3,2,1,0:T(2,128)(2,1)}, u32[]{:S(2)}) copy-start(bf16[1,8,2,128]{3,2,1,0:T(2,128)(2,1)} %param.17) | copy-start | bytes 12292
  19.6 12.4 %copy-start.6 = (bf16[1,8,1024]{2,1,0:T(8,128)(2,1)S(1)}, bf16[1,8,1024]{2,1,0:T(8,128)(2,1)}, u32[]{:S(2)}) copy-start(bf16[1,8,1024]{2,1,0:T(8,128)(2,1)} %param.13) | copy-start | bytes 49156
  19.6 12.4 %copy-start.2 = (bf16[1,8,1024]{2,1,0:T(8,128)(2,1)S(1)}, bf16[1,8,1024]{2,1,0:T(8,128)(2,1)}, u32[]{:S(2)}) copy-start(bf16[1,8,1024]{2,1,0:T(8,128)(2,1)} %param.14) | copy-start | bytes 49156
  19.6 62.3 %copy-start.4 = (bf16[1,8,1024]{2,1,0:T(8,128)(2,1)S(1)}, bf16[1,8,1024]{2,1,0:T(8,128)(2,1)}, u32[]{:S(2)}) copy-start(bf16[1,8,1024]{2,1,0:T(8,128)(2,1)} %param.16) | copy-start | bytes 49156
  22.8 129.5 %collective-permute-start.1 = (bf16[4,2,1024,128]{3,2,1,0:T(8,128)(2,1)S(1)}, bf16[4,2,1024,128]{3,2,1,0:T(8,128)(2,1)}, u32[]{:S(2)}, u32[]{:S(2)}) collective-permute-start(bf16[4,2,1024,128]{3,2,1,0:T(8,128)(2,1)S(1)} %gather_fusion.3), channel_id=1, source_target_pairs={{0,256},{256,0},{8,264},{264,8},{16,272},{272,16},{24,280},{280,24... | collective-permute-start | bytes 6291464 | tf_op jit(solution)/shard_map/ppermute | solution.py:21
  148.1 3.8 %copy-start.1 = (bf16[1,8,2,1024,128]{4,3,1,2,0:T(8,128)(2,1)S(1)}, bf16[1,8,2,1024,128]{4,3,1,2,0:T(8,128)(2,1)}, u32[]{:S(2)}) copy-start(bf16[1,8,2,1024,128]{4,3,1,2,0:T(8,128)(2,1)} %copy.97) | copy-start | bytes 12582916
  156.2 34.3 %copy-start.5 = (bf16[8,1024]{1,0:T(8,128)(2,1)}, bf16[8,1024]{1,0:T(8,128)(2,1)S(1)}, u32[]{:S(2)}) copy-start(bf16[8,1024]{1,0:T(8,128)(2,1)S(1)} %fusion.20) | copy-start | bytes 49156
where the time goes:
time: 191 us
  blocking collectives  92.6 us (48%)
  waiting for transfers between devices  49.3 us (26%)
  local copies, waits for them, and re-layouts  17.4 us (9%)
  matrix products  14.9 us (8%)
  starting transfers between devices  12.8 us (7%)
  other arithmetic  2.48 us (1%)
    psum x1, blocking collectives, query_section(): rank_value = lax.psum(rank_part, 'tensor').astype(jnp.bfloat16)  60.2 us
    ppermute x3, waiting for transfers between devices, swapped(): return lax.ppermute(block, axis, route)  49.3 us
    psum x1, blocking collectives, output_section(): rank_value = lax.psum(rank_part, 'tensor').astype(jnp.bfloat16)  32.4 us
    ppermute x3, starting transfers between devices, swapped(): return lax.ppermute(block, axis, route)  12.8 us
    dot_general x3, matrix products, attend(): jnp.einsum('rkgd,rckd->rkgc', grouped, keys_main, preferred_element_type=...  6.51 us
    unnamed x23, local copies, waits for them, and re-layouts  5.75 us
    dot_general x3, matrix products, attend(): jnp.einsum('rkgc,rckd->rkgd', probs_main, values_main, preferred_element_...  4.01 us
  transfers between devices with their start and end apart: 3, of which 1 were waited for; matrix products, arithmetic and copies ran while one was open for 14% of the time, Pallas kernels for 0%

commit v1 on v0

v1 whole, which is shorter than its diff:
```python
import math

import jax
import jax.numpy as jnp
from jax import lax
from jax.experimental import pallas as pl
from jax.experimental.pallas import tpu as pltpu
from jax.sharding import PartitionSpec as P

HEAD = 128
masked_score = -1e30
f32 = jnp.float32
bf16 = jnp.bfloat16


def dot_t(a, b):
    return lax.dot_general(a, b, (((1,), (1,)), ((), ())), preferred_element_type=f32)


def dot(a, b):
    return lax.dot_general(a, b, (((1,), (0,)), ((), ())), preferred_element_type=f32)


def twice(table):
    flat = table.reshape(-1, table.shape[-1])
    return jnp.concatenate([flat, flat], 0)


def row_iota(shape):
    return lax.broadcasted_iota(jnp.int32, shape, 0)


def lane_iota(shape):
    return lax.broadcasted_iota(jnp.int32, shape, 1)


def own_adapter(ids, me, slots, lanes, rank):
    rows, columns = row_iota((slots, lanes)), lane_iota((slots, lanes))
    adapter = jnp.zeros((slots, lanes), jnp.int32)
    for s in range(slots):
        adapter = jnp.where(rows == s, ids[me, s], adapter)
    return lax.rem(columns, lanes // 2) // rank == adapter


def moved_in(base, rows_at, counts, targets, sources, me, other):
    row = row_iota(base.shape)
    for m in range(targets.shape[1]):
        picked = rows_at[pl.ds(sources[other, m], 1), :]
        live = m < counts[other]
        base = jnp.where((row == targets[other, m]) & live, picked, base)
    return base


def is_row(shape, counts, table, instance):
    row = row_iota(shape)
    found = jnp.zeros(shape, jnp.bool_)
    for m in range(table.shape[1]):
        found = found | ((row == table[instance, m]) & (m < counts[instance]))
    return found


def rank_kernel(ids, counts, leave, land, h1, h2, h2_other, down, out, scratch):
    me = lax.axis_index("inst")
    peers, slots, lanes = out.shape
    rank = down.shape[2]
    table = twice(down[:, 0])
    first = dot_t(h1[...], table)
    second = dot_t(h2[...], table)
    scratch[...] = dot_t(h2_other[...], table)
    second = moved_in(second, scratch, counts, leave, land, me, me)
    both = jnp.where(lane_iota((slots, lanes)) < lanes // 2, first, second)
    both = jnp.where(own_adapter(ids, me, slots, lanes, rank), both, 0.0)
    for peer in range(peers):
        out[peer] = both


def attention_kernel(
    lengths, ids, counts, leave, land,
    ranks, base1, pack_own, pack_other, fresh1, up, down, cache,
    attn1_out, attn2_out, send_out, ranks_out,
    kv, other_rows, queries, mixed, second_rows, rank_rows, sems,
):
    me = lax.axis_index("inst")
    half = lax.axis_size("inst") // 2
    slots, width = base1.shape
    heads = width // HEAD
    cached = cache.shape[2]
    lanes = ranks.shape[2]
    rank = up.shape[2]
    copies = [pltpu.make_async_copy(cache.at[s], kv.at[s], sems.at[s]) for s in range(slots)]
    for copy in copies:
        copy.start()

    lane = lane_iota((slots, lanes))
    low = lane < lanes // 2
    total = ranks[0]
    for peer in range(1, ranks.shape[0]):
        total = total + ranks[peer]
    total = jnp.concatenate([jnp.where(low, total, 0.0), jnp.where(low, 0.0, total)], 0).astype(bf16)
    update = dot(total, twice(up[:, 0]))
    other_rows[...] = pack_other[...].astype(f32)
    own = pack_own[...].astype(f32)
    second = moved_in(own, other_rows, counts, leave, land, me, me)
    query1 = (base1[...].astype(f32) + update[:slots]).astype(bf16).astype(f32)
    query2 = (second[:, :width] + update[slots:]).astype(bf16).astype(f32)
    for h in range(heads):
        columns = slice(h * HEAD, (h + 1) * HEAD)
        queries[h, :slots] = query1[:, columns]
        queries[h, slots:] = query2[:, columns]
    key1 = fresh1[:, :HEAD].astype(f32)
    value1 = fresh1[:, HEAD:].astype(f32)
    key2 = second[:, width : width + HEAD]
    value2 = second[:, width + HEAD :]

    scaling = 1.0 / math.sqrt(HEAD)
    score_shape = (2 * heads, cached)
    position = lane_iota(score_shape)
    extra = (position == cached - 2) | ((position == cached - 1) & (row_iota(score_shape) >= heads))
    last = pl.ds(cached - 16, 16)
    tail_row = row_iota((16, HEAD))

    def with_fresh(tile, one, two):
        tile = jnp.where(tail_row == 14, one, tile.astype(f32))
        return jnp.where(tail_row == 15, two, tile).astype(bf16)

    for s in range(slots):
        copies[s].wait()
        row = slice(s, s + 1)
        kv[s, 0, last, :] = with_fresh(kv[s, 0, last, :], key1[row], key2[row])
        kv[s, 1, last, :] = with_fresh(kv[s, 1, last, :], value1[row], value2[row])
        query = jnp.concatenate([queries[:, s, :], queries[:, slots + s, :]], 0).astype(bf16)
        scores = dot_t(query, kv[s, 0]) * scaling
        scores = jnp.where((position < lengths[me, s]) | extra, scores, masked_score)
        weights = jnp.exp(scores - jnp.max(scores, 1, keepdims=True))
        probs = (weights / jnp.sum(weights, 1, keepdims=True)).astype(bf16)
        attended = dot(probs, kv[s, 1]).astype(bf16).astype(f32)
        mixed[0, s] = attended[:heads]
        mixed[1, s] = attended[heads:]

    vacated = is_row((slots, HEAD), counts, leave, me)
    fresh_value = own[:, width + HEAD :]
    for h in range(heads):
        columns = slice(h * HEAD, (h + 1) * HEAD)
        attn1_out[:, columns] = mixed[0, :, h, :].astype(bf16)
        served = mixed[1, :, h, :]
        second_rows[:, columns] = served
        attn2_out[:, columns] = jnp.where(vacated, fresh_value, served).astype(bf16)

    table = twice(down[:, 0])
    mask = own_adapter(ids, me, slots, lanes, rank)
    rank1 = jnp.where(mask, dot_t(attn1_out[...], table), 0.0)
    rank2 = jnp.where(mask, dot_t(attn2_out[...], table), 0.0)
    served_rows = second_rows[...]
    rank_rows[...] = jnp.where(mask, dot_t(served_rows.astype(bf16), table), 0.0)
    send_out[...] = moved_in(served_rows, second_rows, counts, land, leave, me, me).astype(bf16)
    for_own = jnp.where(low, rank1, rank2)
    for_other = moved_in(jnp.zeros_like(for_own), rank_rows, counts, land, leave, me, me)
    peers = ranks_out.shape[0] // 2
    lower = me < half
    for peer in range(peers):
        ranks_out[peer] = jnp.where(lower, for_own, for_other)
        ranks_out[peers + peer] = jnp.where(lower, for_other, for_own)


def delta_kernel(counts, land, ranks, up, up_other, attn2_own, attn2_other, delta1_out, delta2_out, attn2_out):
    me = lax.axis_index("inst")
    half = lax.axis_size("inst") // 2
    other = jnp.bitwise_xor(me, half)
    peers = ranks.shape[0] // 2
    _, slots, lanes = ranks.shape
    sums = []
    for part in range(2):
        total = ranks[part * peers]
        for peer in range(1, peers):
            total = total + ranks[part * peers + peer]
        sums.append(total)
    lower = me < half
    own = jnp.where(lower, sums[0], sums[1])
    got = jnp.where(lower, sums[1], sums[0])
    low = lane_iota((slots, lanes)) < lanes // 2
    incoming = is_row((slots, lanes), counts, land, other)
    rank1 = jnp.where(low, own, 0.0)
    rank2 = jnp.where(low, pltpu.roll(own, lanes // 2, 1), got)
    rank2 = jnp.where(incoming == low, 0.0, rank2)
    table = jnp.concatenate([up[:, 0].reshape(-1, up.shape[3]), up_other[...]], 0)
    delta = dot(jnp.concatenate([rank1, rank2], 0).astype(bf16), table).astype(bf16)
    delta1_out[...] = delta[:slots]
    delta2_out[...] = delta[slots:]
    incoming = is_row(attn2_out.shape, counts, land, other)
    attn2_out[...] = jnp.where(incoming, attn2_other[...].astype(f32), attn2_own[...].astype(f32)).astype(bf16)


def per_device(
    query_first,
    query_second,
    hidden_first,
    hidden_second,
    fresh_first,
    fresh_second,
    kv_cache,
    adapters,
    lengths,
    adapter_ids,
    move_counts,
    move_from,
    move_to,
):
    inst_count = lax.axis_size("inst")
    peers = lax.axis_size("tensor")
    half = inst_count // 2
    swap = [(i, i ^ half) for i in range(inst_count)]
    groups = [
        [i * peers + t for t in range(peers)] + [(i + half) * peers + t for t in range(peers)] for i in range(half)
    ]
    _, slots, width = query_first.shape
    tables = adapters[0]
    pool, _, rank, _ = tables.shape
    lanes = 2 * pool * rank
    heads = width // HEAD
    cached = kv_cache.shape[3]

    smem = pl.BlockSpec(memory_space=pltpu.SMEM)
    vmem = pl.BlockSpec(memory_space=pltpu.VMEM)
    anywhere = pl.BlockSpec(memory_space=pl.ANY)

    def part(which):
        return pl.BlockSpec((pool, 1, rank, width), lambda step: (0, which, 0, 0))

    def shape(dims, dtype):
        return jax.ShapeDtypeStruct(dims, dtype)

    hidden_other = lax.ppermute(hidden_second[0], "inst", swap)
    pack_own = jnp.concatenate([query_second[0], fresh_second[0].reshape(slots, 2 * HEAD)], 1)
    pack_other = lax.ppermute(pack_own, "inst", swap)
    fresh1 = fresh_first[0].reshape(slots, 2 * HEAD)

    ranks = pl.pallas_call(
        rank_kernel,
        name="rank_partials",
        grid=(1,),
        out_shape=shape((peers, slots, lanes), f32),
        in_specs=[smem] * 4 + [vmem] * 3 + [part(0)],
        out_specs=vmem,
        scratch_shapes=[pltpu.VMEM((slots, lanes), f32)],
    )(adapter_ids, move_counts, move_from, move_to, hidden_first[0], hidden_second[0], hidden_other, tables)
    ranks = lax.all_to_all(ranks, "tensor", 0, 0)

    up_other = lax.ppermute(tables[:, 3].reshape(pool * rank, width), "inst", swap)

    attn1, attn2_own, attn2_send, ranks_two = pl.pallas_call(
        attention_kernel,
        name="attention",
        grid=(1,),
        out_shape=(
            shape((slots, width), bf16),
            shape((slots, width), bf16),
            shape((slots, width), bf16),
            shape((2 * peers, slots, lanes), f32),
        ),
        in_specs=[smem] * 5 + [vmem] * 5 + [part(1), part(2), anywhere],
        out_specs=(vmem,) * 4,
        scratch_shapes=[
            pltpu.VMEM((slots, 2, cached, HEAD), bf16),
            pltpu.VMEM((slots, width + 2 * HEAD), f32),
            pltpu.VMEM((heads, 2 * slots, HEAD), f32),
            pltpu.VMEM((2, slots, heads, HEAD), f32),
            pltpu.VMEM((slots, width), f32),
            pltpu.VMEM((slots, lanes), f32),
            pltpu.SemaphoreType.DMA((slots,)),
        ],
        compiler_params=pltpu.CompilerParams(vmem_limit_bytes=16 * 1024 * 1024),
    )(
        lengths, adapter_ids, move_counts, move_from, move_to,
        ranks, query_first[0], pack_own, pack_other, fresh1, tables, tables, kv_cache[0],
    )
    ranks_two = lax.all_to_all(ranks_two, ("inst", "tensor"), 0, 0, axis_index_groups=groups)
    attn2_other = lax.ppermute(attn2_send, "inst", swap)

    delta1, delta2, attn2 = pl.pallas_call(
        delta_kernel,
        name="deltas",
        grid=(1,),
        out_shape=(shape((slots, width), bf16),) * 3,
        in_specs=[smem] * 2 + [vmem, part(3)] + [vmem] * 3,
        out_specs=(vmem,) * 3,
    )(move_counts, move_to, ranks_two, tables, up_other, attn2_own, attn2_other)
    return (attn1[None], delta1[None], attn2[None], delta2[None])


def solution(mesh):
    row = P("inst", None, "tensor")
    fresh = P("inst", None, None, "tensor")
    whole = P("inst", None, None, None, "tensor")
    return jax.shard_map(
        per_device,
        mesh=mesh,
        in_specs=(row, row, row, row, fresh, fresh, whole, whole, P(), P(), P(), P(), P()),
        out_specs=(row, row, row, row),
        check_vma=False,
    )
```

time: 191 us -> 75.7 us (0.40)
  the two profiles are of different devices: /device:TPU:66 before, /device:TPU:24 now
where the time goes in v1:
time: 75.7 us; the launch traced here: 74.7 us
  starting transfers between devices  37.9 us (50%)
  local copies, waits for them, and re-layouts  15.9 us (21%)
  Pallas kernels  13.7 us (18%)
  waiting for transfers between devices  5.76 us (8%)
    unnamed x30, local copies, waits for them, and re-layouts  15 us
    all_to_all x1, starting transfers between devices, per_device(): ranks = lax.all_to_all(ranks, 'tensor', 0, 0)  10.9 us
    all_to_all x1, starting transfers between devices, per_device(): lax.all_to_all(ranks_two, ('inst', 'tensor'), 0, 0, axis_index_groups=gro...  9.41 us
    pallas_call x1, Pallas kernels, per_device(): pl.pallas_call(attention_kernel, name='attention', grid=(1,), out_shape=(...  8.3 us
    ppermute x1, starting transfers between devices, per_device(): hidden_other = lax.ppermute(hidden_second[0], 'inst', swap)  6.09 us
    ppermute x1, starting transfers between devices, per_device(): attn2_other = lax.ppermute(attn2_send, 'inst', swap)  4.72 us
    ppermute x1, starting transfers between devices, per_device(): lax.ppermute(tables[:, 3].reshape(pool * rank, width), 'inst', swap)  4.29 us
    all_to_all x1, waiting for transfers between devices, per_device(): lax.all_to_all(ranks_two, ('inst', 'tensor'), 0, 0, axis_index_groups=gro...  3.64 us
  transfers between devices with their start and end apart: 6, of which 3 were waited for; matrix products, arithmetic and copies ran while one was open for 11% of the time, Pallas kernels for 11%

profile of v1, /device:TPU:24, one launch (start us, length us, event | category | flops | bytes accessed | tf_op | source)
XLA Modules:
  0.0 74.7 jit_solution(6644447585469864424)
XLA Ops:
  0.6 6.1 %collective-permute-start = (bf16[8,1024]{1,0:T(8,128)(2,1)}, bf16[8,1024]{1,0:T(8,128)(2,1)S(1)}, u32[]{:S(2)}, u32[]{:S(2)}) collective-permute-start(bf16[8,1024]{1,0:T(8,128)(2,1)} %bitcast.31), channel_id=1, source_target_pairs={{0,256},{8,264},{16,272},{24,280},{32,288},{40,296},{48,304},{56,3... | collective-permute-start | bytes 49160 | tf_op jit(solution)/shard_map/ppermute | solution.py:232
  7.4 1.4 %copy.23.land = s32[64,4]{1,0:T(8,128)} copy(s32[64,4]{0,1:T(4,128)} %param.25) | data formatting | bytes 2048 | tf_op args[12]
  8.8 1.4 %copy.21.ids = s32[64,8]{1,0:T(8,128)} copy(s32[64,8]{0,1:T(8,128)} %param.22) | data formatting | bytes 4096 | tf_op args[9]
  10.2 1.4 %copy.22.leave = s32[64,4]{1,0:T(8,128)} copy(s32[64,4]{0,1:T(4,128)} %param.24) | data formatting | bytes 2048 | tf_op args[11]
  12.2 3.4 %rank_partials.1 = f32[8,8,128]{2,1,0:T(8,128)} custom-call(s32[64,8]{1,0:T(8,128)} %copy.21.ids, s32[64]{0:T(128)} %counts.5, s32[64,4]{1,0:T(8,128)} %copy.22.leave, s32[64,4]{1,0:T(8,128)} %copy.23.land, bf16[8,1024]{1,0:T(8,128)(2,1)} %bitcast.30, bf16[8,1024]{1,0:T(8,128)(2,1)} %bitcast.32, bf16[8,1024]{1,0:T(8,128)(2,1)} %copy-done.11, ...), custom_call_target="tpu_custom_call" | custom-call | tf_op jit(solution)/shard_map/rank_partials/pallas_call | solution.py:237
  15.5 10.9 %all-to-all-start = ((f32[8,8,128]{2,1,0:T(8,128)}), f32[8,8,128]{2,1,0:T(8,128)S(1)}, u32[]{:S(2)}, u32[]{:S(2)}) async-start(f32[8,8,128]{2,1,0:T(8,128)} %rank_partials.1), calls=%async_computation | async-start | bytes 65536 | tf_op jit(solution)/shard_map/all_to_all | solution.py:246
  26.4 0.7 pad_maximum_fusion.pack_own
  27.2 2.4 %collective-permute-start.1 = (bf16[8,1280]{1,0:T(8,128)(2,1)S(1)}, bf16[8,1280]{1,0:T(8,128)(2,1)S(1)}, u32[]{:S(2)}, u32[]{:S(2)}) collective-permute-start(bf16[8,1280]{1,0:T(8,128)(2,1)S(1)} %pad_maximum_fusion.pack_own), channel_id=1, source_target_pairs={{0,256},{8,264},{16,272},{24,280},{32,288},{40,296},{48,304},{56,3... | collective-permute-start | bytes 61448 | tf_op jit(solution)/shard_map/ppermute | solution.py:234
  29.6 0.9 %slice.4 = bf16[4,1,16,1024]{3,2,1,0:T(8,128)(2,1)S(1)} slice(bf16[4,4,16,1024]{3,2,1,0:T(8,128)(2,1)} %bitcast.22), slice={[0:4], [3:4], [0:16], [0:1024]} | slice | bytes 262144 | tf_op jit(solution)/shard_map/slice | solution.py:248
  30.5 4.3 %collective-permute-start.2 = (bf16[64,1024]{1,0:T(8,128)(2,1)S(1)}, bf16[64,1024]{1,0:T(8,128)(2,1)S(1)}, u32[]{:S(2)}, u32[]{:S(2)}) collective-permute-start(bf16[64,1024]{1,0:T(8,128)(2,1)S(1)} %bitcast.29), channel_id=1, source_target_pairs={{0,256},{8,264},{16,272},{24,280},{32,288},{40,296},{48,304},{56,3... | collective-permute-start | bytes 393224 | tf_op jit(solution)/shard_map/ppermute | solution.py:248
  34.8 0.7 copy.29
  35.5 0.8 %copy.20.lengths = s32[64,8]{1,0:T(8,128)S(1)} copy(s32[64,8]{0,1:T(8,128)} %param.21) | data formatting | bytes 4096 | tf_op args[8]
  36.6 1.0 %copy-done = bf16[1,4,4,16,1024]{4,3,2,1,0:T(8,128)(2,1)S(1)} copy-done((bf16[1,4,4,16,1024]{4,3,2,1,0:T(8,128)(2,1)S(1)}, bf16[1,4,4,16,1024]{4,3,2,1,0:T(8,128)(2,1)}, u32[]{:S(2)}) %copy-start) | copy-done | bytes 524312
  37.7 2.2 %copy-done.1 = bf16[1,8,2,1024,128]{4,3,2,1,0:T(8,128)(2,1)S(1)} copy-done((bf16[1,8,2,1024,128]{4,3,2,1,0:T(8,128)(2,1)S(1)}, bf16[1,8,2,1024,128]{4,3,2,1,0:T(8,128)(2,1)}, u32[]{:S(2)}) %copy-start.1) | copy-done | bytes 4194328
  39.8 0.8 %copy-done.2 = s32[64,4]{1,0:T(8,128)S(1)} copy-done((s32[64,4]{1,0:T(8,128)S(1)}, s32[64,4]{1,0:T(8,128)}, u32[]{:S(2)}) %copy-start.2) | copy-done | bytes 1048
  40.6 0.8 %copy-done.3 = s32[64,8]{1,0:T(8,128)S(1)} copy-done((s32[64,8]{1,0:T(8,128)S(1)}, s32[64,8]{1,0:T(8,128)}, u32[]{:S(2)}) %copy-start.3) | copy-done | bytes 2072
  41.4 0.8 %copy-done.4 = s32[64,4]{1,0:T(8,128)S(1)} copy-done((s32[64,4]{1,0:T(8,128)S(1)}, s32[64,4]{1,0:T(8,128)}, u32[]{:S(2)}) %copy-start.4) | copy-done | bytes 1048
  42.1 0.7 copy-done.5
  43.5 8.3 %attention.1 = (bf16[8,1024]{1,0:T(8,128)(2,1)}, bf16[8,1024]{1,0:T(8,128)(2,1)S(1)}, bf16[8,1024]{1,0:T(8,128)(2,1)S(1)}, f32[16,8,128]{2,1,0:T(8,128)}) custom-call(s32[64,8]{1,0:T(8,128)S(1)} %copy.20.lengths, s32[64,8]{1,0:T(8,128)S(1)} %copy-done.3, s32[64]{0:T(128)S(1)} %copy-done.7, s32[64,4]{1,0:T(8,128)S(1)} %copy-done.4, s32[64,4]{1,0:T(8,128)S(1)} %copy-done.2, ...), custom_call_target="tpu_custom_call" | custom-call | tf_op jit(solution)/shard_map/attention/pallas_call | solution.py:250
  52.4 9.4 %all-to-all-start.1 = ((f32[16,8,128]{2,1,0:T(8,128)}), f32[16,8,128]{2,1,0:T(8,128)S(1)}, u32[]{:S(2)}, u32[]{:S(2)}) async-start(f32[16,8,128]{2,1,0:T(8,128)} %get-tuple-element.12), calls=%async_computation.1 | async-start | bytes 131072 | tf_op jit(solution)/shard_map/all_to_all | solution.py:276
  61.8 4.7 %collective-permute-start.3 = (bf16[8,1024]{1,0:T(8,128)(2,1)S(1)}, bf16[8,1024]{1,0:T(8,128)(2,1)S(1)}, u32[]{:S(2)}, u32[]{:S(2)}) collective-permute-start(bf16[8,1024]{1,0:T(8,128)(2,1)S(1)} %get-tuple-element.14), channel_id=1, source_target_pairs={{0,256},{8,264},{16,272},{24,280},{32,288},{40,296},{48,304},{56,3... | collective-permute-start | bytes 49160 | tf_op jit(solution)/shard_map/ppermute | solution.py:277
  66.6 1.8 %collective-permute-done.3.attn2_other = bf16[8,1024]{1,0:T(8,128)(2,1)S(1)} collective-permute-done((bf16[8,1024]{1,0:T(8,128)(2,1)S(1)}, bf16[8,1024]{1,0:T(8,128)(2,1)S(1)}, u32[]{:S(2)}, u32[]{:S(2)}) %collective-permute-start.3) | collective-permute-done | bytes 16416 | tf_op jit(solution)/shard_map/ppermute | solution.py:277
  68.4 3.6 %all-to-all-done.1.ranks = f32[16,8,128]{2,1,0:T(8,128)S(1)} async-done(((f32[16,8,128]{2,1,0:T(8,128)}), f32[16,8,128]{2,1,0:T(8,128)S(1)}, u32[]{:S(2)}, u32[]{:S(2)}) %all-to-all-start.1) | async-done | bytes 65568 | tf_op jit(solution)/shard_map/all_to_all | solution.py:276
  72.6 2.0 %deltas.1 = (bf16[8,1024]{1,0:T(8,128)(2,1)}, bf16[8,1024]{1,0:T(8,128)(2,1)}, bf16[8,1024]{1,0:T(8,128)(2,1)}) custom-call(s32[64]{0:T(128)} %counts.5, s32[64,4]{1,0:T(8,128)} %copy.23.land, f32[16,8,128]{2,1,0:T(8,128)} %copy-done.8, bf16[4,4,16,1024]{3,2,1,0:T(8,128)(2,1)} %bitcast.23, bf16[64,1024]{1,0:T(8,128)(2,1)} %copy-done.9, ...), custom_call_target="tpu_custom_call" | custom-call | tf_op jit(solution)/shard_map/deltas/pallas_call | solution.py:279
  (23 shorter events, 3.5 us)
Async XLA Ops:
  0.6 10.9 %collective-permute-start = (bf16[8,1024]{1,0:T(8,128)(2,1)}, bf16[8,1024]{1,0:T(8,128)(2,1)S(1)}, u32[]{:S(2)}, u32[]{:S(2)}) collective-permute-start(bf16[8,1024]{1,0:T(8,128)(2,1)} %bitcast.31), channel_id=1, source_target_pairs={{0,256},{8,264},{16,272},{24,280},{32,288},{40,296},{48,304},{56,3... | collective-permute-start | bytes 49160 | tf_op jit(solution)/shard_map/ppermute | solution.py:232
  11.5 0.6 copy-start.11
  15.5 21.1 %all-to-all-start = ((f32[8,8,128]{2,1,0:T(8,128)}), f32[8,8,128]{2,1,0:T(8,128)S(1)}, u32[]{:S(2)}, u32[]{:S(2)}) async-start(f32[8,8,128]{2,1,0:T(8,128)} %rank_partials.1), calls=%async_computation | async-start | bytes 65536 | tf_op jit(solution)/shard_map/all_to_all | solution.py:246
  27.2 9.1 %collective-permute-start.1 = (bf16[8,1280]{1,0:T(8,128)(2,1)S(1)}, bf16[8,1280]{1,0:T(8,128)(2,1)S(1)}, u32[]{:S(2)}, u32[]{:S(2)}) collective-permute-start(bf16[8,1280]{1,0:T(8,128)(2,1)S(1)} %pad_maximum_fusion.pack_own), channel_id=1, source_target_pairs={{0,256},{8,264},{16,272},{24,280},{32,288},{40,296},{48,304},{56,3... | collective-permute-start | bytes 61448 | tf_op jit(solution)/shard_map/ppermute | solution.py:234
  30.5 37.8 %collective-permute-start.2 = (bf16[64,1024]{1,0:T(8,128)(2,1)S(1)}, bf16[64,1024]{1,0:T(8,128)(2,1)S(1)}, u32[]{:S(2)}, u32[]{:S(2)}) collective-permute-start(bf16[64,1024]{1,0:T(8,128)(2,1)S(1)} %bitcast.29), channel_id=1, source_target_pairs={{0,256},{8,264},{16,272},{24,280},{32,288},{40,296},{48,304},{56,3... | collective-permute-start | bytes 393224 | tf_op jit(solution)/shard_map/ppermute | solution.py:248
  36.6 1.0 %copy-start = (bf16[1,4,4,16,1024]{4,3,2,1,0:T(8,128)(2,1)S(1)}, bf16[1,4,4,16,1024]{4,3,2,1,0:T(8,128)(2,1)}, u32[]{:S(2)}) copy-start(bf16[1,4,4,16,1024]{4,3,2,1,0:T(8,128)(2,1)} %param.20) | copy-start | bytes 1572868
  37.7 2.2 %copy-start.1 = (bf16[1,8,2,1024,128]{4,3,2,1,0:T(8,128)(2,1)S(1)}, bf16[1,8,2,1024,128]{4,3,2,1,0:T(8,128)(2,1)}, u32[]{:S(2)}) copy-start(bf16[1,8,2,1024,128]{4,3,2,1,0:T(8,128)(2,1)} %param.19) | copy-start | bytes 12582916
  39.8 0.8 %copy-start.2 = (s32[64,4]{1,0:T(8,128)S(1)}, s32[64,4]{1,0:T(8,128)}, u32[]{:S(2)}) copy-start(s32[64,4]{1,0:T(8,128)} %copy.23.land) | copy-start | bytes 3076
  40.6 0.8 %copy-start.3 = (s32[64,8]{1,0:T(8,128)S(1)}, s32[64,8]{1,0:T(8,128)}, u32[]{:S(2)}) copy-start(s32[64,8]{1,0:T(8,128)} %copy.21.ids) | copy-start | bytes 6148
  41.4 0.8 %copy-start.4 = (s32[64,4]{1,0:T(8,128)S(1)}, s32[64,4]{1,0:T(8,128)}, u32[]{:S(2)}) copy-start(s32[64,4]{1,0:T(8,128)} %copy.22.leave) | copy-start | bytes 3076
  42.1 0.7 copy-start.5
  42.8 0.7 copy-start.7
  51.8 0.6 copy-start.6
  52.4 19.6 %all-to-all-start.1 = ((f32[16,8,128]{2,1,0:T(8,128)}), f32[16,8,128]{2,1,0:T(8,128)S(1)}, u32[]{:S(2)}, u32[]{:S(2)}) async-start(f32[16,8,128]{2,1,0:T(8,128)} %get-tuple-element.12), calls=%async_computation.1 | async-start | bytes 131072 | tf_op jit(solution)/shard_map/all_to_all | solution.py:276
  61.8 6.5 %collective-permute-start.3 = (bf16[8,1024]{1,0:T(8,128)(2,1)S(1)}, bf16[8,1024]{1,0:T(8,128)(2,1)S(1)}, u32[]{:S(2)}, u32[]{:S(2)}) collective-permute-start(bf16[8,1024]{1,0:T(8,128)(2,1)S(1)} %get-tuple-element.14), channel_id=1, source_target_pairs={{0,256},{8,264},{16,272},{24,280},{32,288},{40,296},{48,304},{56,3... | collective-permute-start | bytes 49160 | tf_op jit(solution)/shard_map/ppermute | solution.py:277
  68.4 3.6 %copy-start.10 = (bf16[8,1024]{1,0:T(8,128)(2,1)}, bf16[8,1024]{1,0:T(8,128)(2,1)S(1)}, u32[]{:S(2)}) copy-start(bf16[8,1024]{1,0:T(8,128)(2,1)S(1)} %collective-permute-done.3.attn2_other) | copy-start | bytes 49156
  68.4 3.6 %copy-start.9 = (bf16[64,1024]{1,0:T(8,128)(2,1)}, bf16[64,1024]{1,0:T(8,128)(2,1)S(1)}, u32[]{:S(2)}) copy-start(bf16[64,1024]{1,0:T(8,128)(2,1)S(1)} %collective-permute-done.2.up_other) | copy-start | bytes 393220
  72.0 0.6 copy-start.8

commit v2 on v1

v2 whole, which is shorter than its diff:
```python
import math

import jax
import jax.numpy as jnp
from jax import lax
from jax.experimental import pallas as pl
from jax.experimental.pallas import tpu as pltpu
from jax.sharding import PartitionSpec as P

HEAD = 128
masked_score = -1e30
f32 = jnp.float32
bf16 = jnp.bfloat16


def dot_t(a, b):
    return lax.dot_general(a, b, (((1,), (1,)), ((), ())), preferred_element_type=f32)


def dot(a, b):
    return lax.dot_general(a, b, (((1,), (0,)), ((), ())), preferred_element_type=f32)


def twice(table):
    flat = table.reshape(-1, table.shape[-1])
    return jnp.concatenate([flat, flat], 0)


def row_iota(shape):
    return lax.broadcasted_iota(jnp.int32, shape, 0)


def lane_iota(shape):
    return lax.broadcasted_iota(jnp.int32, shape, 1)


def own_adapter(ids, me, slots, lanes, rank):
    rows, columns = row_iota((slots, lanes)), lane_iota((slots, lanes))
    adapter = jnp.zeros((slots, lanes), jnp.int32)
    for s in range(slots):
        adapter = jnp.where(rows == s, ids[s, me], adapter)
    return lax.rem(columns, lanes // 2) // rank == adapter


def moved_in(base, rows_at, counts, targets, sources, me):
    row = row_iota(base.shape)
    for m in range(targets.shape[0]):
        picked = rows_at[pl.ds(sources[m, me], 1), :]
        base = jnp.where((row == targets[m, me]) & (m < counts[me]), picked, base)
    return base


def is_row(shape, counts, table, instance):
    row = row_iota(shape)
    found = jnp.zeros(shape, jnp.bool_)
    for m in range(table.shape[0]):
        found = found | ((row == table[m, instance]) & (m < counts[instance]))
    return found


def start_all(pairs, sems, first=0):
    copies = [pltpu.make_async_copy(src, dst, sems.at[first + n]) for n, (src, dst) in enumerate(pairs)]
    for copy in copies:
        copy.start()
    return copies


def wait_all(copies):
    for copy in copies:
        copy.wait()


def rank_kernel(
    ids_at, counts_at, leave_at, land_at, h1_at, h2_at, query_at, fresh_at, tables_at, h2_other,
    out, pack_out,
    ids, counts, leave, land, h1, h2, query, fresh, down, fresh_wide, scratch, sems,
):
    me = lax.axis_index("inst")
    copies = start_all(
        [
            (h1_at.at[0], h1), (h2_at.at[0], h2), (tables_at.at[0, :, 0], down), (ids_at, ids), (counts_at, counts),
            (leave_at, leave), (land_at, land), (query_at.at[0], query), (fresh_at.at[0], fresh),
        ],
        sems,
    )
    peers, slots, lanes = out.shape
    width = h1.shape[1]
    rank = down.shape[1]
    wait_all(copies)
    table = twice(down[...])
    hidden = jnp.concatenate([h1[...].astype(f32), h2[...].astype(f32), h2_other[...].astype(f32)], 0).astype(bf16)
    partials = dot_t(hidden, table)
    scratch[...] = partials[2 * slots :]
    second = moved_in(partials[slots : 2 * slots], scratch, counts, leave, land, me)
    both = jnp.where(lane_iota((slots, lanes)) < lanes // 2, partials[:slots], second)
    both = jnp.where(own_adapter(ids, me, slots, lanes, rank), both, 0.0)
    for peer in range(peers):
        out[peer] = both
    pack_out[:, :width] = query[...]
    fresh_wide[...] = fresh[...].astype(f32)
    pack_out[:, width : width + HEAD] = fresh_wide[:, 0, :].astype(bf16)
    pack_out[:, width + HEAD :] = fresh_wide[:, 1, :].astype(bf16)


def attention_kernel(
    lengths_at, ids_at, counts_at, leave_at, land_at, base1_at, fresh1_at, tables_at, cache_at,
    ranks, pack_own, pack_other,
    attn1_out, attn2_out, send_out, ranks_out, up_out, incoming_out,
    lengths, ids, counts, leave, land, base1, fresh1, up, down,
    kv, other_rows, queries, scores, mixed, second_rows, rank_rows, sems,
):
    me = lax.axis_index("inst")
    half = lax.axis_size("inst") // 2
    other = jnp.bitwise_xor(me, half)
    slots, width = base1.shape
    heads = width // HEAD
    cached = kv.shape[2]
    lanes = ranks.shape[2]
    rank = up.shape[1]
    small = start_all(
        [
            (tables_at.at[0, :, 1], up), (base1_at.at[0], base1), (lengths_at, lengths), (ids_at, ids),
            (counts_at, counts), (leave_at, leave), (land_at, land), (fresh1_at.at[0], fresh1),
        ],
        sems,
    )
    keys = start_all([(cache_at.at[0, s, 0], kv.at[0, s]) for s in range(slots)], sems, 8)
    values = start_all([(cache_at.at[0, s, 1], kv.at[1, s]) for s in range(slots)], sems, 8 + slots)
    late = start_all(
        [(tables_at.at[0, :, 2], down), (tables_at.at[0, :, 3], up_out)], sems, 8 + 2 * slots
    )

    lane = lane_iota((slots, lanes))
    low = lane < lanes // 2
    total = ranks[0]
    for peer in range(1, ranks.shape[0]):
        total = total + ranks[peer]
    total = jnp.concatenate([jnp.where(low, total, 0.0), jnp.where(low, 0.0, total)], 0).astype(bf16)
    other_rows[...] = pack_other[...].astype(f32)
    own = pack_own[...].astype(f32)
    wait_all(small)
    update = dot(total, twice(up[...]))
    second = moved_in(own, other_rows, counts, leave, land, me)
    query1 = (base1[...].astype(f32) + update[:slots]).astype(bf16).astype(f32)
    query2 = (second[:, :width] + update[slots:]).astype(bf16).astype(f32)
    for h in range(heads):
        columns = slice(h * HEAD, (h + 1) * HEAD)
        queries[h, :slots] = query1[:, columns]
        queries[h, slots:] = query2[:, columns]
    first = fresh1[...].astype(f32)
    key2 = second[:, width : width + HEAD]
    value2 = second[:, width + HEAD :]

    scaling = math.log2(math.e) / math.sqrt(HEAD)
    score_shape = (2 * heads, cached)
    position = lane_iota(score_shape)
    extra = (position == cached - 2) | ((position == cached - 1) & (row_iota(score_shape) >= heads))
    last = pl.ds(cached - 16, 16)
    tail_row = row_iota((16, HEAD))

    def with_fresh(tile, one, two):
        tile = jnp.where(tail_row == 14, one, tile.astype(f32))
        return jnp.where(tail_row == 15, two, tile).astype(bf16)

    step = 2
    for block in range(0, slots, step):
        wait_all(keys[block : block + step])
        for s in range(block, block + step):
            kv[0, s, last, :] = with_fresh(kv[0, s, last, :], first[s, 0:1], key2[s : s + 1])
            query = jnp.concatenate([queries[:, s, :], queries[:, slots + s, :]], 0).astype(bf16)
            score = dot_t(query, kv[0, s]) * scaling
            scores[s] = jnp.where((position < lengths[s, me]) | extra, score, masked_score)
    for block in range(0, slots, step):
        wait_all(values[block : block + step])
        for s in range(block, block + step):
            kv[1, s, last, :] = with_fresh(kv[1, s, last, :], first[s, 1:2], value2[s : s + 1])
            score = scores[s]
            weights = jnp.exp2(score - jnp.max(score, 1, keepdims=True))
            probs = (weights * (1.0 / jnp.sum(weights, 1, keepdims=True))).astype(bf16)
            attended = dot(probs, kv[1, s]).astype(bf16).astype(f32)
            mixed[0, s] = attended[:heads]
            mixed[1, s] = attended[heads:]

    vacated = is_row((slots, HEAD), counts, leave, me)
    fresh_value = own[:, width + HEAD :]
    for h in range(heads):
        columns = slice(h * HEAD, (h + 1) * HEAD)
        attn1_out[:, columns] = mixed[0, :, h, :].astype(bf16)
        served = mixed[1, :, h, :]
        second_rows[:, columns] = served
        attn2_out[:, columns] = jnp.where(vacated, fresh_value, served).astype(bf16)

    wait_all(late)
    mask = own_adapter(ids, me, slots, lanes, rank)
    served_rows = second_rows[...]
    stacked = jnp.concatenate([attn1_out[...].astype(f32), attn2_out[...].astype(f32), served_rows], 0).astype(bf16)
    partials = dot_t(stacked, twice(down[...]))
    rank_rows[...] = jnp.where(mask, partials[2 * slots :], 0.0)
    send_out[...] = moved_in(served_rows, second_rows, counts, land, leave, me).astype(bf16)
    for_own = jnp.where(mask, jnp.where(low, partials[:slots], partials[slots : 2 * slots]), 0.0)
    for_other = moved_in(jnp.zeros_like(for_own), rank_rows, counts, land, leave, me)
    peers = ranks_out.shape[0] // 2
    lower = me < half
    for peer in range(peers):
        ranks_out[peer] = jnp.where(lower, for_own, for_other)
        ranks_out[peers + peer] = jnp.where(lower, for_other, for_own)
    incoming_out[...] = jnp.where(is_row(incoming_out.shape, counts, land, other), 1.0, 0.0)


def delta_kernel(ranks, up, up_other, attn2_own, attn2_other, incoming, delta1_out, delta2_out, attn2_out):
    lower = lax.axis_index("inst") < lax.axis_size("inst") // 2
    peers = ranks.shape[0] // 2
    _, slots, lanes = ranks.shape
    sums = []
    for part in range(2):
        total = ranks[part * peers]
        for peer in range(1, peers):
            total = total + ranks[part * peers + peer]
        sums.append(total)
    own = jnp.where(lower, sums[0], sums[1])
    got = jnp.where(lower, sums[1], sums[0])
    low = lane_iota((slots, lanes)) < lanes // 2
    comes = incoming[...] > 0.5
    rank1 = jnp.where(low, own, 0.0)
    rank2_own = jnp.where(low, pltpu.roll(own, lanes // 2, 1), 0.0)
    rank2_got = jnp.where(low, 0.0, got)
    rank2 = jnp.where(comes, rank2_got, rank2_own)
    table = jnp.concatenate([up[...].reshape(-1, up.shape[2]), up_other[...]], 0)
    delta = dot(jnp.concatenate([rank1, rank2], 0).astype(bf16), table)
    delta1_out[...] = delta[:slots].astype(bf16)
    delta2_out[...] = delta[slots:].astype(bf16)
    for first in range(0, attn2_out.shape[1], lanes):
        columns = slice(first, first + lanes)
        attn2_out[:, columns] = jnp.where(
            comes, attn2_other[:, columns].astype(f32), attn2_own[:, columns].astype(f32)
        ).astype(bf16)


def per_device(
    query_first,
    query_second,
    hidden_first,
    hidden_second,
    fresh_first,
    fresh_second,
    kv_cache,
    adapters,
    lengths,
    adapter_ids,
    move_counts,
    move_from,
    move_to,
):
    inst_count = lax.axis_size("inst")
    peers = lax.axis_size("tensor")
    half = inst_count // 2
    swap = [(i, i ^ half) for i in range(inst_count)]
    groups = [
        [i * peers + t for t in range(peers)] + [(i + half) * peers + t for t in range(peers)] for i in range(half)
    ]
    _, slots, width = query_first.shape
    _, pool, _, rank, _ = adapters.shape
    moves = move_from.shape[1]
    lanes = 2 * pool * rank
    heads = width // HEAD
    cached = kv_cache.shape[3]
    lengths, adapter_ids, move_from, move_to = lengths.T, adapter_ids.T, move_from.T, move_to.T

    hbm = pl.BlockSpec(memory_space=pltpu.HBM)
    vmem = pl.BlockSpec(memory_space=pltpu.VMEM)

    def shape(dims, dtype):
        return jax.ShapeDtypeStruct(dims, dtype)

    def far(*arrays):
        return [pltpu.with_memory_space_constraint(array, pltpu.HBM) for array in arrays]

    def near(*arrays):
        return [pltpu.with_memory_space_constraint(array, pltpu.VMEM) for array in arrays]

    def near_shape(dims, dtype):
        return pltpu.VMEM(dims, dtype)

    table = pltpu.VMEM((pool, rank, width), bf16)
    rows = pltpu.VMEM((slots, width), bf16)
    fresh = pltpu.VMEM((slots, 2, HEAD), bf16)
    by_slot = pltpu.SMEM((slots, inst_count), jnp.int32)
    by_inst = pltpu.SMEM((inst_count,), jnp.int32)
    by_move = pltpu.SMEM((moves, inst_count), jnp.int32)

    hidden_other = lax.ppermute(hidden_second[0], "inst", swap)
    up_other = lax.ppermute(adapters[0, :, 3].reshape(pool * rank, width), "inst", swap)

    ranks, pack_own = pl.pallas_call(
        rank_kernel,
        name="rank_partials",
        out_shape=(shape((peers, slots, lanes), f32), shape((slots, width + 2 * HEAD), bf16)),
        in_specs=[hbm] * 9 + [vmem],
        out_specs=(vmem,) * 2,
        scratch_shapes=[
            by_slot, by_inst, by_move, by_move, rows, rows, rows, fresh, table,
            pltpu.VMEM((slots, 2, HEAD), f32),
            pltpu.VMEM((slots, lanes), f32),
            pltpu.SemaphoreType.DMA((9,)),
        ],
        compiler_params=pltpu.CompilerParams(vmem_limit_bytes=16 * 1024 * 1024),
    )(
        *far(
            adapter_ids, move_counts, move_from, move_to,
            hidden_first, hidden_second, query_second, fresh_second, adapters,
        ),
        *near(hidden_other),
    )
    ranks = lax.all_to_all(ranks, "tensor", 0, 0)
    pack_other = lax.ppermute(pack_own, "inst", swap)

    attn1, attn2_own, attn2_send, ranks_two, up_own, incoming = pl.pallas_call(
        attention_kernel,
        name="attention",
        out_shape=(
            shape((slots, width), bf16),
            shape((slots, width), bf16),
            shape((slots, width), bf16),
            shape((2 * peers, slots, lanes), f32),
            shape((pool, rank, width), bf16),
            shape((slots, lanes), f32),
        ),
        in_specs=[hbm] * 9 + [vmem] * 3,
        out_specs=(vmem,) * 6,
        scratch_shapes=[
            by_slot, by_slot, by_inst, by_move, by_move, rows, fresh, table, table,
            pltpu.VMEM((2, slots, cached, HEAD), bf16),
            pltpu.VMEM((slots, width + 2 * HEAD), f32),
            pltpu.VMEM((heads, 2 * slots, HEAD), f32),
            pltpu.VMEM((slots, 2 * heads, cached), f32),
            pltpu.VMEM((2, slots, heads, HEAD), f32),
            pltpu.VMEM((slots, width), f32),
            pltpu.VMEM((slots, lanes), f32),
            pltpu.SemaphoreType.DMA((10 + 2 * slots,)),
        ],
        compiler_params=pltpu.CompilerParams(vmem_limit_bytes=16 * 1024 * 1024),
    )(
        *far(lengths, adapter_ids, move_counts, move_from, move_to, query_first, fresh_first, adapters, kv_cache),
        *near(ranks, pack_own, pack_other),
    )
    ranks_two = lax.all_to_all(ranks_two, ("inst", "tensor"), 0, 0, axis_index_groups=groups)
    attn2_other = lax.ppermute(attn2_send, "inst", swap)

    delta1, delta2, attn2 = pl.pallas_call(
        delta_kernel,
        name="deltas",
        out_shape=(shape((slots, width), bf16),) * 3,
        in_specs=[vmem] * 6,
        out_specs=(vmem,) * 3,
        compiler_params=pltpu.CompilerParams(vmem_limit_bytes=16 * 1024 * 1024),
    )(*near(ranks_two, up_own, up_other, attn2_own, attn2_other, incoming))
    return (attn1[None], delta1[None], attn2[None], delta2[None])


def solution(mesh):
    row = P("inst", None, "tensor")
    fresh = P("inst", None, None, "tensor")
    whole = P("inst", None, None, None, "tensor")
    return jax.shard_map(
        per_device,
        mesh=mesh,
        in_specs=(row, row, row, row, fresh, fresh, whole, whole, P(), P(), P(), P(), P()),
        out_specs=(row, row, row, row),
        check_vma=False,
    )
```

time: 75.7 us -> 55.8 us (0.74)
  the two profiles are of different devices: /device:TPU:24 before, /device:TPU:48 now
where the time goes in v2:
time: 55.8 us; the launch traced here: 55.3 us
  starting transfers between devices  36.3 us (65%)
  waiting for transfers between devices  9.84 us (18%)
  Pallas kernels  7.55 us (14%)
  local copies, waits for them, and re-layouts  0.92 us (2%)
  between operations  0.7 us (1%)
    all_to_all x1, starting transfers between devices, per_device(): ranks = lax.all_to_all(ranks, 'tensor', 0, 0)  11.5 us
    all_to_all x1, starting transfers between devices, per_device(): lax.all_to_all(ranks_two, ('inst', 'tensor'), 0, 0, axis_index_groups=gro...  7.3 us
    ppermute x1, starting transfers between devices, per_device(): hidden_other = lax.ppermute(hidden_second[0], 'inst', swap)  6.09 us
    pallas_call x1, Pallas kernels, per_device(): pl.pallas_call(attention_kernel, name='attention', out_shape=(shape((slot...  4.84 us
    ppermute x1, starting transfers between devices, per_device(): attn2_other = lax.ppermute(attn2_send, 'inst', swap)  4.72 us
    ppermute x1, starting transfers between devices, per_device(): pack_other = lax.ppermute(pack_own, 'inst', swap)  4.3 us
    all_to_all x1, waiting for transfers between devices, per_device(): lax.all_to_all(ranks_two, ('inst', 'tensor'), 0, 0, axis_index_groups=gro...  3.49 us
    all_to_all x1, waiting for transfers between devices, per_device(): ranks = lax.all_to_all(ranks, 'tensor', 0, 0)  2.49 us
  transfers between devices with their start and end apart: 6, of which 4 were waited for; matrix products, arithmetic and copies ran while one was open for 2% of the time, Pallas kernels for 9%

profile of v2, /device:TPU:48, one launch (start us, length us, event | category | flops | bytes accessed | tf_op | source)
XLA Modules:
  0.0 55.3 jit_solution(2608647524935093266)
XLA Ops:
  0.6 6.1 %collective-permute-start = (bf16[8,1024]{1,0:T(8,128)(2,1)}, bf16[8,1024]{1,0:T(8,128)(2,1)S(1)}, u32[]{:S(2)}, u32[]{:S(2)}) collective-permute-start(bf16[8,1024]{1,0:T(8,128)(2,1)} %bitcast.13), channel_id=1, source_target_pairs={{0,256},{8,264},{16,272},{24,280},{32,288},{40,296},{48,304},{56,3... | collective-permute-start | bytes 49160 | tf_op jit(solution)/shard_map/ppermute | solution.py:291
  6.7 1.9 %collective-permute-done.h2_other = bf16[8,1024]{1,0:T(8,128)(2,1)S(1)} collective-permute-done((bf16[8,1024]{1,0:T(8,128)(2,1)}, bf16[8,1024]{1,0:T(8,128)(2,1)S(1)}, u32[]{:S(2)}, u32[]{:S(2)}) %collective-permute-start) | collective-permute-done | bytes 16416 | tf_op jit(solution)/shard_map/ppermute | solution.py:291
  8.6 1.9 %rank_partials.1 = (f32[8,8,128]{2,1,0:T(8,128)}, bf16[8,1280]{1,0:T(8,128)(2,1)S(1)}) custom-call(s32[8,64]{1,0:T(8,128)} %bitcast.11, s32[64]{0:T(128)} %counts_at.3, s32[4,64]{1,0:T(4,128)} %bitcast.14, s32[4,64]{1,0:T(4,128)} %bitcast.16, bf16[1,8,1024]{2,1,0:T(8,128)(2,1)} %h1_at.1, bf16[1,8,1024]{2,1,0:T(8,128)(2,1)} %h2_at.1, ...), custom_call_target="tpu_custom_call" | custom-call | tf_op jit(solution)/shard_map/rank_partials/pallas_call | solution.py:294
  10.5 11.5 %all-to-all-start = ((f32[8,8,128]{2,1,0:T(8,128)}), f32[8,8,128]{2,1,0:T(8,128)S(1)}, u32[]{:S(2)}, u32[]{:S(2)}) async-start(f32[8,8,128]{2,1,0:T(8,128)} %get-tuple-element.15), calls=%async_computation | async-start | bytes 65536 | tf_op jit(solution)/shard_map/all_to_all | solution.py:314
  22.0 4.3 %collective-permute-start.1 = (bf16[8,1280]{1,0:T(8,128)(2,1)S(1)}, bf16[8,1280]{1,0:T(8,128)(2,1)S(1)}, u32[]{:S(2)}, u32[]{:S(2)}) collective-permute-start(bf16[8,1280]{1,0:T(8,128)(2,1)S(1)} %get-tuple-element.16.pack_own), channel_id=1, source_target_pairs={{0,256},{8,264},{16,272},{24,280},{32,288},{40,296},{48,304},{56,3... | collective-permute-start | bytes 61448 | tf_op jit(solution)/shard_map/ppermute | solution.py:315
  26.3 0.9 %slice.3 = bf16[1,4,1,16,1024]{4,3,2,1,0:T(8,128)(2,1)S(1)} slice(bf16[1,4,4,16,1024]{4,3,2,1,0:T(8,128)(2,1)} %tables_at.3), slice={[0:1], [0:4], [3:4], [0:16], [0:1024]} | slice | bytes 262144 | tf_op jit(solution)/shard_map/slice | solution.py:292
  27.2 2.4 %collective-permute-start.2 = (bf16[64,1024]{1,0:T(8,128)(2,1)S(1)}, bf16[64,1024]{1,0:T(8,128)(2,1)S(1)}, u32[]{:S(2)}, u32[]{:S(2)}) collective-permute-start(bf16[64,1024]{1,0:T(8,128)(2,1)S(1)} %bitcast.10), channel_id=1, source_target_pairs={{0,256},{8,264},{16,272},{24,280},{32,288},{40,296},{48,304},{56,3... | collective-permute-start | bytes 393224 | tf_op jit(solution)/shard_map/ppermute | solution.py:292
  29.7 0.0 collective-permute-done.1.pack_other
  29.7 2.5 %all-to-all-done.ranks = f32[8,8,128]{2,1,0:T(8,128)S(1)} async-done(((f32[8,8,128]{2,1,0:T(8,128)}), f32[8,8,128]{2,1,0:T(8,128)S(1)}, u32[]{:S(2)}, u32[]{:S(2)}) %all-to-all-start) | async-done | bytes 32800 | tf_op jit(solution)/shard_map/all_to_all | solution.py:314
  32.2 4.8 %attention.1 = (bf16[8,1024]{1,0:T(8,128)(2,1)}, bf16[8,1024]{1,0:T(8,128)(2,1)S(1)}, bf16[8,1024]{1,0:T(8,128)(2,1)S(1)}, f32[16,8,128]{2,1,0:T(8,128)}, bf16[4...) custom-call(s32[8,64]{1,0:T(8,128)} %bitcast.18, s32[8,64]{1,0:T(8,128)} %bitcast.12, s32[64]{0:T(128)} %counts_at.3, ...), custom_call_target="tpu_custom_call" | custom-call | tf_op jit(solution)/shard_map/attention/pallas_call | solution.py:317
  37.0 7.3 %all-to-all-start.1 = ((f32[16,8,128]{2,1,0:T(8,128)}), f32[16,8,128]{2,1,0:T(8,128)S(1)}, u32[]{:S(2)}, u32[]{:S(2)}) async-start(f32[16,8,128]{2,1,0:T(8,128)} %get-tuple-element.18), calls=%async_computation.1 | async-start | bytes 131072 | tf_op jit(solution)/shard_map/all_to_all | solution.py:346
  44.3 4.7 %collective-permute-start.3 = (bf16[8,1024]{1,0:T(8,128)(2,1)S(1)}, bf16[8,1024]{1,0:T(8,128)(2,1)S(1)}, u32[]{:S(2)}, u32[]{:S(2)}) collective-permute-start(bf16[8,1024]{1,0:T(8,128)(2,1)S(1)} %get-tuple-element.21), channel_id=1, source_target_pairs={{0,256},{8,264},{16,272},{24,280},{32,288},{40,296},{48,304},{56,3... | collective-permute-start | bytes 49160 | tf_op jit(solution)/shard_map/ppermute | solution.py:347
  49.1 1.9 %collective-permute-done.3.attn2_other = bf16[8,1024]{1,0:T(8,128)(2,1)S(1)} collective-permute-done((bf16[8,1024]{1,0:T(8,128)(2,1)S(1)}, bf16[8,1024]{1,0:T(8,128)(2,1)S(1)}, u32[]{:S(2)}, u32[]{:S(2)}) %collective-permute-start.3) | collective-permute-done | bytes 16416 | tf_op jit(solution)/shard_map/ppermute | solution.py:347
  51.0 0.0 collective-permute-done.2.up_other
  51.0 3.5 %all-to-all-done.1.ranks = f32[16,8,128]{2,1,0:T(8,128)S(1)} async-done(((f32[16,8,128]{2,1,0:T(8,128)}), f32[16,8,128]{2,1,0:T(8,128)S(1)}, u32[]{:S(2)}, u32[]{:S(2)}) %all-to-all-start.1) | async-done | bytes 65568 | tf_op jit(solution)/shard_map/all_to_all | solution.py:346
  54.5 0.8 %deltas.1 = (bf16[8,1024]{1,0:T(8,128)(2,1)}, bf16[8,1024]{1,0:T(8,128)(2,1)}, bf16[8,1024]{1,0:T(8,128)(2,1)}) custom-call(f32[16,8,128]{2,1,0:T(8,128)S(1)} %all-to-all-done.1.ranks, bf16[4,16,1024]{2,1,0:T(8,128)(2,1)S(1)} %get-tuple-element.19.up, bf16[64,1024]{1,0:T(8,128)(2,1)S(1)} %collective-permute-done.2.up_other, ...), custom_call_target="tpu_custom_call" | custom-call | tf_op jit(solution)/shard_map/deltas/pallas_call | solution.py:349
Async XLA Ops:
  0.6 8.0 %collective-permute-start = (bf16[8,1024]{1,0:T(8,128)(2,1)}, bf16[8,1024]{1,0:T(8,128)(2,1)S(1)}, u32[]{:S(2)}, u32[]{:S(2)}) collective-permute-start(bf16[8,1024]{1,0:T(8,128)(2,1)} %bitcast.13), channel_id=1, source_target_pairs={{0,256},{8,264},{16,272},{24,280},{32,288},{40,296},{48,304},{56,3... | collective-permute-start | bytes 49160 | tf_op jit(solution)/shard_map/ppermute | solution.py:291
  10.5 21.7 %all-to-all-start = ((f32[8,8,128]{2,1,0:T(8,128)}), f32[8,8,128]{2,1,0:T(8,128)S(1)}, u32[]{:S(2)}, u32[]{:S(2)}) async-start(f32[8,8,128]{2,1,0:T(8,128)} %get-tuple-element.15), calls=%async_computation | async-start | bytes 65536 | tf_op jit(solution)/shard_map/all_to_all | solution.py:314
  22.0 7.7 %collective-permute-start.1 = (bf16[8,1280]{1,0:T(8,128)(2,1)S(1)}, bf16[8,1280]{1,0:T(8,128)(2,1)S(1)}, u32[]{:S(2)}, u32[]{:S(2)}) collective-permute-start(bf16[8,1280]{1,0:T(8,128)(2,1)S(1)} %get-tuple-element.16.pack_own), channel_id=1, source_target_pairs={{0,256},{8,264},{16,272},{24,280},{32,288},{40,296},{48,304},{56,3... | collective-permute-start | bytes 61448 | tf_op jit(solution)/shard_map/ppermute | solution.py:315
  27.2 23.8 %collective-permute-start.2 = (bf16[64,1024]{1,0:T(8,128)(2,1)S(1)}, bf16[64,1024]{1,0:T(8,128)(2,1)S(1)}, u32[]{:S(2)}, u32[]{:S(2)}) collective-permute-start(bf16[64,1024]{1,0:T(8,128)(2,1)S(1)} %bitcast.10), channel_id=1, source_target_pairs={{0,256},{8,264},{16,272},{24,280},{32,288},{40,296},{48,304},{56,3... | collective-permute-start | bytes 393224 | tf_op jit(solution)/shard_map/ppermute | solution.py:292
  37.0 17.5 %all-to-all-start.1 = ((f32[16,8,128]{2,1,0:T(8,128)}), f32[16,8,128]{2,1,0:T(8,128)S(1)}, u32[]{:S(2)}, u32[]{:S(2)}) async-start(f32[16,8,128]{2,1,0:T(8,128)} %get-tuple-element.18), calls=%async_computation.1 | async-start | bytes 131072 | tf_op jit(solution)/shard_map/all_to_all | solution.py:346
  44.3 6.7 %collective-permute-start.3 = (bf16[8,1024]{1,0:T(8,128)(2,1)S(1)}, bf16[8,1024]{1,0:T(8,128)(2,1)S(1)}, u32[]{:S(2)}, u32[]{:S(2)}) collective-permute-start(bf16[8,1024]{1,0:T(8,128)(2,1)S(1)} %get-tuple-element.21), channel_id=1, source_target_pairs={{0,256},{8,264},{16,272},{24,280},{32,288},{40,296},{48,304},{56,3... | collective-permute-start | bytes 49160 | tf_op jit(solution)/shard_map/ppermute | solution.py:347

commit v3 on v2

v3 whole, which is shorter than its diff:
```python
import math

import jax
import jax.numpy as jnp
from jax import lax
from jax.experimental import pallas as pl
from jax.experimental.pallas import tpu as pltpu
from jax.sharding import PartitionSpec as P

HEAD = 128
masked_score = -1e30
f32 = jnp.float32
bf16 = jnp.bfloat16


def dot_t(a, b):
    return lax.dot_general(a, b, (((1,), (1,)), ((), ())), preferred_element_type=f32)


def dot(a, b):
    return lax.dot_general(a, b, (((1,), (0,)), ((), ())), preferred_element_type=f32)


def twice(table):
    flat = table.reshape(-1, table.shape[-1])
    return jnp.concatenate([flat, flat], 0)


def row_iota(shape):
    return lax.broadcasted_iota(jnp.int32, shape, 0)


def lane_iota(shape):
    return lax.broadcasted_iota(jnp.int32, shape, 1)


def own_adapter(ids, me, slots, lanes, rank):
    rows, columns = row_iota((slots, lanes)), lane_iota((slots, lanes))
    adapter = jnp.zeros((slots, lanes), jnp.int32)
    for s in range(slots):
        adapter = jnp.where(rows == s, ids[s, me], adapter)
    return lax.rem(columns, lanes // 2) // rank == adapter


def moved_in(base, rows_at, counts, targets, sources, me):
    row = row_iota(base.shape)
    for m in range(targets.shape[0]):
        picked = rows_at[pl.ds(sources[m, me], 1), :]
        base = jnp.where((row == targets[m, me]) & (m < counts[me]), picked, base)
    return base


def is_row(shape, counts, table, instance):
    row = row_iota(shape)
    found = jnp.zeros(shape, jnp.bool_)
    for m in range(table.shape[0]):
        found = found | ((row == table[m, instance]) & (m < counts[instance]))
    return found


def start_all(pairs, sems, first=0):
    copies = [pltpu.make_async_copy(src, dst, sems.at[first + n]) for n, (src, dst) in enumerate(pairs)]
    for copy in copies:
        copy.start()
    return copies


def wait_all(copies):
    for copy in copies:
        copy.wait()


def halves(value):
    high = value.astype(bf16).astype(f32)
    return jnp.concatenate([high, value - high], 0)


def stage_kernel(
    h1, h2, q1, q2, f1, f2, tables_at,
    first_out, second_out, tables_out, up_out,
    fresh, fresh_wide, sems,
):
    width = h1.shape[2]
    copies = start_all(
        [
            (f1.at[0], fresh.at[0]), (f2.at[0], fresh.at[1]),
            (h1.at[0], first_out.at[:, :width]), (h2.at[0], second_out.at[:, :width]),
            (q1.at[0], first_out.at[:, width : 2 * width]), (q2.at[0], second_out.at[:, width : 2 * width]),
            (tables_at.at[0, :, 3], up_out), (tables_at.at[0], tables_out),
        ],
        sems,
    )
    wait_all(copies[:2])
    fresh_wide[...] = fresh[...].astype(f32)
    for step, out in enumerate((first_out, second_out)):
        out[:, 2 * width : 2 * width + HEAD] = fresh_wide[step, :, 0, :].astype(bf16)
        out[:, 2 * width + HEAD :] = fresh_wide[step, :, 1, :].astype(bf16)
    wait_all(copies[2:])


def rank_kernel(
    ids_at, counts_at, leave_at, land_at, first, second, other, tables,
    out,
    ids, counts, leave, land, scratch, sems,
):
    me = lax.axis_index("inst")
    copies = start_all([(ids_at, ids), (counts_at, counts), (leave_at, leave), (land_at, land)], sems)
    peers, _, lanes = out.shape
    slots = first.shape[0]
    width = tables.shape[3]
    rank = tables.shape[2]
    table = twice(tables[:, 0])
    hidden = [ref[:, :width].astype(f32) for ref in (first, second, other)]
    partials = dot_t(jnp.concatenate(hidden, 0).astype(bf16), table)
    scratch[...] = partials[2 * slots :]
    wait_all(copies)
    moved = moved_in(partials[slots : 2 * slots], scratch, counts, leave, land, me)
    both = jnp.where(lane_iota((slots, lanes)) < lanes // 2, partials[:slots], moved)
    both = jnp.where(own_adapter(ids, me, slots, lanes, rank), both, 0.0)
    for peer in range(peers):
        out[peer] = both


def attention_kernel(
    lengths_at, ids_at, counts_at, leave_at, land_at, cache_at,
    ranks, first_rows, second_rows, got_rows, tables, up_other,
    attn1_out, own_out, landing_out, sums_out,
    lengths, ids, counts, leave, land,
    kv, other_rows, queries, scores, mixed, served_rows, rank_rows, sems,
):
    me = lax.axis_index("inst")
    half = lax.axis_size("inst") // 2
    slots, width = attn1_out.shape
    heads = width // HEAD
    cached = kv.shape[2]
    lanes = ranks.shape[2]
    rank = tables.shape[2]
    moves = leave.shape[0]
    small = start_all(
        [(counts_at, counts), (leave_at, leave), (land_at, land), (lengths_at, lengths), (ids_at, ids)], sems
    )
    keys = start_all([(cache_at.at[0, s, 0], kv.at[0, s]) for s in range(slots)], sems, 5)
    values = start_all([(cache_at.at[0, s, 1], kv.at[1, s]) for s in range(slots)], sems, 5 + slots)

    lane = lane_iota((slots, lanes))
    low = lane < lanes // 2
    total = ranks[0]
    for peer in range(1, ranks.shape[0]):
        total = total + ranks[peer]
    total = jnp.concatenate([jnp.where(low, total, 0.0), jnp.where(low, 0.0, total)], 0).astype(bf16)
    update = dot(total, twice(tables[:, 1]))
    other_rows[...] = got_rows[:, width:].astype(f32)
    first = first_rows[:, width:].astype(f32)
    own = second_rows[:, width:].astype(f32)
    wait_all(small)
    second = moved_in(own, other_rows, counts, leave, land, me)
    query1 = (first[:, :width] + update[:slots]).astype(bf16).astype(f32)
    query2 = (second[:, :width] + update[slots:]).astype(bf16).astype(f32)
    for h in range(heads):
        columns = slice(h * HEAD, (h + 1) * HEAD)
        queries[h, :slots] = query1[:, columns]
        queries[h, slots:] = query2[:, columns]
    key1, value1 = first[:, width : width + HEAD], first[:, width + HEAD :]
    key2, value2 = second[:, width : width + HEAD], second[:, width + HEAD :]

    scaling = math.log2(math.e) / math.sqrt(HEAD)
    score_shape = (2 * heads, cached)
    position = lane_iota(score_shape)
    extra = (position == cached - 2) | ((position == cached - 1) & (row_iota(score_shape) >= heads))
    last = pl.ds(cached - 16, 16)
    tail_row = row_iota((16, HEAD))

    def with_fresh(tile, one, two):
        tile = jnp.where(tail_row == 14, one, tile.astype(f32))
        return jnp.where(tail_row == 15, two, tile).astype(bf16)

    step = 2
    for block in range(0, slots, step):
        wait_all(keys[block : block + step])
        for s in range(block, block + step):
            kv[0, s, last, :] = with_fresh(kv[0, s, last, :], key1[s : s + 1], key2[s : s + 1])
            query = jnp.concatenate([queries[:, s, :], queries[:, slots + s, :]], 0).astype(bf16)
            score = dot_t(query, kv[0, s]) * scaling
            scores[s] = jnp.where((position < lengths[s, me]) | extra, score, masked_score)
    for block in range(0, slots, step):
        wait_all(values[block : block + step])
        for s in range(block, block + step):
            kv[1, s, last, :] = with_fresh(kv[1, s, last, :], value1[s : s + 1], value2[s : s + 1])
            score = scores[s]
            weights = jnp.exp2(score - jnp.max(score, 1, keepdims=True))
            probs = (weights * (1.0 / jnp.sum(weights, 1, keepdims=True))).astype(bf16)
            attended = dot(probs, kv[1, s]).astype(bf16).astype(f32)
            mixed[s] = attended[:heads]
            mixed[slots + s] = attended[heads:]

    vacated = is_row((slots, HEAD), counts, leave, me)
    for h in range(heads):
        columns = slice(h * HEAD, (h + 1) * HEAD)
        served = mixed[slots:, h, :]
        served_rows[:slots, columns] = mixed[:slots, h, :]
        served_rows[slots : 2 * slots, columns] = jnp.where(vacated, own[:, width + HEAD :], served)
        served_rows[2 * slots :, columns] = served
    stacked = served_rows[...].astype(bf16)
    attn1_out[...] = served_rows[:slots].astype(bf16)
    own_out[...] = served_rows[slots : 2 * slots]

    partials = dot_t(stacked, twice(tables[:, 2]))
    mask = own_adapter(ids, me, slots, lanes, rank)
    rank_rows[...] = jnp.where(mask, partials[2 * slots :], 0.0)
    for_own = jnp.where(mask, jnp.where(low, partials[:slots], partials[slots : 2 * slots]), 0.0)
    for_other = moved_in(jnp.zeros_like(for_own), rank_rows, counts, land, leave, me)
    peers = sums_out.shape[0] // 2
    lower = me < half
    for_own, for_other = halves(for_own), halves(for_other)
    in_low = jnp.where(lower, for_own, for_other).astype(bf16)
    in_high = jnp.where(lower, for_other, for_own).astype(bf16)
    sent = jnp.concatenate([mixed[slots + leave[m, me]] for m in range(moves)], 0).astype(bf16)
    for peer in range(peers):
        sums_out[peer, : 2 * slots] = in_low
        sums_out[peers + peer, : 2 * slots] = in_high
        sums_out[peer, 2 * slots :] = sent
        sums_out[peers + peer, 2 * slots :] = sent
    other = jnp.bitwise_xor(me, half)
    row = row_iota((slots, lanes))
    for m in range(moves):
        lands = (row == land[m, other]) & (m < counts[other])
        landing_out[m] = jnp.where(lands, 1.0, 0.0)


def delta_kernel(sums, up, up_other, attn2_own, landing, delta1_out, delta2_out, attn2_out):
    lower = lax.axis_index("inst") < lax.axis_size("inst") // 2
    peers = sums.shape[0] // 2
    lanes = sums.shape[2]
    slots, width = attn2_out.shape
    heads = width // HEAD
    moves = landing.shape[0]
    totals = []
    for part in range(2):
        total = sums[part * peers, : 2 * slots].astype(f32)
        for peer in range(1, peers):
            total = total + sums[part * peers + peer, : 2 * slots].astype(f32)
        totals.append(total[:slots] + total[slots:])
    own = jnp.where(lower, totals[0], totals[1])
    got = jnp.where(lower, totals[1], totals[0])
    low = lane_iota((slots, lanes)) < lanes // 2
    rank1 = jnp.where(low, own, 0.0)
    rank2_own = jnp.where(low, pltpu.roll(own, lanes // 2, 1), 0.0)
    rank2_got = jnp.where(low, 0.0, got)
    lands = [landing[m] > 0.5 for m in range(moves)]
    rank2 = rank2_own
    for m in range(moves):
        rank2 = jnp.where(lands[m], rank2_got, rank2)
    table = jnp.concatenate([up[...], up_other[...]], 0)
    delta = dot(jnp.concatenate([rank1, rank2], 0).astype(bf16), table)
    delta1_out[...] = delta[:slots].astype(bf16)
    delta2_out[...] = delta[slots:].astype(bf16)
    sender = jnp.where(lower, peers, 0) + lax.axis_index("tensor")
    moved = sums[sender, 2 * slots :, :].astype(f32)
    for h in range(heads):
        columns = slice(h * HEAD, (h + 1) * HEAD)
        rows = attn2_own[:, columns]
        for m in range(moves):
            rows = jnp.where(lands[m], moved[m * heads + h : m * heads + h + 1], rows)
        attn2_out[:, columns] = rows.astype(bf16)


def per_device(
    query_first,
    query_second,
    hidden_first,
    hidden_second,
    fresh_first,
    fresh_second,
    kv_cache,
    adapters,
    lengths,
    adapter_ids,
    move_counts,
    move_from,
    move_to,
):
    inst_count = lax.axis_size("inst")
    peers = lax.axis_size("tensor")
    half = inst_count // 2
    swap = [(i, i ^ half) for i in range(inst_count)]
    groups = [
        [i * peers + t for t in range(peers)] + [(i + half) * peers + t for t in range(peers)] for i in range(half)
    ]
    _, slots, width = query_first.shape
    _, pool, _, rank, _ = adapters.shape
    moves = move_from.shape[1]
    lanes = 2 * pool * rank
    heads = width // HEAD
    cached = kv_cache.shape[3]
    lengths, adapter_ids, move_from, move_to = lengths.T, adapter_ids.T, move_from.T, move_to.T

    hbm = pl.BlockSpec(memory_space=pltpu.HBM)
    vmem = pl.BlockSpec(memory_space=pltpu.VMEM)
    params = pltpu.CompilerParams(vmem_limit_bytes=16 * 1024 * 1024)

    def shape(dims, dtype):
        return jax.ShapeDtypeStruct(dims, dtype)

    def far(*arrays):
        return [pltpu.with_memory_space_constraint(array, pltpu.HBM) for array in arrays]

    def near(*arrays):
        return [pltpu.with_memory_space_constraint(array, pltpu.VMEM) for array in arrays]

    by_slot = pltpu.SMEM((slots, inst_count), jnp.int32)
    by_inst = pltpu.SMEM((inst_count,), jnp.int32)
    by_move = pltpu.SMEM((moves, inst_count), jnp.int32)
    rows = shape((slots, 2 * width + 2 * HEAD), bf16)

    first, second, tables, up_own = pl.pallas_call(
        stage_kernel,
        name="stage",
        out_shape=(rows, rows, shape(adapters.shape[1:], bf16), shape((pool, rank, width), bf16)),
        in_specs=[hbm] * 7,
        out_specs=(vmem,) * 4,
        scratch_shapes=[
            pltpu.VMEM((2, slots, 2, HEAD), bf16),
            pltpu.VMEM((2, slots, 2, HEAD), f32),
            pltpu.SemaphoreType.DMA((8,)),
        ],
        compiler_params=params,
    )(*far(hidden_first, hidden_second, query_first, query_second, fresh_first, fresh_second, adapters))
    up_own = up_own.reshape(pool * rank, width)
    up_other = lax.ppermute(up_own, "inst", swap)
    other = lax.ppermute(second, "inst", swap)

    ranks = pl.pallas_call(
        rank_kernel,
        name="rank_partials",
        out_shape=shape((peers, slots, lanes), f32),
        in_specs=[hbm] * 4 + [vmem] * 4,
        out_specs=vmem,
        scratch_shapes=[
            by_slot, by_inst, by_move, by_move,
            pltpu.VMEM((slots, lanes), f32),
            pltpu.SemaphoreType.DMA((4,)),
        ],
        cost_estimate=pl.CostEstimate(flops=2 * 10**10, bytes_accessed=10**8, transcendentals=0),
        compiler_params=params,
    )(*far(adapter_ids, move_counts, move_from, move_to), *near(first, second, other, tables))
    ranks = lax.all_to_all(ranks, "tensor", 0, 0)

    attn1, attn2_own, landing, sums = pl.pallas_call(
        attention_kernel,
        name="attention",
        out_shape=(
            shape((slots, width), bf16),
            shape((slots, width), f32),
            shape((moves, slots, lanes), f32),
            shape((2 * peers, 2 * slots + moves * heads, lanes), bf16),
        ),
        in_specs=[hbm] * 6 + [vmem] * 6,
        out_specs=(vmem,) * 4,
        scratch_shapes=[
            by_slot, by_slot, by_inst, by_move, by_move,
            pltpu.VMEM((2, slots, cached, HEAD), bf16),
            pltpu.VMEM((slots, width + 2 * HEAD), f32),
            pltpu.VMEM((heads, 2 * slots, HEAD), f32),
            pltpu.VMEM((slots, 2 * heads, cached), f32),
            pltpu.VMEM((2 * slots, heads, HEAD), f32),
            pltpu.VMEM((3 * slots, width), f32),
            pltpu.VMEM((slots, lanes), f32),
            pltpu.SemaphoreType.DMA((5 + 2 * slots,)),
        ],
        compiler_params=params,
    )(
        *far(lengths, adapter_ids, move_counts, move_from, move_to, kv_cache),
        *near(ranks, first, second, other, tables, up_other),
    )
    sums = lax.all_to_all(sums, ("inst", "tensor"), 0, 0, axis_index_groups=groups)

    delta1, delta2, attn2 = pl.pallas_call(
        delta_kernel,
        name="deltas",
        out_shape=(shape((slots, width), bf16),) * 3,
        in_specs=[vmem] * 5,
        out_specs=(vmem,) * 3,
        compiler_params=params,
    )(*near(sums, up_own, up_other, attn2_own, landing))
    return (attn1[None], delta1[None], attn2[None], delta2[None])


def solution(mesh):
    row = P("inst", None, "tensor")
    fresh = P("inst", None, None, "tensor")
    whole = P("inst", None, None, None, "tensor")
    return jax.shard_map(
        per_device,
        mesh=mesh,
        in_specs=(row, row, row, row, fresh, fresh, whole, whole, P(), P(), P(), P(), P()),
        out_specs=(row, row, row, row),
        check_vma=False,
    )
```

time: 55.8 us -> 53.3 us (0.955)
  blocking collectives: 0 us -> 36.9 us
  starting transfers between devices: 36.3 us -> 8.01 us
  waiting for transfers between devices: 9.84 us -> 0.01 us
  local copies, waits for them, and re-layouts: 0.92 us -> 0 us
    all_to_all x0 -> x2, blocking collectives: none -> 36.9 us  [the longest x1 21.7 us: per_device(): ranks = lax.all_to_all(ranks, 'tensor', 0, 0)]
    all_to_all x2 -> x0, starting transfers between devices: 18.8 us -> none  [the longest x1 11.5 us: per_device(): ranks = lax.all_to_all(ranks, 'tensor', 0, 0)]
    ppermute x4 -> x2, starting transfers between devices: 17.5 us -> 8.01 us  [the longest x1 6.09 us: per_device(): other = lax.ppermute(second, 'inst', swap)]
    all_to_all x2 -> x0, waiting for transfers between devices: 5.98 us -> none  [the longest x1 3.49 us: per_device(): lax.all_to_all(ranks_two, ('inst', 'tensor'), 0, 0, axis_index_groups=gro...]
    ppermute x4 -> x2, waiting for transfers between devices: 3.86 us -> 0.01 us  [the longest x1 0.01 us: per_device(): up_other = lax.ppermute(up_own, 'inst', swap)]
    slice x1 -> x0, local copies, waits for them, and re-layouts: 0.92 us -> none  [per_device(): adapters[0, :, 3].reshape(pool * rank, width)]
    pallas_call x1 -> x2, Pallas kernels: 1.88 us -> 2.14 us  [the longest x1 1.28 us: per_device(): pl.pallas_call(stage_kernel, name='stage', out_shape=(rows, rows, shape(a...]
  transfers between devices with their start and end apart: 6 -> 2, of which waited for: 4 -> 0; matrix products, arithmetic and copies ran while one was open for 2% -> 0% of each run, Pallas kernels for 9% -> 2%
where the time goes in v3:
time: 53.3 us; the launch traced here: 53 us
  blocking collectives  36.9 us (69%)
  starting transfers between devices  8.01 us (15%)
  Pallas kernels  7.36 us (14%)
  between operations  0.68 us (1%)
    all_to_all x1, blocking collectives, per_device(): ranks = lax.all_to_all(ranks, 'tensor', 0, 0)  21.7 us
    all_to_all x1, blocking collectives, per_device(): lax.all_to_all(sums, ('inst', 'tensor'), 0, 0, axis_index_groups=groups)  15.3 us
    ppermute x1, starting transfers between devices, per_device(): other = lax.ppermute(second, 'inst', swap)  6.09 us
    pallas_call x1, Pallas kernels, per_device(): pl.pallas_call(attention_kernel, name='attention', out_shape=(shape((slot...  4.39 us
    ppermute x1, starting transfers between devices, per_device(): up_other = lax.ppermute(up_own, 'inst', swap)  1.92 us
    pallas_call x1, Pallas kernels, per_device(): pl.pallas_call(stage_kernel, name='stage', out_shape=(rows, rows, shape(a...  1.28 us
  transfers between devices with their start and end apart: 2, of which 0 were waited for; matrix products, arithmetic and copies ran while one was open for 0% of the time, Pallas kernels for 2%

profile of v3, /device:TPU:48, one launch (start us, length us, event | category | flops | bytes accessed | tf_op | source)
XLA Modules:
  0.0 53.0 jit_solution(9587121768783024367)
XLA Ops:
  0.6 1.3 %stage.1 = (bf16[8,2304]{1,0:T(8,128)(2,1)S(1)}, bf16[8,2304]{1,0:T(8,128)(2,1)S(1)}, bf16[4,4,16,1024]{3,2,1,0:T(8,128)(2,1)S(1)}, bf16[4,16,1024]{2,1,0:T(8,128)(2,1)S(1)}) custom-call(bf16[1,8,1024]{2,1,0:T(8,128)(2,1)} %h1.1, bf16[1,8,1024]{2,1,0:T(8,128)(2,1)} %h2.1, bf16[1,8,1024]{2,1,0:T(8,128)(2,1)} %q1.1, bf16[1,8,1024]{2,1,0:T(8,128)(2,1)} %q2.1, ...), custom_call_target="tpu_custom_call" | custom-call | tf_op jit(solution)/shard_map/stage/pallas_call | solution.py:315
  1.9 6.1 %collective-permute-start = (bf16[8,2304]{1,0:T(8,128)(2,1)S(1)}, bf16[8,2304]{1,0:T(8,128)(2,1)S(1)}, u32[]{:S(2)}, u32[]{:S(2)}) collective-permute-start(bf16[8,2304]{1,0:T(8,128)(2,1)S(1)} %get-tuple-element.16.second.second_rows), channel_id=1, source_target_pairs={{0,256},{8,264},{16,272},{24,280},{32,288},{40,296},{48,304},{56,3... | collective-permute-start | bytes 110600 | tf_op jit(solution)/shard_map/ppermute | solution.py:330
  8.0 1.9 %collective-permute-start.1 = (bf16[64,1024]{1,0:T(8,128)(2,1)S(1)}, bf16[64,1024]{1,0:T(8,128)(2,1)S(1)}, u32[]{:S(2)}, u32[]{:S(2)}) collective-permute-start(bf16[64,1024]{1,0:T(8,128)(2,1)S(1)} %bitcast.9), channel_id=1, source_target_pairs={{0,256},{8,264},{16,272},{24,280},{32,288},{40,296},{48,304},{56,3... | collective-permute-start | bytes 393224 | tf_op jit(solution)/shard_map/ppermute | solution.py:329
  9.9 0.0 collective-permute-done.other.got_rows
  10.0 0.9 %rank_partials.1 = f32[8,8,128]{2,1,0:T(8,128)S(1)} custom-call(s32[8,64]{1,0:T(8,128)} %bitcast.12, s32[64]{0:T(128)} %counts_at.3, s32[4,64]{1,0:T(4,128)} %bitcast.14, s32[4,64]{1,0:T(4,128)} %bitcast.16, bf16[8,2304]{1,0:T(8,128)(2,1)S(1)} %get-tuple-element.15.first.first_rows, bf16[8,2304]{1,0:T(8,128)(2,1)S(1)} %get-tuple-element.16.second.second_rows, ...), custom_call_target="tpu_custom_call" | custom-call | flops 20000000000 | bytes 100000000 | tf_op jit(solution)/shard_map/rank_partials/pallas_call | solution.py:332
  10.8 21.7 %all_to_all.10.ranks = f32[8,8,128]{2,1,0:T(8,128)S(1)} all-to-all(f32[8,8,128]{2,1,0:T(8,128)S(1)} %rank_partials.1), channel_id=1, replica_groups=mesh['inst'=64,'tensor'=8] {'tensor'}, dimensions={0} | all-to-all | bytes 65536 | tf_op jit(solution)/shard_map/all_to_all | solution.py:346
  32.5 0.0 collective-permute-done.1.up_other
  32.5 4.4 %attention.1 = (bf16[8,1024]{1,0:T(8,128)(2,1)}, f32[8,1024]{1,0:T(8,128)S(1)}, f32[4,8,128]{2,1,0:T(8,128)S(1)}, bf16[16,48,128]{2,1,0:T(8,128)(2,1)S(1)}) custom-call(s32[8,64]{1,0:T(8,128)} %bitcast.11, s32[8,64]{1,0:T(8,128)} %bitcast.13, s32[64]{0:T(128)} %counts_at.3, s32[4,64]{1,0:T(4,128)} %bitcast.15, s32[4,64]{1,0:T(4,128)} %bitcast.17, ...), custom_call_target="tpu_custom_call" | custom-call | tf_op jit(solution)/shard_map/attention/pallas_call | solution.py:348
  36.9 15.3 %all_to_all.11.sums = bf16[16,48,128]{2,1,0:T(8,128)(2,1)S(1)} all-to-all(bf16[16,48,128]{2,1,0:T(8,128)(2,1)S(1)} %get-tuple-element.20), channel_id=1, replica_groups={{0,1,2,3,4,5,6,7,256,257,258,259,260,261,262,263},{8,9,10,11,12,13,14,1..., dimensions={0} | all-to-all | bytes 393216 | tf_op jit(solution)/shard_map/all_to_all | solution.py:375
  52.1 0.8 %deltas.1 = (bf16[8,1024]{1,0:T(8,128)(2,1)}, bf16[8,1024]{1,0:T(8,128)(2,1)}, bf16[8,1024]{1,0:T(8,128)(2,1)}) custom-call(bf16[16,48,128]{2,1,0:T(8,128)(2,1)S(1)} %all_to_all.11.sums, bf16[64,1024]{1,0:T(8,128)(2,1)S(1)} %bitcast.10, bf16[64,1024]{1,0:T(8,128)(2,1)S(1)} %collective-permute-done.1.up_other, f32[8,1024]{1,0:T(8,128)S(1)} %get-tuple-element.21.attn2_own, ...), custom_call_target="tpu_custom_call" | custom-call | tf_op jit(solution)/shard_map/deltas/pallas_call | solution.py:377
Async XLA Ops:
  1.9 8.0 %collective-permute-start = (bf16[8,2304]{1,0:T(8,128)(2,1)S(1)}, bf16[8,2304]{1,0:T(8,128)(2,1)S(1)}, u32[]{:S(2)}, u32[]{:S(2)}) collective-permute-start(bf16[8,2304]{1,0:T(8,128)(2,1)S(1)} %get-tuple-element.16.second.second_rows), channel_id=1, source_target_pairs={{0,256},{8,264},{16,272},{24,280},{32,288},{40,296},{48,304},{56,3... | collective-permute-start | bytes 110600 | tf_op jit(solution)/shard_map/ppermute | solution.py:330
  8.0 24.5 %collective-permute-start.1 = (bf16[64,1024]{1,0:T(8,128)(2,1)S(1)}, bf16[64,1024]{1,0:T(8,128)(2,1)S(1)}, u32[]{:S(2)}, u32[]{:S(2)}) collective-permute-start(bf16[64,1024]{1,0:T(8,128)(2,1)S(1)} %bitcast.9), channel_id=1, source_target_pairs={{0,256},{8,264},{16,272},{24,280},{32,288},{40,296},{48,304},{56,3... | collective-permute-start | bytes 393224 | tf_op jit(solution)/shard_map/ppermute | solution.py:329

commit v4 on v3

--- a/solution.py
+++ b/solution.py
@@ -34,28 +34,13 @@
     return lax.broadcasted_iota(jnp.int32, shape, 1)
 
 
-def own_adapter(ids, me, slots, lanes, rank):
-    rows, columns = row_iota((slots, lanes)), lane_iota((slots, lanes))
-    adapter = jnp.zeros((slots, lanes), jnp.int32)
-    for s in range(slots):
-        adapter = jnp.where(rows == s, ids[s, me], adapter)
-    return lax.rem(columns, lanes // 2) // rank == adapter
-
-
-def moved_in(base, rows_at, counts, targets, sources, me):
-    row = row_iota(base.shape)
-    for m in range(targets.shape[0]):
-        picked = rows_at[pl.ds(sources[m, me], 1), :]
-        base = jnp.where((row == targets[m, me]) & (m < counts[me]), picked, base)
+def moved_in(base, rows, arrives):
+    for r in range(rows.shape[0]):
+        taken = arrives[r] > 0.5
+        if base.shape[1] != taken.shape[1]:
+            taken = jnp.concatenate([taken] * (base.shape[1] // taken.shape[1]), 1)
+        base = jnp.where(taken, rows[r : r + 1], base)
     return base
-
-
-def is_row(shape, counts, table, instance):
-    row = row_iota(shape)
-    found = jnp.zeros(shape, jnp.bool_)
-    for m in range(table.shape[0]):
-        found = found | ((row == table[m, instance]) & (m < counts[instance]))
-    return found
 
 
 def start_all(pairs, sems, first=0):
@@ -76,71 +61,72 @@
 
 
 def stage_kernel(
-    h1, h2, q1, q2, f1, f2, tables_at,
-    first_out, second_out, tables_out, up_out,
-    fresh, fresh_wide, sems,
+    ids_at, counts_at, leave_at, land_at, lengths_at, h1, h2, q1, q2, f1, f2, tables_at,
+    first_out, second_out, tables_out, up_out, arrives_out, adapter_out, lengths_out,
+    ids, counts, leave, land, lengths, fresh, fresh_wide, sems,
 ):
+    me = lax.axis_index("inst")
     width = h1.shape[2]
     copies = start_all(
         [
             (f1.at[0], fresh.at[0]), (f2.at[0], fresh.at[1]),
             (h1.at[0], first_out.at[:, :width]), (h2.at[0], second_out.at[:, :width]),
             (q1.at[0], first_out.at[:, width : 2 * width]), (q2.at[0], second_out.at[:, width : 2 * width]),
+            (ids_at, ids), (counts_at, counts), (leave_at, leave), (land_at, land), (lengths_at, lengths),
             (tables_at.at[0, :, 3], up_out), (tables_at.at[0], tables_out),
         ],
         sems,
     )
+    slots, lanes = adapter_out.shape
+    rank = tables_out.shape[2]
     wait_all(copies[:2])
     fresh_wide[...] = fresh[...].astype(f32)
     for step, out in enumerate((first_out, second_out)):
         out[:, 2 * width : 2 * width + HEAD] = fresh_wide[step, :, 0, :].astype(bf16)
         out[:, 2 * width + HEAD :] = fresh_wide[step, :, 1, :].astype(bf16)
-    wait_all(copies[2:])
-
-
-def rank_kernel(
-    ids_at, counts_at, leave_at, land_at, first, second, other, tables,
-    out,
-    ids, counts, leave, land, scratch, sems,
-):
-    me = lax.axis_index("inst")
-    copies = start_all([(ids_at, ids), (counts_at, counts), (leave_at, leave), (land_at, land)], sems)
-    peers, _, lanes = out.shape
-    slots = first.shape[0]
+    wait_all(copies[6:11])
+    row, lane = row_iota((slots, lanes)), lane_iota((slots, lanes))
+    adapter = jnp.zeros((slots, lanes), jnp.int32)
+    length = jnp.zeros((slots, lanes), jnp.int32)
+    target = jnp.full((slots, lanes), -1, jnp.int32)
+    for s in range(slots):
+        adapter = jnp.where(row == s, ids[s, me], adapter)
+        length = jnp.where(row == s, lengths[s, me], length)
+    for m in range(leave.shape[0]):
+        target = jnp.where((row == leave[m, me]) & (m < counts[me]), land[m, me], target)
+    adapter_out[...] = jnp.where(lax.rem(lane, lanes // 2) // rank == adapter, 1.0, 0.0)
+    lengths_out[...] = length
+    for r in range(slots):
+        arrives_out[r] = jnp.where(target == r, 1.0, 0.0)
+    wait_all(copies[2:6] + copies[11:])
+
+
+def rank_kernel(first, second, other, tables, arrives, adapter, out):
+    peers, slots, lanes = out.shape
     width = tables.shape[3]
-    rank = tables.shape[2]
-    table = twice(tables[:, 0])
     hidden = [ref[:, :width].astype(f32) for ref in (first, second, other)]
-    partials = dot_t(jnp.concatenate(hidden, 0).astype(bf16), table)
-    scratch[...] = partials[2 * slots :]
-    wait_all(copies)
-    moved = moved_in(partials[slots : 2 * slots], scratch, counts, leave, land, me)
+    partials = dot_t(jnp.concatenate(hidden, 0).astype(bf16), twice(tables[:, 0]))
+    moved = moved_in(partials[slots : 2 * slots], partials[2 * slots :], arrives)
     both = jnp.where(lane_iota((slots, lanes)) < lanes // 2, partials[:slots], moved)
-    both = jnp.where(own_adapter(ids, me, slots, lanes, rank), both, 0.0)
+    both = jnp.where(adapter[...] > 0.5, both, 0.0)
     for peer in range(peers):
         out[peer] = both
 
 
 def attention_kernel(
-    lengths_at, ids_at, counts_at, leave_at, land_at, cache_at,
-    ranks, first_rows, second_rows, got_rows, tables, up_other,
+    counts_at, leave_at, land_at, kv, ranks, first_rows, second_rows, got_rows, tables, up_other,
+    arrives, adapter, lengths,
     attn1_out, own_out, landing_out, sums_out,
-    lengths, ids, counts, leave, land,
-    kv, other_rows, queries, scores, mixed, served_rows, rank_rows, sems,
+    counts, leave, land, queries, scores, mixed, served_rows, rank_rows, sems,
 ):
     me = lax.axis_index("inst")
     half = lax.axis_size("inst") // 2
     slots, width = attn1_out.shape
     heads = width // HEAD
-    cached = kv.shape[2]
+    cached = kv.shape[3]
     lanes = ranks.shape[2]
-    rank = tables.shape[2]
     moves = leave.shape[0]
-    small = start_all(
-        [(counts_at, counts), (leave_at, leave), (land_at, land), (lengths_at, lengths), (ids_at, ids)], sems
-    )
-    keys = start_all([(cache_at.at[0, s, 0], kv.at[0, s]) for s in range(slots)], sems, 5)
-    values = start_all([(cache_at.at[0, s, 1], kv.at[1, s]) for s in range(slots)], sems, 5 + slots)
+    small = start_all([(counts_at, counts), (leave_at, leave), (land_at, land)], sems)
 
     lane = lane_iota((slots, lanes))
     low = lane < lanes // 2
@@ -149,11 +135,9 @@
         total = total + ranks[peer]
     total = jnp.concatenate([jnp.where(low, total, 0.0), jnp.where(low, 0.0, total)], 0).astype(bf16)
     update = dot(total, twice(tables[:, 1]))
-    other_rows[...] = got_rows[:, width:].astype(f32)
     first = first_rows[:, width:].astype(f32)
     own = second_rows[:, width:].astype(f32)
-    wait_all(small)
-    second = moved_in(own, other_rows, counts, leave, land, me)
+    second = moved_in(own, got_rows[:, width:].astype(f32), arrives)
     query1 = (first[:, :width] + update[:slots]).astype(bf16).astype(f32)
     query2 = (second[:, :width] + update[slots:]).astype(bf16).astype(f32)
     for h in range(heads):
@@ -174,26 +158,30 @@
         tile = jnp.where(tail_row == 14, one, tile.astype(f32))
         return jnp.where(tail_row == 15, two, tile).astype(bf16)
 
-    step = 2
-    for block in range(0, slots, step):
-        wait_all(keys[block : block + step])
-        for s in range(block, block + step):
-            kv[0, s, last, :] = with_fresh(kv[0, s, last, :], key1[s : s + 1], key2[s : s + 1])
-            query = jnp.concatenate([queries[:, s, :], queries[:, slots + s, :]], 0).astype(bf16)
-            score = dot_t(query, kv[0, s]) * scaling
-            scores[s] = jnp.where((position < lengths[s, me]) | extra, score, masked_score)
-    for block in range(0, slots, step):
-        wait_all(values[block : block + step])
-        for s in range(block, block + step):
-            kv[1, s, last, :] = with_fresh(kv[1, s, last, :], value1[s : s + 1], value2[s : s + 1])
-            score = scores[s]
-            weights = jnp.exp2(score - jnp.max(score, 1, keepdims=True))
-            probs = (weights * (1.0 / jnp.sum(weights, 1, keepdims=True))).astype(bf16)
-            attended = dot(probs, kv[1, s]).astype(bf16).astype(f32)
-            mixed[s] = attended[:heads]
-            mixed[slots + s] = attended[heads:]
-
-    vacated = is_row((slots, HEAD), counts, leave, me)
+    def with_tail(s, which, one, two):
+        body = kv[0, s, which, : cached - 128]
+        keep = kv[0, s, which, cached - 128 : cached - 16]
+        return body, jnp.concatenate([keep, with_fresh(kv[0, s, which, last, :], one, two)], 0)
+
+    for s in range(slots):
+        body, tail = with_tail(s, 0, key1[s : s + 1], key2[s : s + 1])
+        query = jnp.concatenate([queries[:, s, :], queries[:, slots + s, :]], 0).astype(bf16)
+        score = jnp.concatenate([dot_t(query, body), dot_t(query, tail)], 1) * scaling
+        scores[s] = jnp.where((position < lengths[s : s + 1, :1]) | extra, score, masked_score)
+    for s in range(slots):
+        body, tail = with_tail(s, 1, value1[s : s + 1], value2[s : s + 1])
+        score = scores[s]
+        weights = jnp.exp2(score - jnp.max(score, 1, keepdims=True))
+        probs = (weights * (1.0 / jnp.sum(weights, 1, keepdims=True))).astype(bf16)
+        attended = dot(probs[:, : cached - 128], body) + dot(probs[:, cached - 128 :], tail)
+        attended = attended.astype(bf16).astype(f32)
+        mixed[s] = attended[:heads]
+        mixed[slots + s] = attended[heads:]
+
+    vacated = arrives[0]
+    for r in range(1, slots):
+        vacated = vacated + arrives[r]
+    vacated = vacated > 0.5
     for h in range(heads):
         columns = slice(h * HEAD, (h + 1) * HEAD)
         served = mixed[slots:, h, :]
@@ -205,10 +193,15 @@
     own_out[...] = served_rows[slots : 2 * slots]
 
     partials = dot_t(stacked, twice(tables[:, 2]))
-    mask = own_adapter(ids, me, slots, lanes, rank)
+    mask = adapter[...] > 0.5
+    for_own = jnp.where(mask, jnp.where(low, partials[:slots], partials[slots : 2 * slots]), 0.0)
     rank_rows[...] = jnp.where(mask, partials[2 * slots :], 0.0)
-    for_own = jnp.where(mask, jnp.where(low, partials[:slots], partials[slots : 2 * slots]), 0.0)
-    for_other = moved_in(jnp.zeros_like(for_own), rank_rows, counts, land, leave, me)
+    for_other = jnp.zeros_like(for_own)
+    row = row_iota((slots, lanes))
+    wait_all(small)
+    for m in range(moves):
+        lands = (row == land[m, me]) & (m < counts[me])
+        for_other = jnp.where(lands, rank_rows[pl.ds(leave[m, me], 1), :], for_other)
     peers = sums_out.shape[0] // 2
     lower = me < half
     for_own, for_other = halves(for_own), halves(for_other)
@@ -221,13 +214,13 @@
         sums_out[peer, 2 * slots :] = sent
         sums_out[peers + peer, 2 * slots :] = sent
     other = jnp.bitwise_xor(me, half)
-    row = row_iota((slots, lanes))
     for m in range(moves):
         lands = (row == land[m, other]) & (m < counts[other])
         landing_out[m] = jnp.where(lands, 1.0, 0.0)
 
 
-def delta_kernel(sums, up, up_other, attn2_own, landing, delta1_out, delta2_out, attn2_out):
+def delta_kernel(sums, up, up_other, attn1, attn2_own, landing, attn1_out, delta1_out, attn2_out, delta2_out):
+    attn1_out[...] = attn1[...]
     lower = lax.axis_index("inst") < lax.axis_size("inst") // 2
     peers = sums.shape[0] // 2
     lanes = sums.shape[2]
@@ -312,19 +305,33 @@
     by_move = pltpu.SMEM((moves, inst_count), jnp.int32)
     rows = shape((slots, 2 * width + 2 * HEAD), bf16)
 
-    first, second, tables, up_own = pl.pallas_call(
+    first, second, tables, up_own, arrives, adapter, slot_lengths = pl.pallas_call(
         stage_kernel,
         name="stage",
-        out_shape=(rows, rows, shape(adapters.shape[1:], bf16), shape((pool, rank, width), bf16)),
-        in_specs=[hbm] * 7,
-        out_specs=(vmem,) * 4,
+        out_shape=(
+            rows,
+            rows,
+            shape(adapters.shape[1:], bf16),
+            shape((pool, rank, width), bf16),
+            shape((slots, slots, lanes), f32),
+            shape((slots, lanes), f32),
+            shape((slots, lanes), jnp.int32),
+        ),
+        in_specs=[hbm] * 12,
+        out_specs=(vmem,) * 7,
         scratch_shapes=[
+            by_slot, by_inst, by_move, by_move, by_slot,
             pltpu.VMEM((2, slots, 2, HEAD), bf16),
             pltpu.VMEM((2, slots, 2, HEAD), f32),
-            pltpu.SemaphoreType.DMA((8,)),
+            pltpu.SemaphoreType.DMA((13,)),
         ],
         compiler_params=params,
-    )(*far(hidden_first, hidden_second, query_first, query_second, fresh_first, fresh_second, adapters))
+    )(
+        *far(
+            adapter_ids, move_counts, move_from, move_to, lengths,
+            hidden_first, hidden_second, query_first, query_second, fresh_first, fresh_second, adapters,
+        )
+    )
     up_own = up_own.reshape(pool * rank, width)
     up_other = lax.ppermute(up_own, "inst", swap)
     other = lax.ppermute(second, "inst", swap)
@@ -333,16 +340,11 @@
         rank_kernel,
         name="rank_partials",
         out_shape=shape((peers, slots, lanes), f32),
-        in_specs=[hbm] * 4 + [vmem] * 4,
+        in_specs=[vmem] * 6,
         out_specs=vmem,
-        scratch_shapes=[
-            by_slot, by_inst, by_move, by_move,
-            pltpu.VMEM((slots, lanes), f32),
-            pltpu.SemaphoreType.DMA((4,)),
-        ],
         cost_estimate=pl.CostEstimate(flops=2 * 10**10, bytes_accessed=10**8, transcendentals=0),
         compiler_params=params,
-    )(*far(adapter_ids, move_counts, move_from, move_to), *near(first, second, other, tables))
+    )(*near(first, second, other, tables, arrives, adapter))
     ranks = lax.all_to_all(ranks, "tensor", 0, 0)
 
     attn1, attn2_own, landing, sums = pl.pallas_call(
@@ -354,34 +356,32 @@
             shape((moves, slots, lanes), f32),
             shape((2 * peers, 2 * slots + moves * heads, lanes), bf16),
         ),
-        in_specs=[hbm] * 6 + [vmem] * 6,
+        in_specs=[hbm] * 3 + [vmem] * 10,
         out_specs=(vmem,) * 4,
         scratch_shapes=[
-            by_slot, by_slot, by_inst, by_move, by_move,
-            pltpu.VMEM((2, slots, cached, HEAD), bf16),
-            pltpu.VMEM((slots, width + 2 * HEAD), f32),
+            by_inst, by_move, by_move,
             pltpu.VMEM((heads, 2 * slots, HEAD), f32),
             pltpu.VMEM((slots, 2 * heads, cached), f32),
             pltpu.VMEM((2 * slots, heads, HEAD), f32),
             pltpu.VMEM((3 * slots, width), f32),
             pltpu.VMEM((slots, lanes), f32),
-            pltpu.SemaphoreType.DMA((5 + 2 * slots,)),
+            pltpu.SemaphoreType.DMA((3,)),
         ],
         compiler_params=params,
     )(
-        *far(lengths, adapter_ids, move_counts, move_from, move_to, kv_cache),
-        *near(ranks, first, second, other, tables, up_other),
+        *far(move_counts, move_from, move_to),
+        *near(kv_cache, ranks, first, second, other, tables, up_other, arrives, adapter, slot_lengths),
     )
     sums = lax.all_to_all(sums, ("inst", "tensor"), 0, 0, axis_index_groups=groups)
 
-    delta1, delta2, attn2 = pl.pallas_call(
+    attn1, delta1, attn2, delta2 = pl.pallas_call(
         delta_kernel,
         name="deltas",
-        out_shape=(shape((slots, width), bf16),) * 3,
-        in_specs=[vmem] * 5,
-        out_specs=(vmem,) * 3,
+        out_shape=(shape((slots, width), bf16),) * 4,
+        in_specs=[vmem] * 6,
+        out_specs=(vmem,) * 4,
         compiler_params=params,
-    )(*near(sums, up_own, up_other, attn2_own, landing))
+    )(*near(sums, up_own, up_other, attn1, attn2_own, landing))
     return (attn1[None], delta1[None], attn2[None], delta2[None])
 
 

time: 53.3 us -> 50.3 us (0.944)
  the two profiles are of different devices: /device:TPU:48 before, /device:TPU:40 now
where the time goes in v4:
time: 50.3 us; the launch traced here: 50 us
  blocking collectives  37.2 us (74%)
  starting transfers between devices  8.01 us (16%)
  Pallas kernels  4.16 us (8%)
  between operations  0.69 us (1%)
    all_to_all x1, blocking collectives, per_device(): ranks = lax.all_to_all(ranks, 'tensor', 0, 0)  21.9 us
    all_to_all x1, blocking collectives, per_device(): lax.all_to_all(sums, ('inst', 'tensor'), 0, 0, axis_index_groups=groups)  15.3 us
    ppermute x1, starting transfers between devices, per_device(): other = lax.ppermute(second, 'inst', swap)  6.09 us
    ppermute x1, starting transfers between devices, per_device(): up_other = lax.ppermute(up_own, 'inst', swap)  1.92 us
    pallas_call x1, Pallas kernels, per_device(): pl.pallas_call(attention_kernel, name='attention', out_shape=(shape((slot...  1.8 us
    pallas_call x1, Pallas kernels, per_device(): pl.pallas_call(stage_kernel, name='stage', out_shape=(rows, rows, shape(a...  1.33 us
  transfers between devices with their start and end apart: 2, of which 0 were waited for; matrix products, arithmetic and copies ran while one was open for 0% of the time, Pallas kernels for 0%

profile of v4, /device:TPU:40, one launch (start us, length us, event | category | flops | bytes accessed | tf_op | source)
XLA Modules:
  0.0 50.0 jit_solution(2990940337442986431)
XLA Ops:
  0.6 1.3 %stage.1 = (bf16[8,2304]{1,0:T(8,128)(2,1)S(1)}, bf16[8,2304]{1,0:T(8,128)(2,1)S(1)}, bf16[4,4,16,1024]{3,2,1,0:T(8,128)(2,1)S(1)}, bf16[4,16,1024]{2,1,0:T(8,12...) custom-call(s32[8,64]{1,0:T(8,128)} %bitcast.15, s32[64]{0:T(128)} %counts_at.3, ...), custom_call_target="tpu_custom_call" | custom-call | tf_op jit(solution)/shard_map/stage/pallas_call | solution.py:308
  2.0 6.1 %collective-permute-start = (bf16[8,2304]{1,0:T(8,128)(2,1)S(1)}, bf16[8,2304]{1,0:T(8,128)(2,1)S(1)}, u32[]{:S(2)}, u32[]{:S(2)}) collective-permute-start(bf16[8,2304]{1,0:T(8,128)(2,1)S(1)} %get-tuple-element.20.second.second_rows), channel_id=1, source_target_pairs={{0,256},{8,264},{16,272},{24,280},{32,288},{40,296},{48,304},{56,3... | collective-permute-start | bytes 110600 | tf_op jit(solution)/shard_map/ppermute | solution.py:337
  8.1 1.9 %collective-permute-start.1 = (bf16[64,1024]{1,0:T(8,128)(2,1)S(1)}, bf16[64,1024]{1,0:T(8,128)(2,1)S(1)}, u32[]{:S(2)}, u32[]{:S(2)}) collective-permute-start(bf16[64,1024]{1,0:T(8,128)(2,1)S(1)} %bitcast.9), channel_id=1, source_target_pairs={{0,256},{8,264},{16,272},{24,280},{32,288},{40,296},{48,304},{56,3... | collective-permute-start | bytes 393224 | tf_op jit(solution)/shard_map/ppermute | solution.py:336
  10.0 0.0 collective-permute-done.other.got_rows
  10.0 0.0 copy-start
  10.0 0.2 rank_partials.1
  10.2 21.9 %all_to_all.10.ranks = f32[8,8,128]{2,1,0:T(8,128)S(1)} all-to-all(f32[8,8,128]{2,1,0:T(8,128)S(1)} %rank_partials.1), channel_id=1, replica_groups=mesh['inst'=64,'tensor'=8] {'tensor'}, dimensions={0} | all-to-all | bytes 65536 | tf_op jit(solution)/shard_map/all_to_all | solution.py:348
  32.1 0.0 collective-permute-done.1.up_other
  32.1 0.0 copy-done
  32.1 1.8 %attention.1 = (bf16[8,1024]{1,0:T(8,128)(2,1)S(1)}, f32[8,1024]{1,0:T(8,128)S(1)}, f32[4,8,128]{2,1,0:T(8,128)S(1)}, bf16[16,48,128]{2,1,0:T(8,128)(2,1)S(1)}) custom-call(s32[64]{0:T(128)} %counts_at.3, s32[4,64]{1,0:T(4,128)} %bitcast.12, s32[4,64]{1,0:T(4,128)} %bitcast.14, bf16[1,8,2,1024,128]{4,3,2,1,0:T(8,128)(2,1)S(1)} %copy-done, ...), custom_call_target="tpu_custom_call" | custom-call | tf_op jit(solution)/shard_map/attention/pallas_call | solution.py:350
  34.0 15.3 %all_to_all.11.sums = bf16[16,48,128]{2,1,0:T(8,128)(2,1)S(1)} all-to-all(bf16[16,48,128]{2,1,0:T(8,128)(2,1)S(1)} %get-tuple-element.26), channel_id=1, replica_groups={{0,1,2,3,4,5,6,7,256,257,258,259,260,261,262,263},{8,9,10,11,12,13,14,1..., dimensions={0} | all-to-all | bytes 393216 | tf_op jit(solution)/shard_map/all_to_all | solution.py:375
  49.2 0.8 %deltas.1 = (bf16[8,1024]{1,0:T(8,128)(2,1)}, bf16[8,1024]{1,0:T(8,128)(2,1)}, bf16[8,1024]{1,0:T(8,128)(2,1)}, bf16[8,1024]{1,0:T(8,128)(2,1)}) custom-call(bf16[16,48,128]{2,1,0:T(8,128)(2,1)S(1)} %all_to_all.11.sums, bf16[64,1024]{1,0:T(8,128)(2,1)S(1)} %bitcast.10, bf16[64,1024]{1,0:T(8,128)(2,1)S(1)} %collective-permute-done.1.up_other, ...), custom_call_target="tpu_custom_call" | custom-call | tf_op jit(solution)/shard_map/deltas/pallas_call | solution.py:377
Async XLA Ops:
  2.0 8.0 %collective-permute-start = (bf16[8,2304]{1,0:T(8,128)(2,1)S(1)}, bf16[8,2304]{1,0:T(8,128)(2,1)S(1)}, u32[]{:S(2)}, u32[]{:S(2)}) collective-permute-start(bf16[8,2304]{1,0:T(8,128)(2,1)S(1)} %get-tuple-element.20.second.second_rows), channel_id=1, source_target_pairs={{0,256},{8,264},{16,272},{24,280},{32,288},{40,296},{48,304},{56,3... | collective-permute-start | bytes 110600 | tf_op jit(solution)/shard_map/ppermute | solution.py:337
  8.1 24.1 %collective-permute-start.1 = (bf16[64,1024]{1,0:T(8,128)(2,1)S(1)}, bf16[64,1024]{1,0:T(8,128)(2,1)S(1)}, u32[]{:S(2)}, u32[]{:S(2)}) collective-permute-start(bf16[64,1024]{1,0:T(8,128)(2,1)S(1)} %bitcast.9), channel_id=1, source_target_pairs={{0,256},{8,264},{16,272},{24,280},{32,288},{40,296},{48,304},{56,3... | collective-permute-start | bytes 393224 | tf_op jit(solution)/shard_map/ppermute | solution.py:336
  10.0 22.1 %copy-start = (bf16[1,8,2,1024,128]{4,3,2,1,0:T(8,128)(2,1)S(1)}, bf16[1,8,2,1024,128]{4,3,2,1,0:T(8,128)(2,1)}, u32[]{:S(2)}) copy-start(bf16[1,8,2,1024,128]{4,3,2,1,0:T(8,128)(2,1)} %kv.1) | copy-start | bytes 12582916

commit v5 on v4

--- a/solution.py
+++ b/solution.py
@@ -247,7 +247,7 @@
     delta = dot(jnp.concatenate([rank1, rank2], 0).astype(bf16), table)
     delta1_out[...] = delta[:slots].astype(bf16)
     delta2_out[...] = delta[slots:].astype(bf16)
-    sender = jnp.where(lower, peers, 0) + lax.axis_index("tensor")
+    sender = jnp.where(lower, peers, 0) + peers - 1 - lax.axis_index("tensor")
     moved = sums[sender, 2 * slots :, :].astype(f32)
     for h in range(heads):
         columns = slice(h * HEAD, (h + 1) * HEAD)
@@ -276,9 +276,8 @@
     peers = lax.axis_size("tensor")
     half = inst_count // 2
     swap = [(i, i ^ half) for i in range(inst_count)]
-    groups = [
-        [i * peers + t for t in range(peers)] + [(i + half) * peers + t for t in range(peers)] for i in range(half)
-    ]
+    teams = [[i * peers + t for t in reversed(range(peers))] for i in range(inst_count)]
+    pairs = [teams[i] + teams[i + half] for i in range(half)]
     _, slots, width = query_first.shape
     _, pool, _, rank, _ = adapters.shape
     moves = move_from.shape[1]
@@ -345,7 +344,7 @@
         cost_estimate=pl.CostEstimate(flops=2 * 10**10, bytes_accessed=10**8, transcendentals=0),
         compiler_params=params,
     )(*near(first, second, other, tables, arrives, adapter))
-    ranks = lax.all_to_all(ranks, "tensor", 0, 0)
+    ranks = lax.all_to_all(ranks, ("inst", "tensor"), 0, 0, axis_index_groups=teams)
 
     attn1, attn2_own, landing, sums = pl.pallas_call(
         attention_kernel,
@@ -372,7 +371,7 @@
         *far(move_counts, move_from, move_to),
         *near(kv_cache, ranks, first, second, other, tables, up_other, arrives, adapter, slot_lengths),
     )
-    sums = lax.all_to_all(sums, ("inst", "tensor"), 0, 0, axis_index_groups=groups)
+    sums = lax.all_to_all(sums, ("inst", "tensor"), 0, 0, axis_index_groups=pairs)
 
     attn1, delta1, attn2, delta2 = pl.pallas_call(
         delta_kernel,

time: 50.3 us -> 45.4 us (0.903)
  the two profiles are of different devices: /device:TPU:40 before, /device:TPU:80 now
where the time goes in v5:
time: 45.4 us; the launch traced here: 45.1 us
  blocking collectives  29.8 us (66%)
  starting transfers between devices  8.01 us (18%)
  Pallas kernels  4.16 us (9%)
  waiting for transfers between devices  2.47 us (5%)
  between operations  0.68 us (1%)
    all_to_all x1, blocking collectives, per_device(): lax.all_to_all(sums, ('inst', 'tensor'), 0, 0, axis_index_groups=pairs)  16.1 us
    all_to_all x1, blocking collectives, per_device(): lax.all_to_all(ranks, ('inst', 'tensor'), 0, 0, axis_index_groups=teams)  13.7 us
    ppermute x1, starting transfers between devices, per_device(): other = lax.ppermute(second, 'inst', swap)  6.09 us
    ppermute x1, waiting for transfers between devices, per_device(): other = lax.ppermute(second, 'inst', swap)  2.47 us
    ppermute x1, starting transfers between devices, per_device(): up_other = lax.ppermute(up_own, 'inst', swap)  1.92 us
    pallas_call x1, Pallas kernels, per_device(): pl.pallas_call(attention_kernel, name='attention', out_shape=(shape((slot...  1.8 us
    pallas_call x1, Pallas kernels, per_device(): pl.pallas_call(stage_kernel, name='stage', out_shape=(rows, rows, shape(a...  1.33 us
  transfers between devices with their start and end apart: 2, of which 1 were waited for; matrix products, arithmetic and copies ran while one was open for 0% of the time, Pallas kernels for 0%

profile of v5, /device:TPU:80, one launch (start us, length us, event | category | flops | bytes accessed | tf_op | source)
XLA Modules:
  0.0 45.1 jit_solution(4844383974868051105)
XLA Ops:
  0.6 1.3 %stage.1 = (bf16[8,2304]{1,0:T(8,128)(2,1)S(1)}, bf16[8,2304]{1,0:T(8,128)(2,1)S(1)}, bf16[4,4,16,1024]{3,2,1,0:T(8,128)(2,1)S(1)}, bf16[4,16,1024]{2,1,0:T(8,12...) custom-call(s32[8,64]{1,0:T(8,128)} %bitcast.15, s32[64]{0:T(128)} %counts_at.3, ...), custom_call_target="tpu_custom_call" | custom-call | tf_op jit(solution)/shard_map/stage/pallas_call | solution.py:307
  2.0 6.1 %collective-permute-start = (bf16[8,2304]{1,0:T(8,128)(2,1)S(1)}, bf16[8,2304]{1,0:T(8,128)(2,1)S(1)}, u32[]{:S(2)}, u32[]{:S(2)}) collective-permute-start(bf16[8,2304]{1,0:T(8,128)(2,1)S(1)} %get-tuple-element.20.second.second_rows), channel_id=1, source_target_pairs={{0,256},{8,264},{16,272},{24,280},{32,288},{40,296},{48,304},{56,3... | collective-permute-start | bytes 110600 | tf_op jit(solution)/shard_map/ppermute | solution.py:336
  8.1 1.9 %collective-permute-start.1 = (bf16[64,1024]{1,0:T(8,128)(2,1)S(1)}, bf16[64,1024]{1,0:T(8,128)(2,1)S(1)}, u32[]{:S(2)}, u32[]{:S(2)}) collective-permute-start(bf16[64,1024]{1,0:T(8,128)(2,1)S(1)} %bitcast.9), channel_id=1, source_target_pairs={{0,256},{8,264},{16,272},{24,280},{32,288},{40,296},{48,304},{56,3... | collective-permute-start | bytes 393224 | tf_op jit(solution)/shard_map/ppermute | solution.py:335
  10.0 2.5 %collective-permute-done.other.got_rows = bf16[8,2304]{1,0:T(8,128)(2,1)S(1)} collective-permute-done((bf16[8,2304]{1,0:T(8,128)(2,1)S(1)}, bf16[8,2304]{1,0:T(8,128)(2,1)S(1)}, u32[]{:S(2)}, u32[]{:S(2)}) %collective-permute-start) | collective-permute-done | bytes 36896 | tf_op jit(solution)/shard_map/ppermute | solution.py:336
  12.5 0.0 copy-start
  12.5 0.2 rank_partials.1
  12.7 13.7 %all_to_all.10.ranks = f32[8,8,128]{2,1,0:T(8,128)S(1)} all-to-all(f32[8,8,128]{2,1,0:T(8,128)S(1)} %rank_partials.1), channel_id=1, replica_groups={{7,6,5,4,3,2,1,0},{15,14,13,12,11,10,9,8},{23,22,21,20,19,18,17,16},{31..., dimensions={0} | all-to-all | bytes 65536 | tf_op jit(solution)/shard_map/all_to_all | solution.py:347
  26.4 0.0 collective-permute-done.1.up_other
  26.4 0.0 copy-done
  26.4 1.8 %attention.1 = (bf16[8,1024]{1,0:T(8,128)(2,1)S(1)}, f32[8,1024]{1,0:T(8,128)S(1)}, f32[4,8,128]{2,1,0:T(8,128)S(1)}, bf16[16,48,128]{2,1,0:T(8,128)(2,1)S(1)}) custom-call(s32[64]{0:T(128)} %counts_at.3, s32[4,64]{1,0:T(4,128)} %bitcast.12, s32[4,64]{1,0:T(4,128)} %bitcast.14, bf16[1,8,2,1024,128]{4,3,2,1,0:T(8,128)(2,1)S(1)} %copy-done, ...), custom_call_target="tpu_custom_call" | custom-call | tf_op jit(solution)/shard_map/attention/pallas_call | solution.py:349
  28.2 16.1 %all_to_all.11.sums = bf16[16,48,128]{2,1,0:T(8,128)(2,1)S(1)} all-to-all(bf16[16,48,128]{2,1,0:T(8,128)(2,1)S(1)} %get-tuple-element.26), channel_id=1, replica_groups={{7,6,5,4,3,2,1,0,263,262,261,260,259,258,257,256},{15,14,13,12,11,10,9,..., dimensions={0} | all-to-all | bytes 393216 | tf_op jit(solution)/shard_map/all_to_all | solution.py:374
  44.3 0.8 %deltas.1 = (bf16[8,1024]{1,0:T(8,128)(2,1)}, bf16[8,1024]{1,0:T(8,128)(2,1)}, bf16[8,1024]{1,0:T(8,128)(2,1)}, bf16[8,1024]{1,0:T(8,128)(2,1)}) custom-call(bf16[16,48,128]{2,1,0:T(8,128)(2,1)S(1)} %all_to_all.11.sums, bf16[64,1024]{1,0:T(8,128)(2,1)S(1)} %bitcast.10, bf16[64,1024]{1,0:T(8,128)(2,1)S(1)} %collective-permute-done.1.up_other, ...), custom_call_target="tpu_custom_call" | custom-call | tf_op jit(solution)/shard_map/deltas/pallas_call | solution.py:376
Async XLA Ops:
  2.0 10.5 %collective-permute-start = (bf16[8,2304]{1,0:T(8,128)(2,1)S(1)}, bf16[8,2304]{1,0:T(8,128)(2,1)S(1)}, u32[]{:S(2)}, u32[]{:S(2)}) collective-permute-start(bf16[8,2304]{1,0:T(8,128)(2,1)S(1)} %get-tuple-element.20.second.second_rows), channel_id=1, source_target_pairs={{0,256},{8,264},{16,272},{24,280},{32,288},{40,296},{48,304},{56,3... | collective-permute-start | bytes 110600 | tf_op jit(solution)/shard_map/ppermute | solution.py:336
  8.1 18.3 %collective-permute-start.1 = (bf16[64,1024]{1,0:T(8,128)(2,1)S(1)}, bf16[64,1024]{1,0:T(8,128)(2,1)S(1)}, u32[]{:S(2)}, u32[]{:S(2)}) collective-permute-start(bf16[64,1024]{1,0:T(8,128)(2,1)S(1)} %bitcast.9), channel_id=1, source_target_pairs={{0,256},{8,264},{16,272},{24,280},{32,288},{40,296},{48,304},{56,3... | collective-permute-start | bytes 393224 | tf_op jit(solution)/shard_map/ppermute | solution.py:335
  12.5 13.9 %copy-start = (bf16[1,8,2,1024,128]{4,3,2,1,0:T(8,128)(2,1)S(1)}, bf16[1,8,2,1024,128]{4,3,2,1,0:T(8,128)(2,1)}, u32[]{:S(2)}) copy-start(bf16[1,8,2,1024,128]{4,3,2,1,0:T(8,128)(2,1)} %kv.1) | copy-start | bytes 12582916

commit v6 on v5

--- a/solution.py
+++ b/solution.py
@@ -62,7 +62,7 @@
 
 def stage_kernel(
     ids_at, counts_at, leave_at, land_at, lengths_at, h1, h2, q1, q2, f1, f2, tables_at,
-    first_out, second_out, tables_out, up_out, arrives_out, adapter_out, lengths_out,
+    first_out, second_out, tables_out, parcel_out, arrives_out, adapter_out, lengths_out,
     ids, counts, leave, land, lengths, fresh, fresh_wide, sems,
 ):
     me = lax.axis_index("inst")
@@ -73,7 +73,7 @@
             (h1.at[0], first_out.at[:, :width]), (h2.at[0], second_out.at[:, :width]),
             (q1.at[0], first_out.at[:, width : 2 * width]), (q2.at[0], second_out.at[:, width : 2 * width]),
             (ids_at, ids), (counts_at, counts), (leave_at, leave), (land_at, land), (lengths_at, lengths),
-            (tables_at.at[0, :, 3], up_out), (tables_at.at[0], tables_out),
+            (tables_at.at[0], tables_out),
         ],
         sems,
     )
@@ -99,12 +99,18 @@
     for r in range(slots):
         arrives_out[r] = jnp.where(target == r, 1.0, 0.0)
     wait_all(copies[2:6] + copies[11:])
-
-
-def rank_kernel(first, second, other, tables, arrives, adapter, out):
+    ups = tables_out[:, 3].reshape(-1, width)
+    parcel_out[: ups.shape[0]] = ups
+    fresh_rows = second_out[:, 2 * width :].astype(f32)
+    fresh_rows = jnp.concatenate([fresh_rows, jnp.zeros((slots, width - 2 * HEAD), f32)], 1)
+    tail = jnp.concatenate([second_out[:, width : 2 * width].astype(f32), fresh_rows], 0)
+    parcel_out[ups.shape[0] :] = tail.astype(bf16)
+
+
+def rank_kernel(first, second, hidden_other, tables, arrives, adapter, out):
     peers, slots, lanes = out.shape
     width = tables.shape[3]
-    hidden = [ref[:, :width].astype(f32) for ref in (first, second, other)]
+    hidden = [ref[:, :width].astype(f32) for ref in (first, second, hidden_other)]
     partials = dot_t(jnp.concatenate(hidden, 0).astype(bf16), twice(tables[:, 0]))
     moved = moved_in(partials[slots : 2 * slots], partials[2 * slots :], arrives)
     both = jnp.where(lane_iota((slots, lanes)) < lanes // 2, partials[:slots], moved)
@@ -114,7 +120,7 @@
 
 
 def attention_kernel(
-    counts_at, leave_at, land_at, kv, ranks, first_rows, second_rows, got_rows, tables, up_other,
+    counts_at, leave_at, land_at, kv, ranks, first_rows, second_rows, parcel, tables,
     arrives, adapter, lengths,
     attn1_out, own_out, landing_out, sums_out,
     counts, leave, land, queries, scores, mixed, served_rows, rank_rows, sems,
@@ -137,7 +143,8 @@
     update = dot(total, twice(tables[:, 1]))
     first = first_rows[:, width:].astype(f32)
     own = second_rows[:, width:].astype(f32)
-    second = moved_in(own, got_rows[:, width:].astype(f32), arrives)
+    got = parcel[pl.ds(parcel.shape[0] - 2 * slots, 2 * slots), :].astype(f32)
+    second = moved_in(own, jnp.concatenate([got[:slots], got[slots:, : 2 * HEAD]], 1), arrives)
     query1 = (first[:, :width] + update[:slots]).astype(bf16).astype(f32)
     query2 = (second[:, :width] + update[slots:]).astype(bf16).astype(f32)
     for h in range(heads):
@@ -219,7 +226,7 @@
         landing_out[m] = jnp.where(lands, 1.0, 0.0)
 
 
-def delta_kernel(sums, up, up_other, attn1, attn2_own, landing, attn1_out, delta1_out, attn2_out, delta2_out):
+def delta_kernel(sums, tables, parcel, attn1, attn2_own, landing, attn1_out, delta1_out, attn2_out, delta2_out):
     attn1_out[...] = attn1[...]
     lower = lax.axis_index("inst") < lax.axis_size("inst") // 2
     peers = sums.shape[0] // 2
@@ -243,7 +250,8 @@
     rank2 = rank2_own
     for m in range(moves):
         rank2 = jnp.where(lands[m], rank2_got, rank2)
-    table = jnp.concatenate([up[...], up_other[...]], 0)
+    ups = tables[:, 3].reshape(-1, width)
+    table = jnp.concatenate([ups, parcel[: ups.shape[0]]], 0)
     delta = dot(jnp.concatenate([rank1, rank2], 0).astype(bf16), table)
     delta1_out[...] = delta[:slots].astype(bf16)
     delta2_out[...] = delta[slots:].astype(bf16)
@@ -304,14 +312,14 @@
     by_move = pltpu.SMEM((moves, inst_count), jnp.int32)
     rows = shape((slots, 2 * width + 2 * HEAD), bf16)
 
-    first, second, tables, up_own, arrives, adapter, slot_lengths = pl.pallas_call(
+    first, second, tables, parcel, arrives, adapter, slot_lengths = pl.pallas_call(
         stage_kernel,
         name="stage",
         out_shape=(
             rows,
             rows,
             shape(adapters.shape[1:], bf16),
-            shape((pool, rank, width), bf16),
+            shape((pool * rank + 2 * slots, width), bf16),
             shape((slots, slots, lanes), f32),
             shape((slots, lanes), f32),
             shape((slots, lanes), jnp.int32),
@@ -322,7 +330,7 @@
             by_slot, by_inst, by_move, by_move, by_slot,
             pltpu.VMEM((2, slots, 2, HEAD), bf16),
             pltpu.VMEM((2, slots, 2, HEAD), f32),
-            pltpu.SemaphoreType.DMA((13,)),
+            pltpu.SemaphoreType.DMA((12,)),
         ],
         compiler_params=params,
     )(
@@ -331,9 +339,8 @@
             hidden_first, hidden_second, query_first, query_second, fresh_first, fresh_second, adapters,
         )
     )
-    up_own = up_own.reshape(pool * rank, width)
-    up_other = lax.ppermute(up_own, "inst", swap)
-    other = lax.ppermute(second, "inst", swap)
+    parcel_other = lax.ppermute(parcel, "inst", swap)
+    hidden_other = lax.ppermute(hidden_second[0], "inst", swap)
 
     ranks = pl.pallas_call(
         rank_kernel,
@@ -343,7 +350,7 @@
         out_specs=vmem,
         cost_estimate=pl.CostEstimate(flops=2 * 10**10, bytes_accessed=10**8, transcendentals=0),
         compiler_params=params,
-    )(*near(first, second, other, tables, arrives, adapter))
+    )(*near(first, second, hidden_other, tables, arrives, adapter))
     ranks = lax.all_to_all(ranks, ("inst", "tensor"), 0, 0, axis_index_groups=teams)
 
     attn1, attn2_own, landing, sums = pl.pallas_call(
@@ -355,7 +362,7 @@
             shape((moves, slots, lanes), f32),
             shape((2 * peers, 2 * slots + moves * heads, lanes), bf16),
         ),
-        in_specs=[hbm] * 3 + [vmem] * 10,
+        in_specs=[hbm] * 3 + [vmem] * 9,
         out_specs=(vmem,) * 4,
         scratch_shapes=[
             by_inst, by_move, by_move,
@@ -369,7 +376,7 @@
         compiler_params=params,
     )(
         *far(move_counts, move_from, move_to),
-        *near(kv_cache, ranks, first, second, other, tables, up_other, arrives, adapter, slot_lengths),
+        *near(kv_cache, ranks, first, second, parcel_other, tables, arrives, adapter, slot_lengths),
     )
     sums = lax.all_to_all(sums, ("inst", "tensor"), 0, 0, axis_index_groups=pairs)
 
@@ -380,7 +387,7 @@
         in_specs=[vmem] * 6,
         out_specs=(vmem,) * 4,
         compiler_params=params,
-    )(*near(sums, up_own, up_other, attn1, attn2_own, landing))
+    )(*near(sums, tables, parcel_other, attn1, attn2_own, landing))
     return (attn1[None], delta1[None], attn2[None], delta2[None])
 
 

time: 45.4 us -> 44.7 us (0.985)
  the two profiles are of different devices: /device:TPU:80 before, /device:TPU:62 now
where the time goes in v6:
time: 44.7 us; the launch traced here: 44.4 us
  blocking collectives  31.6 us (71%)
  starting transfers between devices  8.01 us (18%)
  Pallas kernels  4.09 us (9%)
  between operations  0.69 us (2%)
    all_to_all x1, blocking collectives, per_device(): lax.all_to_all(sums, ('inst', 'tensor'), 0, 0, axis_index_groups=pairs)  16.2 us
    all_to_all x1, blocking collectives, per_device(): lax.all_to_all(ranks, ('inst', 'tensor'), 0, 0, axis_index_groups=teams)  15.4 us
    ppermute x1, starting transfers between devices, per_device(): hidden_other = lax.ppermute(hidden_second[0], 'inst', swap)  6.09 us
    ppermute x1, starting transfers between devices, per_device(): parcel_other = lax.ppermute(parcel, 'inst', swap)  1.92 us
    pallas_call x1, Pallas kernels, per_device(): pl.pallas_call(attention_kernel, name='attention', out_shape=(shape((slot...  1.78 us
    pallas_call x1, Pallas kernels, per_device(): pl.pallas_call(stage_kernel, name='stage', out_shape=(rows, rows, shape(a...  1.27 us
  transfers between devices with their start and end apart: 2, of which 0 were waited for; matrix products, arithmetic and copies ran while one was open for 0% of the time, Pallas kernels for 3%

profile of v6, /device:TPU:62, one launch (start us, length us, event | category | flops | bytes accessed | tf_op | source)
XLA Modules:
  0.0 44.4 jit_solution(7278465175429996193)
XLA Ops:
  0.6 6.1 %collective-permute-start = (bf16[8,1024]{1,0:T(8,128)(2,1)}, bf16[8,1024]{1,0:T(8,128)(2,1)S(1)}, u32[]{:S(2)}, u32[]{:S(2)}) collective-permute-start(bf16[8,1024]{1,0:T(8,128)(2,1)} %bitcast.9), channel_id=1, source_target_pairs={{0,256},{8,264},{16,272},{24,280},{32,288},{40,296},{48,304},{56,3... | collective-permute-start | bytes 49160 | tf_op jit(solution)/shard_map/ppermute | solution.py:343
  6.7 1.3 %stage.1 = (bf16[8,2304]{1,0:T(8,128)(2,1)S(1)}, bf16[8,2304]{1,0:T(8,128)(2,1)S(1)}, bf16[4,4,16,1024]{3,2,1,0:T(8,128)(2,1)S(1)}, bf16[80,1024]{1,0:T(8,128)(2...) custom-call(s32[8,64]{1,0:T(8,128)} %bitcast.14, s32[64]{0:T(128)} %counts_at.3, ...), custom_call_target="tpu_custom_call" | custom-call | tf_op jit(solution)/shard_map/stage/pallas_call | solution.py:315
  8.0 1.9 %collective-permute-start.1 = (bf16[80,1024]{1,0:T(8,128)(2,1)S(1)}, bf16[80,1024]{1,0:T(8,128)(2,1)S(1)}, u32[]{:S(2)}, u32[]{:S(2)}) collective-permute-start(bf16[80,1024]{1,0:T(8,128)(2,1)S(1)} %get-tuple-element.24), channel_id=1, source_target_pairs={{0,256},{8,264},{16,272},{24,280},{32,288},{40,296},{48,304},{56,3... | collective-permute-start | bytes 491528 | tf_op jit(solution)/shard_map/ppermute | solution.py:342
  9.9 0.0 collective-permute-done.hidden_other
  9.9 0.0 copy-start
  10.0 0.2 rank_partials.1
  10.2 15.4 %all_to_all.10.ranks = f32[8,8,128]{2,1,0:T(8,128)S(1)} all-to-all(f32[8,8,128]{2,1,0:T(8,128)S(1)} %rank_partials.1), channel_id=1, replica_groups={{7,6,5,4,3,2,1,0},{15,14,13,12,11,10,9,8},{23,22,21,20,19,18,17,16},{31..., dimensions={0} | all-to-all | bytes 65536 | tf_op jit(solution)/shard_map/all_to_all | solution.py:354
  25.6 0.0 collective-permute-done.1.parcel
  25.6 0.0 copy-done
  25.6 1.8 %attention.1 = (bf16[8,1024]{1,0:T(8,128)(2,1)S(1)}, f32[8,1024]{1,0:T(8,128)S(1)}, f32[4,8,128]{2,1,0:T(8,128)S(1)}, bf16[16,48,128]{2,1,0:T(8,128)(2,1)S(1)}) custom-call(s32[64]{0:T(128)} %counts_at.3, s32[4,64]{1,0:T(4,128)} %bitcast.11, s32[4,64]{1,0:T(4,128)} %bitcast.13, bf16[1,8,2,1024,128]{4,3,2,1,0:T(8,128)(2,1)S(1)} %copy-done, ...), custom_call_target="tpu_custom_call" | custom-call | tf_op jit(solution)/shard_map/attention/pallas_call | solution.py:356
  27.4 16.2 %all_to_all.11.sums = bf16[16,48,128]{2,1,0:T(8,128)(2,1)S(1)} all-to-all(bf16[16,48,128]{2,1,0:T(8,128)(2,1)S(1)} %get-tuple-element.26), channel_id=1, replica_groups={{7,6,5,4,3,2,1,0,263,262,261,260,259,258,257,256},{15,14,13,12,11,10,9,..., dimensions={0} | all-to-all | bytes 393216 | tf_op jit(solution)/shard_map/all_to_all | solution.py:381
  43.6 0.8 %deltas.1 = (bf16[8,1024]{1,0:T(8,128)(2,1)}, bf16[8,1024]{1,0:T(8,128)(2,1)}, bf16[8,1024]{1,0:T(8,128)(2,1)}, bf16[8,1024]{1,0:T(8,128)(2,1)}) custom-call(bf16[16,48,128]{2,1,0:T(8,128)(2,1)S(1)} %all_to_all.11.sums, bf16[4,4,16,1024]{3,2,1,0:T(8,128)(2,1)S(1)} %get-tuple-element.21.tables, bf16[80,1024]{1,0:T(8,128)(2,1)S(1)} %collective-permute-done.1.parcel, ...), custom_call_target="tpu_custom_call" | custom-call | tf_op jit(solution)/shard_map/deltas/pallas_call | solution.py:383
Async XLA Ops:
  0.6 9.3 %collective-permute-start = (bf16[8,1024]{1,0:T(8,128)(2,1)}, bf16[8,1024]{1,0:T(8,128)(2,1)S(1)}, u32[]{:S(2)}, u32[]{:S(2)}) collective-permute-start(bf16[8,1024]{1,0:T(8,128)(2,1)} %bitcast.9), channel_id=1, source_target_pairs={{0,256},{8,264},{16,272},{24,280},{32,288},{40,296},{48,304},{56,3... | collective-permute-start | bytes 49160 | tf_op jit(solution)/shard_map/ppermute | solution.py:343
  8.0 17.6 %collective-permute-start.1 = (bf16[80,1024]{1,0:T(8,128)(2,1)S(1)}, bf16[80,1024]{1,0:T(8,128)(2,1)S(1)}, u32[]{:S(2)}, u32[]{:S(2)}) collective-permute-start(bf16[80,1024]{1,0:T(8,128)(2,1)S(1)} %get-tuple-element.24), channel_id=1, source_target_pairs={{0,256},{8,264},{16,272},{24,280},{32,288},{40,296},{48,304},{56,3... | collective-permute-start | bytes 491528 | tf_op jit(solution)/shard_map/ppermute | solution.py:342
  9.9 15.7 %copy-start = (bf16[1,8,2,1024,128]{4,3,2,1,0:T(8,128)(2,1)S(1)}, bf16[1,8,2,1024,128]{4,3,2,1,0:T(8,128)(2,1)}, u32[]{:S(2)}) copy-start(bf16[1,8,2,1024,128]{4,3,2,1,0:T(8,128)(2,1)} %kv.1) | copy-start | bytes 12582916

commit v7 on v6

--- a/solution.py
+++ b/solution.py
@@ -173,7 +173,7 @@
     for s in range(slots):
         body, tail = with_tail(s, 0, key1[s : s + 1], key2[s : s + 1])
         query = jnp.concatenate([queries[:, s, :], queries[:, slots + s, :]], 0).astype(bf16)
-        score = jnp.concatenate([dot_t(query, body), dot_t(query, tail)], 1) * scaling
+        score = dot_t(query, jnp.concatenate([body, tail], 0)) * scaling
         scores[s] = jnp.where((position < lengths[s : s + 1, :1]) | extra, score, masked_score)
     for s in range(slots):
         body, tail = with_tail(s, 1, value1[s : s + 1], value2[s : s + 1])

time: 44.7 us -> 44.5 us (level)
  no operation moved by 1% of the time
where the time goes in v7:
time: 44.5 us; the launch traced here: 44.2 us
  blocking collectives  31.6 us (71%)
  starting transfers between devices  8.01 us (18%)
  Pallas kernels  3.86 us (9%)
  between operations  0.69 us (2%)
    all_to_all x1, blocking collectives, per_device(): lax.all_to_all(sums, ('inst', 'tensor'), 0, 0, axis_index_groups=pairs)  16.2 us
    all_to_all x1, blocking collectives, per_device(): lax.all_to_all(ranks, ('inst', 'tensor'), 0, 0, axis_index_groups=teams)  15.4 us
    ppermute x1, starting transfers between devices, per_device(): hidden_other = lax.ppermute(hidden_second[0], 'inst', swap)  6.09 us
    ppermute x1, starting transfers between devices, per_device(): parcel_other = lax.ppermute(parcel, 'inst', swap)  1.92 us
    pallas_call x1, Pallas kernels, per_device(): pl.pallas_call(attention_kernel, name='attention', out_shape=(shape((slot...  1.55 us
    pallas_call x1, Pallas kernels, per_device(): pl.pallas_call(stage_kernel, name='stage', out_shape=(rows, rows, shape(a...  1.27 us
  transfers between devices with their start and end apart: 2, of which 0 were waited for; matrix products, arithmetic and copies ran while one was open for 0% of the time, Pallas kernels for 3%

profile of v7, /device:TPU:62, one launch (start us, length us, event | category | flops | bytes accessed | tf_op | source)
XLA Modules:
  0.0 44.2 jit_solution(42123212044212238)
XLA Ops:
  0.6 6.1 %collective-permute-start = (bf16[8,1024]{1,0:T(8,128)(2,1)}, bf16[8,1024]{1,0:T(8,128)(2,1)S(1)}, u32[]{:S(2)}, u32[]{:S(2)}) collective-permute-start(bf16[8,1024]{1,0:T(8,128)(2,1)} %bitcast.9), channel_id=1, source_target_pairs={{0,256},{8,264},{16,272},{24,280},{32,288},{40,296},{48,304},{56,3... | collective-permute-start | bytes 49160 | tf_op jit(solution)/shard_map/ppermute | solution.py:343
  6.7 1.3 %stage.1 = (bf16[8,2304]{1,0:T(8,128)(2,1)S(1)}, bf16[8,2304]{1,0:T(8,128)(2,1)S(1)}, bf16[4,4,16,1024]{3,2,1,0:T(8,128)(2,1)S(1)}, bf16[80,1024]{1,0:T(8,128)(2...) custom-call(s32[8,64]{1,0:T(8,128)} %bitcast.14, s32[64]{0:T(128)} %counts_at.3, ...), custom_call_target="tpu_custom_call" | custom-call | tf_op jit(solution)/shard_map/stage/pallas_call | solution.py:315
  8.0 1.9 %collective-permute-start.1 = (bf16[80,1024]{1,0:T(8,128)(2,1)S(1)}, bf16[80,1024]{1,0:T(8,128)(2,1)S(1)}, u32[]{:S(2)}, u32[]{:S(2)}) collective-permute-start(bf16[80,1024]{1,0:T(8,128)(2,1)S(1)} %get-tuple-element.24), channel_id=1, source_target_pairs={{0,256},{8,264},{16,272},{24,280},{32,288},{40,296},{48,304},{56,3... | collective-permute-start | bytes 491528 | tf_op jit(solution)/shard_map/ppermute | solution.py:342
  9.9 0.0 collective-permute-done.hidden_other
  9.9 0.0 copy-start
  10.0 0.2 rank_partials.1
  10.2 15.4 %all_to_all.10.ranks = f32[8,8,128]{2,1,0:T(8,128)S(1)} all-to-all(f32[8,8,128]{2,1,0:T(8,128)S(1)} %rank_partials.1), channel_id=1, replica_groups={{7,6,5,4,3,2,1,0},{15,14,13,12,11,10,9,8},{23,22,21,20,19,18,17,16},{31..., dimensions={0} | all-to-all | bytes 65536 | tf_op jit(solution)/shard_map/all_to_all | solution.py:354
  25.6 0.0 collective-permute-done.1.parcel
  25.6 0.0 copy-done
  25.6 1.6 %attention.1 = (bf16[8,1024]{1,0:T(8,128)(2,1)S(1)}, f32[8,1024]{1,0:T(8,128)S(1)}, f32[4,8,128]{2,1,0:T(8,128)S(1)}, bf16[16,48,128]{2,1,0:T(8,128)(2,1)S(1)}) custom-call(s32[64]{0:T(128)} %counts_at.3, s32[4,64]{1,0:T(4,128)} %bitcast.11, s32[4,64]{1,0:T(4,128)} %bitcast.13, bf16[1,8,2,1024,128]{4,3,2,1,0:T(8,128)(2,1)S(1)} %copy-done, ...), custom_call_target="tpu_custom_call" | custom-call | tf_op jit(solution)/shard_map/attention/pallas_call | solution.py:356
  27.2 16.2 %all_to_all.11.sums = bf16[16,48,128]{2,1,0:T(8,128)(2,1)S(1)} all-to-all(bf16[16,48,128]{2,1,0:T(8,128)(2,1)S(1)} %get-tuple-element.26), channel_id=1, replica_groups={{7,6,5,4,3,2,1,0,263,262,261,260,259,258,257,256},{15,14,13,12,11,10,9,..., dimensions={0} | all-to-all | bytes 393216 | tf_op jit(solution)/shard_map/all_to_all | solution.py:381
  43.4 0.8 %deltas.1 = (bf16[8,1024]{1,0:T(8,128)(2,1)}, bf16[8,1024]{1,0:T(8,128)(2,1)}, bf16[8,1024]{1,0:T(8,128)(2,1)}, bf16[8,1024]{1,0:T(8,128)(2,1)}) custom-call(bf16[16,48,128]{2,1,0:T(8,128)(2,1)S(1)} %all_to_all.11.sums, bf16[4,4,16,1024]{3,2,1,0:T(8,128)(2,1)S(1)} %get-tuple-element.21.tables, bf16[80,1024]{1,0:T(8,128)(2,1)S(1)} %collective-permute-done.1.parcel, ...), custom_call_target="tpu_custom_call" | custom-call | tf_op jit(solution)/shard_map/deltas/pallas_call | solution.py:383
Async XLA Ops:
  0.6 9.3 %collective-permute-start = (bf16[8,1024]{1,0:T(8,128)(2,1)}, bf16[8,1024]{1,0:T(8,128)(2,1)S(1)}, u32[]{:S(2)}, u32[]{:S(2)}) collective-permute-start(bf16[8,1024]{1,0:T(8,128)(2,1)} %bitcast.9), channel_id=1, source_target_pairs={{0,256},{8,264},{16,272},{24,280},{32,288},{40,296},{48,304},{56,3... | collective-permute-start | bytes 49160 | tf_op jit(solution)/shard_map/ppermute | solution.py:343
  8.0 17.6 %collective-permute-start.1 = (bf16[80,1024]{1,0:T(8,128)(2,1)S(1)}, bf16[80,1024]{1,0:T(8,128)(2,1)S(1)}, u32[]{:S(2)}, u32[]{:S(2)}) collective-permute-start(bf16[80,1024]{1,0:T(8,128)(2,1)S(1)} %get-tuple-element.24), channel_id=1, source_target_pairs={{0,256},{8,264},{16,272},{24,280},{32,288},{40,296},{48,304},{56,3... | collective-permute-start | bytes 491528 | tf_op jit(solution)/shard_map/ppermute | solution.py:342
  9.9 15.7 %copy-start = (bf16[1,8,2,1024,128]{4,3,2,1,0:T(8,128)(2,1)S(1)}, bf16[1,8,2,1024,128]{4,3,2,1,0:T(8,128)(2,1)}, u32[]{:S(2)}) copy-start(bf16[1,8,2,1024,128]{4,3,2,1,0:T(8,128)(2,1)} %kv.1) | copy-start | bytes 12582916

commit v8 on v7

--- a/solution.py
+++ b/solution.py
@@ -62,8 +62,8 @@
 
 def stage_kernel(
     ids_at, counts_at, leave_at, land_at, lengths_at, h1, h2, q1, q2, f1, f2, tables_at,
-    first_out, second_out, tables_out, parcel_out, arrives_out, adapter_out, lengths_out,
-    ids, counts, leave, land, lengths, fresh, fresh_wide, sems,
+    first_out, second_out, down_out, parcel_out, arrives_out, adapter_out, lengths_out,
+    ids, counts, leave, land, lengths, fresh, fresh_wide, up, sems,
 ):
     me = lax.axis_index("inst")
     width = h1.shape[2]
@@ -73,12 +73,12 @@
             (h1.at[0], first_out.at[:, :width]), (h2.at[0], second_out.at[:, :width]),
             (q1.at[0], first_out.at[:, width : 2 * width]), (q2.at[0], second_out.at[:, width : 2 * width]),
             (ids_at, ids), (counts_at, counts), (leave_at, leave), (land_at, land), (lengths_at, lengths),
-            (tables_at.at[0], tables_out),
+            (tables_at.at[0, :, 0], down_out), (tables_at.at[0, :, 3], up),
         ],
         sems,
     )
     slots, lanes = adapter_out.shape
-    rank = tables_out.shape[2]
+    rank = down_out.shape[1]
     wait_all(copies[:2])
     fresh_wide[...] = fresh[...].astype(f32)
     for step, out in enumerate((first_out, second_out)):
@@ -99,7 +99,7 @@
     for r in range(slots):
         arrives_out[r] = jnp.where(target == r, 1.0, 0.0)
     wait_all(copies[2:6] + copies[11:])
-    ups = tables_out[:, 3].reshape(-1, width)
+    ups = up[...].reshape(-1, width)
     parcel_out[: ups.shape[0]] = ups
     fresh_rows = second_out[:, 2 * width :].astype(f32)
     fresh_rows = jnp.concatenate([fresh_rows, jnp.zeros((slots, width - 2 * HEAD), f32)], 1)
@@ -107,11 +107,11 @@
     parcel_out[ups.shape[0] :] = tail.astype(bf16)
 
 
-def rank_kernel(first, second, hidden_other, tables, arrives, adapter, out):
+def rank_kernel(first, second, hidden_other, down, arrives, adapter, out):
     peers, slots, lanes = out.shape
-    width = tables.shape[3]
+    width = down.shape[2]
     hidden = [ref[:, :width].astype(f32) for ref in (first, second, hidden_other)]
-    partials = dot_t(jnp.concatenate(hidden, 0).astype(bf16), twice(tables[:, 0]))
+    partials = dot_t(jnp.concatenate(hidden, 0).astype(bf16), twice(down[...]))
     moved = moved_in(partials[slots : 2 * slots], partials[2 * slots :], arrives)
     both = jnp.where(lane_iota((slots, lanes)) < lanes // 2, partials[:slots], moved)
     both = jnp.where(adapter[...] > 0.5, both, 0.0)
@@ -140,7 +140,7 @@
     for peer in range(1, ranks.shape[0]):
         total = total + ranks[peer]
     total = jnp.concatenate([jnp.where(low, total, 0.0), jnp.where(low, 0.0, total)], 0).astype(bf16)
-    update = dot(total, twice(tables[:, 1]))
+    update = dot(total, twice(tables[0, :, 1]))
     first = first_rows[:, width:].astype(f32)
     own = second_rows[:, width:].astype(f32)
     got = parcel[pl.ds(parcel.shape[0] - 2 * slots, 2 * slots), :].astype(f32)
@@ -199,7 +199,7 @@
     attn1_out[...] = served_rows[:slots].astype(bf16)
     own_out[...] = served_rows[slots : 2 * slots]
 
-    partials = dot_t(stacked, twice(tables[:, 2]))
+    partials = dot_t(stacked, twice(tables[0, :, 2]))
     mask = adapter[...] > 0.5
     for_own = jnp.where(mask, jnp.where(low, partials[:slots], partials[slots : 2 * slots]), 0.0)
     rank_rows[...] = jnp.where(mask, partials[2 * slots :], 0.0)
@@ -250,7 +250,7 @@
     rank2 = rank2_own
     for m in range(moves):
         rank2 = jnp.where(lands[m], rank2_got, rank2)
-    ups = tables[:, 3].reshape(-1, width)
+    ups = tables[0, :, 3].reshape(-1, width)
     table = jnp.concatenate([ups, parcel[: ups.shape[0]]], 0)
     delta = dot(jnp.concatenate([rank1, rank2], 0).astype(bf16), table)
     delta1_out[...] = delta[:slots].astype(bf16)
@@ -312,13 +312,13 @@
     by_move = pltpu.SMEM((moves, inst_count), jnp.int32)
     rows = shape((slots, 2 * width + 2 * HEAD), bf16)
 
-    first, second, tables, parcel, arrives, adapter, slot_lengths = pl.pallas_call(
+    first, second, down, parcel, arrives, adapter, slot_lengths = pl.pallas_call(
         stage_kernel,
         name="stage",
         out_shape=(
             rows,
             rows,
-            shape(adapters.shape[1:], bf16),
+            shape((pool, rank, width), bf16),
             shape((pool * rank + 2 * slots, width), bf16),
             shape((slots, slots, lanes), f32),
             shape((slots, lanes), f32),
@@ -330,7 +330,8 @@
             by_slot, by_inst, by_move, by_move, by_slot,
             pltpu.VMEM((2, slots, 2, HEAD), bf16),
             pltpu.VMEM((2, slots, 2, HEAD), f32),
-            pltpu.SemaphoreType.DMA((12,)),
+            pltpu.VMEM((pool, rank, width), bf16),
+            pltpu.SemaphoreType.DMA((13,)),
         ],
         compiler_params=params,
     )(
@@ -350,7 +351,7 @@
         out_specs=vmem,
         cost_estimate=pl.CostEstimate(flops=2 * 10**10, bytes_accessed=10**8, transcendentals=0),
         compiler_params=params,
-    )(*near(first, second, hidden_other, tables, arrives, adapter))
+    )(*near(first, second, hidden_other, down, arrives, adapter))
     ranks = lax.all_to_all(ranks, ("inst", "tensor"), 0, 0, axis_index_groups=teams)
 
     attn1, attn2_own, landing, sums = pl.pallas_call(
@@ -376,7 +377,7 @@
         compiler_params=params,
     )(
         *far(move_counts, move_from, move_to),
-        *near(kv_cache, ranks, first, second, parcel_other, tables, arrives, adapter, slot_lengths),
+        *near(kv_cache, ranks, first, second, parcel_other, adapters, arrives, adapter, slot_lengths),
     )
     sums = lax.all_to_all(sums, ("inst", "tensor"), 0, 0, axis_index_groups=pairs)
 
@@ -387,7 +388,7 @@
         in_specs=[vmem] * 6,
         out_specs=(vmem,) * 4,
         compiler_params=params,
-    )(*near(sums, tables, parcel_other, attn1, attn2_own, landing))
+    )(*near(sums, adapters, parcel_other, attn1, attn2_own, landing))
     return (attn1[None], delta1[None], attn2[None], delta2[None])
 
 

time: 44.5 us -> 44.4 us (level)
  no operation moved by 1% of the time
where the time goes in v8:
time: 44.4 us; the launch traced here: 44.2 us
  blocking collectives  31.6 us (71%)
  starting transfers between devices  8.01 us (18%)
  Pallas kernels  3.8 us (9%)
  between operations  0.7 us (2%)
    all_to_all x1, blocking collectives, per_device(): lax.all_to_all(sums, ('inst', 'tensor'), 0, 0, axis_index_groups=pairs)  16.2 us
    all_to_all x1, blocking collectives, per_device(): lax.all_to_all(ranks, ('inst', 'tensor'), 0, 0, axis_index_groups=teams)  15.4 us
    ppermute x1, starting transfers between devices, per_device(): hidden_other = lax.ppermute(hidden_second[0], 'inst', swap)  6.09 us
    ppermute x1, starting transfers between devices, per_device(): parcel_other = lax.ppermute(parcel, 'inst', swap)  1.92 us
    pallas_call x1, Pallas kernels, per_device(): pl.pallas_call(attention_kernel, name='attention', out_shape=(shape((slot...  1.56 us
    pallas_call x1, Pallas kernels, per_device(): pl.pallas_call(stage_kernel, name='stage', out_shape=(rows, rows, shape((...  1.2 us
  transfers between devices with their start and end apart: 2, of which 0 were waited for; matrix products, arithmetic and copies ran while one was open for 0% of the time, Pallas kernels for 3%

profile of v8, /device:TPU:62, one launch (start us, length us, event | category | flops | bytes accessed | tf_op | source)
XLA Modules:
  0.0 44.2 jit_solution(2308830294443053268)
XLA Ops:
  0.6 6.1 %collective-permute-start = (bf16[8,1024]{1,0:T(8,128)(2,1)}, bf16[8,1024]{1,0:T(8,128)(2,1)S(1)}, u32[]{:S(2)}, u32[]{:S(2)}) collective-permute-start(bf16[8,1024]{1,0:T(8,128)(2,1)} %bitcast.9), channel_id=1, source_target_pairs={{0,256},{8,264},{16,272},{24,280},{32,288},{40,296},{48,304},{56,3... | collective-permute-start | bytes 49160 | tf_op jit(solution)/shard_map/ppermute | solution.py:344
  6.7 1.2 %stage.1 = (bf16[8,2304]{1,0:T(8,128)(2,1)S(1)}, bf16[8,2304]{1,0:T(8,128)(2,1)S(1)}, bf16[4,16,1024]{2,1,0:T(8,128)(2,1)S(1)}, bf16[80,1024]{1,0:T(8,128)(2,1)S...) custom-call(s32[8,64]{1,0:T(8,128)} %bitcast.14, s32[64]{0:T(128)} %counts_at.3, ...), custom_call_target="tpu_custom_call" | custom-call | tf_op jit(solution)/shard_map/stage/pallas_call | solution.py:315
  7.9 1.9 %collective-permute-start.1 = (bf16[80,1024]{1,0:T(8,128)(2,1)S(1)}, bf16[80,1024]{1,0:T(8,128)(2,1)S(1)}, u32[]{:S(2)}, u32[]{:S(2)}) collective-permute-start(bf16[80,1024]{1,0:T(8,128)(2,1)S(1)} %get-tuple-element.24), channel_id=1, source_target_pairs={{0,256},{8,264},{16,272},{24,280},{32,288},{40,296},{48,304},{56,3... | collective-permute-start | bytes 491528 | tf_op jit(solution)/shard_map/ppermute | solution.py:343
  9.9 0.0 collective-permute-done.hidden_other
  9.9 0.0 copy-start
  9.9 0.0 copy-start.1
  9.9 0.2 rank_partials.1
  10.1 15.4 %all_to_all.10.ranks = f32[8,8,128]{2,1,0:T(8,128)S(1)} all-to-all(f32[8,8,128]{2,1,0:T(8,128)S(1)} %rank_partials.1), channel_id=1, replica_groups={{7,6,5,4,3,2,1,0},{15,14,13,12,11,10,9,8},{23,22,21,20,19,18,17,16},{31..., dimensions={0} | all-to-all | bytes 65536 | tf_op jit(solution)/shard_map/all_to_all | solution.py:355
  25.6 0.0 collective-permute-done.1.parcel
  25.6 0.0 copy-done
  25.6 0.0 copy-done.1
  25.6 1.6 %attention.1 = (bf16[8,1024]{1,0:T(8,128)(2,1)S(1)}, f32[8,1024]{1,0:T(8,128)S(1)}, f32[4,8,128]{2,1,0:T(8,128)S(1)}, bf16[16,48,128]{2,1,0:T(8,128)(2,1)S(1)}) custom-call(s32[64]{0:T(128)} %counts_at.3, s32[4,64]{1,0:T(4,128)} %bitcast.11, s32[4,64]{1,0:T(4,128)} %bitcast.13, bf16[1,8,2,1024,128]{4,3,2,1,0:T(8,128)(2,1)S(1)} %copy-done.1, ...), custom_call_target="tpu_custom_call" | custom-call | tf_op jit(solution)/shard_map/attention/pallas_call | solution.py:357
  27.1 16.2 %all_to_all.11.sums = bf16[16,48,128]{2,1,0:T(8,128)(2,1)S(1)} all-to-all(bf16[16,48,128]{2,1,0:T(8,128)(2,1)S(1)} %get-tuple-element.26), channel_id=1, replica_groups={{7,6,5,4,3,2,1,0,263,262,261,260,259,258,257,256},{15,14,13,12,11,10,9,..., dimensions={0} | all-to-all | bytes 393216 | tf_op jit(solution)/shard_map/all_to_all | solution.py:382
  43.3 0.8 %deltas.1 = (bf16[8,1024]{1,0:T(8,128)(2,1)}, bf16[8,1024]{1,0:T(8,128)(2,1)}, bf16[8,1024]{1,0:T(8,128)(2,1)}, bf16[8,1024]{1,0:T(8,128)(2,1)}) custom-call(bf16[16,48,128]{2,1,0:T(8,128)(2,1)S(1)} %all_to_all.11.sums, bf16[1,4,4,16,1024]{4,3,2,1,0:T(8,128)(2,1)S(1)} %copy-done, bf16[80,1024]{1,0:T(8,128)(2,1)S(1)} %collective-permute-done.1.parcel, ...), custom_call_target="tpu_custom_call" | custom-call | tf_op jit(solution)/shard_map/deltas/pallas_call | solution.py:384
Async XLA Ops:
  0.6 9.2 %collective-permute-start = (bf16[8,1024]{1,0:T(8,128)(2,1)}, bf16[8,1024]{1,0:T(8,128)(2,1)S(1)}, u32[]{:S(2)}, u32[]{:S(2)}) collective-permute-start(bf16[8,1024]{1,0:T(8,128)(2,1)} %bitcast.9), channel_id=1, source_target_pairs={{0,256},{8,264},{16,272},{24,280},{32,288},{40,296},{48,304},{56,3... | collective-permute-start | bytes 49160 | tf_op jit(solution)/shard_map/ppermute | solution.py:344
  7.9 17.6 %collective-permute-start.1 = (bf16[80,1024]{1,0:T(8,128)(2,1)S(1)}, bf16[80,1024]{1,0:T(8,128)(2,1)S(1)}, u32[]{:S(2)}, u32[]{:S(2)}) collective-permute-start(bf16[80,1024]{1,0:T(8,128)(2,1)S(1)} %get-tuple-element.24), channel_id=1, source_target_pairs={{0,256},{8,264},{16,272},{24,280},{32,288},{40,296},{48,304},{56,3... | collective-permute-start | bytes 491528 | tf_op jit(solution)/shard_map/ppermute | solution.py:343
  9.9 15.7 %copy-start = (bf16[1,4,4,16,1024]{4,3,2,1,0:T(8,128)(2,1)S(1)}, bf16[1,4,4,16,1024]{4,3,2,1,0:T(8,128)(2,1)}, u32[]{:S(2)}) copy-start(bf16[1,4,4,16,1024]{4,3,2,1,0:T(8,128)(2,1)} %tables.3) | copy-start | bytes 1572868
  9.9 15.7 %copy-start.1 = (bf16[1,8,2,1024,128]{4,3,2,1,0:T(8,128)(2,1)S(1)}, bf16[1,8,2,1024,128]{4,3,2,1,0:T(8,128)(2,1)}, u32[]{:S(2)}) copy-start(bf16[1,8,2,1024,128]{4,3,2,1,0:T(8,128)(2,1)} %kv.1) | copy-start | bytes 12582916

commit v9 on v8

--- a/solution.py
+++ b/solution.py
@@ -61,7 +61,7 @@
 
 
 def stage_kernel(
-    ids_at, counts_at, leave_at, land_at, lengths_at, h1, h2, q1, q2, f1, f2, tables_at,
+    ids_at, counts_at, leave_at, land_at, lengths_at, h1, h2, q2, f2, tables_at,
     first_out, second_out, down_out, parcel_out, arrives_out, adapter_out, lengths_out,
     ids, counts, leave, land, lengths, fresh, fresh_wide, up, sems,
 ):
@@ -69,9 +69,8 @@
     width = h1.shape[2]
     copies = start_all(
         [
-            (f1.at[0], fresh.at[0]), (f2.at[0], fresh.at[1]),
-            (h1.at[0], first_out.at[:, :width]), (h2.at[0], second_out.at[:, :width]),
-            (q1.at[0], first_out.at[:, width : 2 * width]), (q2.at[0], second_out.at[:, width : 2 * width]),
+            (f2.at[0], fresh), (h1.at[0], first_out),
+            (h2.at[0], second_out.at[:, :width]), (q2.at[0], second_out.at[:, width : 2 * width]),
             (ids_at, ids), (counts_at, counts), (leave_at, leave), (land_at, land), (lengths_at, lengths),
             (tables_at.at[0, :, 0], down_out), (tables_at.at[0, :, 3], up),
         ],
@@ -79,12 +78,11 @@
     )
     slots, lanes = adapter_out.shape
     rank = down_out.shape[1]
-    wait_all(copies[:2])
+    wait_all(copies[:1])
     fresh_wide[...] = fresh[...].astype(f32)
-    for step, out in enumerate((first_out, second_out)):
-        out[:, 2 * width : 2 * width + HEAD] = fresh_wide[step, :, 0, :].astype(bf16)
-        out[:, 2 * width + HEAD :] = fresh_wide[step, :, 1, :].astype(bf16)
-    wait_all(copies[6:11])
+    second_out[:, 2 * width : 2 * width + HEAD] = fresh_wide[:, 0, :].astype(bf16)
+    second_out[:, 2 * width + HEAD :] = fresh_wide[:, 1, :].astype(bf16)
+    wait_all(copies[4:9])
     row, lane = row_iota((slots, lanes)), lane_iota((slots, lanes))
     adapter = jnp.zeros((slots, lanes), jnp.int32)
     length = jnp.zeros((slots, lanes), jnp.int32)
@@ -98,7 +96,7 @@
     lengths_out[...] = length
     for r in range(slots):
         arrives_out[r] = jnp.where(target == r, 1.0, 0.0)
-    wait_all(copies[2:6] + copies[11:])
+    wait_all(copies[1:4] + copies[9:])
     ups = up[...].reshape(-1, width)
     parcel_out[: ups.shape[0]] = ups
     fresh_rows = second_out[:, 2 * width :].astype(f32)
@@ -120,10 +118,10 @@
 
 
 def attention_kernel(
-    counts_at, leave_at, land_at, kv, ranks, first_rows, second_rows, parcel, tables,
+    counts_at, leave_at, land_at, kv, ranks, base1, fresh1, second_rows, parcel, tables,
     arrives, adapter, lengths,
     attn1_out, own_out, landing_out, sums_out,
-    counts, leave, land, queries, scores, mixed, served_rows, rank_rows, sems,
+    counts, leave, land, queries, scores, mixed, served_rows, rank_rows, fresh_wide, sems,
 ):
     me = lax.axis_index("inst")
     half = lax.axis_size("inst") // 2
@@ -141,17 +139,17 @@
         total = total + ranks[peer]
     total = jnp.concatenate([jnp.where(low, total, 0.0), jnp.where(low, 0.0, total)], 0).astype(bf16)
     update = dot(total, twice(tables[0, :, 1]))
-    first = first_rows[:, width:].astype(f32)
+    fresh_wide[...] = fresh1[0].astype(f32)
     own = second_rows[:, width:].astype(f32)
     got = parcel[pl.ds(parcel.shape[0] - 2 * slots, 2 * slots), :].astype(f32)
     second = moved_in(own, jnp.concatenate([got[:slots], got[slots:, : 2 * HEAD]], 1), arrives)
-    query1 = (first[:, :width] + update[:slots]).astype(bf16).astype(f32)
+    query1 = (base1[0].astype(f32) + update[:slots]).astype(bf16).astype(f32)
     query2 = (second[:, :width] + update[slots:]).astype(bf16).astype(f32)
     for h in range(heads):
         columns = slice(h * HEAD, (h + 1) * HEAD)
         queries[h, :slots] = query1[:, columns]
         queries[h, slots:] = query2[:, columns]
-    key1, value1 = first[:, width : width + HEAD], first[:, width + HEAD :]
+    key1, value1 = fresh_wide[:, 0, :], fresh_wide[:, 1, :]
     key2, value2 = second[:, width : width + HEAD], second[:, width + HEAD :]
 
     scaling = math.log2(math.e) / math.sqrt(HEAD)
@@ -316,7 +314,7 @@
         stage_kernel,
         name="stage",
         out_shape=(
-            rows,
+            shape((slots, width), bf16),
             rows,
             shape((pool, rank, width), bf16),
             shape((pool * rank + 2 * slots, width), bf16),
@@ -324,20 +322,20 @@
             shape((slots, lanes), f32),
             shape((slots, lanes), jnp.int32),
         ),
-        in_specs=[hbm] * 12,
+        in_specs=[hbm] * 10,
         out_specs=(vmem,) * 7,
         scratch_shapes=[
             by_slot, by_inst, by_move, by_move, by_slot,
-            pltpu.VMEM((2, slots, 2, HEAD), bf16),
-            pltpu.VMEM((2, slots, 2, HEAD), f32),
+            pltpu.VMEM((slots, 2, HEAD), bf16),
+            pltpu.VMEM((slots, 2, HEAD), f32),
             pltpu.VMEM((pool, rank, width), bf16),
-            pltpu.SemaphoreType.DMA((13,)),
+            pltpu.SemaphoreType.DMA((11,)),
         ],
         compiler_params=params,
     )(
         *far(
             adapter_ids, move_counts, move_from, move_to, lengths,
-            hidden_first, hidden_second, query_first, query_second, fresh_first, fresh_second, adapters,
+            hidden_first, hidden_second, query_second, fresh_second, adapters,
         )
     )
     parcel_other = lax.ppermute(parcel, "inst", swap)
@@ -363,7 +361,7 @@
             shape((moves, slots, lanes), f32),
             shape((2 * peers, 2 * slots + moves * heads, lanes), bf16),
         ),
-        in_specs=[hbm] * 3 + [vmem] * 9,
+        in_specs=[hbm] * 3 + [vmem] * 10,
         out_specs=(vmem,) * 4,
         scratch_shapes=[
             by_inst, by_move, by_move,
@@ -372,12 +370,13 @@
             pltpu.VMEM((2 * slots, heads, HEAD), f32),
             pltpu.VMEM((3 * slots, width), f32),
             pltpu.VMEM((slots, lanes), f32),
+            pltpu.VMEM((slots, 2, HEAD), f32),
             pltpu.SemaphoreType.DMA((3,)),
         ],
         compiler_params=params,
     )(
         *far(move_counts, move_from, move_to),
-        *near(kv_cache, ranks, first, second, parcel_other, adapters, arrives, adapter, slot_lengths),
+        *near(kv_cache, ranks, query_first, fresh_first, second, parcel_other, adapters, arrives, adapter, slot_lengths),
     )
     sums = lax.all_to_all(sums, ("inst", "tensor"), 0, 0, axis_index_groups=pairs)
 

time: 44.4 us -> 44.4 us (level)
  no operation moved by 1% of the time
where the time goes in v9:
time: 44.4 us; the launch traced here: 44.1 us
  blocking collectives  31.6 us (71%)
  starting transfers between devices  8.01 us (18%)
  Pallas kernels  3.76 us (8%)
  between operations  0.73 us (2%)
    all_to_all x1, blocking collectives, per_device(): lax.all_to_all(sums, ('inst', 'tensor'), 0, 0, axis_index_groups=pairs)  16.2 us
    all_to_all x1, blocking collectives, per_device(): lax.all_to_all(ranks, ('inst', 'tensor'), 0, 0, axis_index_groups=teams)  15.4 us
    ppermute x1, starting transfers between devices, per_device(): hidden_other = lax.ppermute(hidden_second[0], 'inst', swap)  6.09 us
    ppermute x1, starting transfers between devices, per_device(): parcel_other = lax.ppermute(parcel, 'inst', swap)  1.92 us
    pallas_call x1, Pallas kernels, per_device(): pl.pallas_call(attention_kernel, name='attention', out_shape=(shape((slot...  1.57 us
    pallas_call x1, Pallas kernels, per_device(): pl.pallas_call(stage_kernel, name='stage', out_shape=(shape((slots, width...  1.16 us
  transfers between devices with their start and end apart: 2, of which 0 were waited for; matrix products, arithmetic and copies ran while one was open for 0% of the time, Pallas kernels for 3%

profile of v9, /device:TPU:62, one launch (start us, length us, event | category | flops | bytes accessed | tf_op | source)
XLA Modules:
  0.0 44.1 jit_solution(17696500902712937091)
XLA Ops:
  0.6 6.1 %collective-permute-start = (bf16[8,1024]{1,0:T(8,128)(2,1)}, bf16[8,1024]{1,0:T(8,128)(2,1)S(1)}, u32[]{:S(2)}, u32[]{:S(2)}) collective-permute-start(bf16[8,1024]{1,0:T(8,128)(2,1)} %bitcast.9), channel_id=1, source_target_pairs={{0,256},{8,264},{16,272},{24,280},{32,288},{40,296},{48,304},{56,3... | collective-permute-start | bytes 49160 | tf_op jit(solution)/shard_map/ppermute | solution.py:342
  6.7 1.2 %stage.1 = (bf16[8,1024]{1,0:T(8,128)(2,1)S(1)}, bf16[8,2304]{1,0:T(8,128)(2,1)S(1)}, bf16[4,16,1024]{2,1,0:T(8,128)(2,1)S(1)}, bf16[80,1024]{1,0:T(8,128)(2,1)S...) custom-call(s32[8,64]{1,0:T(8,128)} %bitcast.14, s32[64]{0:T(128)} %counts_at.3, ...), custom_call_target="tpu_custom_call" | custom-call | tf_op jit(solution)/shard_map/stage/pallas_call | solution.py:313
  7.9 1.9 %collective-permute-start.1 = (bf16[80,1024]{1,0:T(8,128)(2,1)S(1)}, bf16[80,1024]{1,0:T(8,128)(2,1)S(1)}, u32[]{:S(2)}, u32[]{:S(2)}) collective-permute-start(bf16[80,1024]{1,0:T(8,128)(2,1)S(1)} %get-tuple-element.24), channel_id=1, source_target_pairs={{0,256},{8,264},{16,272},{24,280},{32,288},{40,296},{48,304},{56,3... | collective-permute-start | bytes 491528 | tf_op jit(solution)/shard_map/ppermute | solution.py:341
  9.8 0.0 collective-permute-done.hidden_other
  9.8 0.0 copy-start
  9.8 0.0 copy-start.1
  9.9 0.0 copy-start.2
  9.9 0.0 copy-start.3
  9.9 0.2 rank_partials.1
  10.1 15.4 %all_to_all.10.ranks = f32[8,8,128]{2,1,0:T(8,128)S(1)} all-to-all(f32[8,8,128]{2,1,0:T(8,128)S(1)} %rank_partials.1), channel_id=1, replica_groups={{7,6,5,4,3,2,1,0},{15,14,13,12,11,10,9,8},{23,22,21,20,19,18,17,16},{31..., dimensions={0} | all-to-all | bytes 65536 | tf_op jit(solution)/shard_map/all_to_all | solution.py:353
  25.5 0.0 collective-permute-done.1.parcel
  25.5 0.0 copy-done
  25.5 0.0 copy-done.1
  25.5 0.0 copy-done.2
  25.6 0.0 copy-done.3
  25.6 1.6 %attention.1 = (bf16[8,1024]{1,0:T(8,128)(2,1)S(1)}, f32[8,1024]{1,0:T(8,128)S(1)}, f32[4,8,128]{2,1,0:T(8,128)S(1)}, bf16[16,48,128]{2,1,0:T(8,128)(2,1)S(1)}) custom-call(s32[64]{0:T(128)} %counts_at.3, s32[4,64]{1,0:T(4,128)} %bitcast.11, s32[4,64]{1,0:T(4,128)} %bitcast.13, bf16[1,8,2,1024,128]{4,3,2,1,0:T(8,128)(2,1)S(1)} %copy-done.1, ...), custom_call_target="tpu_custom_call" | custom-call | tf_op jit(solution)/shard_map/attention/pallas_call | solution.py:355
  27.1 16.2 %all_to_all.11.sums = bf16[16,48,128]{2,1,0:T(8,128)(2,1)S(1)} all-to-all(bf16[16,48,128]{2,1,0:T(8,128)(2,1)S(1)} %get-tuple-element.26), channel_id=1, replica_groups={{7,6,5,4,3,2,1,0,263,262,261,260,259,258,257,256},{15,14,13,12,11,10,9,..., dimensions={0} | all-to-all | bytes 393216 | tf_op jit(solution)/shard_map/all_to_all | solution.py:381
  43.3 0.8 %deltas.1 = (bf16[8,1024]{1,0:T(8,128)(2,1)}, bf16[8,1024]{1,0:T(8,128)(2,1)}, bf16[8,1024]{1,0:T(8,128)(2,1)}, bf16[8,1024]{1,0:T(8,128)(2,1)}) custom-call(bf16[16,48,128]{2,1,0:T(8,128)(2,1)S(1)} %all_to_all.11.sums, bf16[1,4,4,16,1024]{4,3,2,1,0:T(8,128)(2,1)S(1)} %copy-done, bf16[80,1024]{1,0:T(8,128)(2,1)S(1)} %collective-permute-done.1.parcel, ...), custom_call_target="tpu_custom_call" | custom-call | tf_op jit(solution)/shard_map/deltas/pallas_call | solution.py:383
Async XLA Ops:
  0.6 9.2 %collective-permute-start = (bf16[8,1024]{1,0:T(8,128)(2,1)}, bf16[8,1024]{1,0:T(8,128)(2,1)S(1)}, u32[]{:S(2)}, u32[]{:S(2)}) collective-permute-start(bf16[8,1024]{1,0:T(8,128)(2,1)} %bitcast.9), channel_id=1, source_target_pairs={{0,256},{8,264},{16,272},{24,280},{32,288},{40,296},{48,304},{56,3... | collective-permute-start | bytes 49160 | tf_op jit(solution)/shard_map/ppermute | solution.py:342
  7.9 17.6 %collective-permute-start.1 = (bf16[80,1024]{1,0:T(8,128)(2,1)S(1)}, bf16[80,1024]{1,0:T(8,128)(2,1)S(1)}, u32[]{:S(2)}, u32[]{:S(2)}) collective-permute-start(bf16[80,1024]{1,0:T(8,128)(2,1)S(1)} %get-tuple-element.24), channel_id=1, source_target_pairs={{0,256},{8,264},{16,272},{24,280},{32,288},{40,296},{48,304},{56,3... | collective-permute-start | bytes 491528 | tf_op jit(solution)/shard_map/ppermute | solution.py:341
  9.8 15.7 %copy-start = (bf16[1,4,4,16,1024]{4,3,2,1,0:T(8,128)(2,1)S(1)}, bf16[1,4,4,16,1024]{4,3,2,1,0:T(8,128)(2,1)}, u32[]{:S(2)}) copy-start(bf16[1,4,4,16,1024]{4,3,2,1,0:T(8,128)(2,1)} %tables.3) | copy-start | bytes 1572868
  9.8 15.7 %copy-start.1 = (bf16[1,8,2,1024,128]{4,3,2,1,0:T(8,128)(2,1)S(1)}, bf16[1,8,2,1024,128]{4,3,2,1,0:T(8,128)(2,1)}, u32[]{:S(2)}) copy-start(bf16[1,8,2,1024,128]{4,3,2,1,0:T(8,128)(2,1)} %kv.1) | copy-start | bytes 12582916
  9.9 15.7 %copy-start.2 = (bf16[1,8,1024]{2,1,0:T(8,128)(2,1)S(1)}, bf16[1,8,1024]{2,1,0:T(8,128)(2,1)}, u32[]{:S(2)}) copy-start(bf16[1,8,1024]{2,1,0:T(8,128)(2,1)} %base1.1) | copy-start | bytes 49156
  9.9 15.7 %copy-start.3 = (bf16[1,8,2,128]{3,2,1,0:T(2,128)(2,1)S(1)}, bf16[1,8,2,128]{3,2,1,0:T(2,128)(2,1)}, u32[]{:S(2)}) copy-start(bf16[1,8,2,128]{3,2,1,0:T(2,128)(2,1)} %fresh1.1) | copy-start | bytes 12292

commit v10 on v9

--- a/solution.py
+++ b/solution.py
@@ -253,7 +253,9 @@
     delta = dot(jnp.concatenate([rank1, rank2], 0).astype(bf16), table)
     delta1_out[...] = delta[:slots].astype(bf16)
     delta2_out[...] = delta[slots:].astype(bf16)
-    sender = jnp.where(lower, peers, 0) + peers - 1 - lax.axis_index("tensor")
+    mine = lax.axis_index("tensor")
+    place = jnp.where(mine >= peers - 2, mine - (peers - 2), peers - 1 - mine)
+    sender = jnp.where(lower, peers, 0) + place
     moved = sums[sender, 2 * slots :, :].astype(f32)
     for h in range(heads):
         columns = slice(h * HEAD, (h + 1) * HEAD)
@@ -283,7 +285,8 @@
     half = inst_count // 2
     swap = [(i, i ^ half) for i in range(inst_count)]
     teams = [[i * peers + t for t in reversed(range(peers))] for i in range(inst_count)]
-    pairs = [teams[i] + teams[i + half] for i in range(half)]
+    swapped = [team[1::-1] + team[2:] for team in teams]
+    pairs = [swapped[i] + swapped[i + half] for i in range(half)]
     _, slots, width = query_first.shape
     _, pool, _, rank, _ = adapters.shape
     moves = move_from.shape[1]

time: 44.4 us -> 44.4 us (level)
  the two profiles are of different devices: /device:TPU:62 before, /device:TPU:52 now
where the time goes in v10:
time: 44.4 us; the launch traced here: 44.2 us
  blocking collectives  31.6 us (71%)
  starting transfers between devices  8.01 us (18%)
  Pallas kernels  3.76 us (8%)
  between operations  0.73 us (2%)
    all_to_all x1, blocking collectives, per_device(): lax.all_to_all(sums, ('inst', 'tensor'), 0, 0, axis_index_groups=pairs)  16.5 us
    all_to_all x1, blocking collectives, per_device(): lax.all_to_all(ranks, ('inst', 'tensor'), 0, 0, axis_index_groups=teams)  15.1 us
    ppermute x1, starting transfers between devices, per_device(): hidden_other = lax.ppermute(hidden_second[0], 'inst', swap)  6.09 us
    ppermute x1, starting transfers between devices, per_device(): parcel_other = lax.ppermute(parcel, 'inst', swap)  1.92 us
    pallas_call x1, Pallas kernels, per_device(): pl.pallas_call(attention_kernel, name='attention', out_shape=(shape((slot...  1.57 us
    pallas_call x1, Pallas kernels, per_device(): pl.pallas_call(stage_kernel, name='stage', out_shape=(shape((slots, width...  1.16 us
  transfers between devices with their start and end apart: 2, of which 0 were waited for; matrix products, arithmetic and copies ran while one was open for 0% of the time, Pallas kernels for 3%

profile of v10, /device:TPU:52, one launch (start us, length us, event | category | flops | bytes accessed | tf_op | source)
XLA Modules:
  0.0 44.2 jit_solution(16709781994381798474)
XLA Ops:
  0.6 6.1 %collective-permute-start = (bf16[8,1024]{1,0:T(8,128)(2,1)}, bf16[8,1024]{1,0:T(8,128)(2,1)S(1)}, u32[]{:S(2)}, u32[]{:S(2)}) collective-permute-start(bf16[8,1024]{1,0:T(8,128)(2,1)} %bitcast.9), channel_id=1, source_target_pairs={{0,256},{8,264},{16,272},{24,280},{32,288},{40,296},{48,304},{56,3... | collective-permute-start | bytes 49160 | tf_op jit(solution)/shard_map/ppermute | solution.py:345
  6.7 1.2 %stage.1 = (bf16[8,1024]{1,0:T(8,128)(2,1)S(1)}, bf16[8,2304]{1,0:T(8,128)(2,1)S(1)}, bf16[4,16,1024]{2,1,0:T(8,128)(2,1)S(1)}, bf16[80,1024]{1,0:T(8,128)(2,1)S...) custom-call(s32[8,64]{1,0:T(8,128)} %bitcast.14, s32[64]{0:T(128)} %counts_at.3, ...), custom_call_target="tpu_custom_call" | custom-call | tf_op jit(solution)/shard_map/stage/pallas_call | solution.py:316
  7.9 1.9 %collective-permute-start.1 = (bf16[80,1024]{1,0:T(8,128)(2,1)S(1)}, bf16[80,1024]{1,0:T(8,128)(2,1)S(1)}, u32[]{:S(2)}, u32[]{:S(2)}) collective-permute-start(bf16[80,1024]{1,0:T(8,128)(2,1)S(1)} %get-tuple-element.24), channel_id=1, source_target_pairs={{0,256},{8,264},{16,272},{24,280},{32,288},{40,296},{48,304},{56,3... | collective-permute-start | bytes 491528 | tf_op jit(solution)/shard_map/ppermute | solution.py:344
  9.8 0.0 collective-permute-done.hidden_other
  9.8 0.0 copy-start
  9.8 0.0 copy-start.1
  9.9 0.0 copy-start.2
  9.9 0.0 copy-start.3
  9.9 0.2 rank_partials.1
  10.1 15.1 %all_to_all.10.ranks = f32[8,8,128]{2,1,0:T(8,128)S(1)} all-to-all(f32[8,8,128]{2,1,0:T(8,128)S(1)} %rank_partials.1), channel_id=1, replica_groups={{7,6,5,4,3,2,1,0},{15,14,13,12,11,10,9,8},{23,22,21,20,19,18,17,16},{31..., dimensions={0} | all-to-all | bytes 65536 | tf_op jit(solution)/shard_map/all_to_all | solution.py:356
  25.2 0.0 collective-permute-done.1.parcel
  25.2 0.0 copy-done
  25.2 0.0 copy-done.1
  25.2 0.0 copy-done.2
  25.2 0.0 copy-done.3
  25.2 1.6 %attention.1 = (bf16[8,1024]{1,0:T(8,128)(2,1)S(1)}, f32[8,1024]{1,0:T(8,128)S(1)}, f32[4,8,128]{2,1,0:T(8,128)S(1)}, bf16[16,48,128]{2,1,0:T(8,128)(2,1)S(1)}) custom-call(s32[64]{0:T(128)} %counts_at.3, s32[4,64]{1,0:T(4,128)} %bitcast.11, s32[4,64]{1,0:T(4,128)} %bitcast.13, bf16[1,8,2,1024,128]{4,3,2,1,0:T(8,128)(2,1)S(1)} %copy-done.1, ...), custom_call_target="tpu_custom_call" | custom-call | tf_op jit(solution)/shard_map/attention/pallas_call | solution.py:358
  26.8 16.5 %all_to_all.11.sums = bf16[16,48,128]{2,1,0:T(8,128)(2,1)S(1)} all-to-all(bf16[16,48,128]{2,1,0:T(8,128)(2,1)S(1)} %get-tuple-element.26), channel_id=1, replica_groups={{6,7,5,4,3,2,1,0,262,263,261,260,259,258,257,256},{14,15,13,12,11,10,9,..., dimensions={0} | all-to-all | bytes 393216 | tf_op jit(solution)/shard_map/all_to_all | solution.py:384
  43.3 0.8 %deltas.1 = (bf16[8,1024]{1,0:T(8,128)(2,1)}, bf16[8,1024]{1,0:T(8,128)(2,1)}, bf16[8,1024]{1,0:T(8,128)(2,1)}, bf16[8,1024]{1,0:T(8,128)(2,1)}) custom-call(bf16[16,48,128]{2,1,0:T(8,128)(2,1)S(1)} %all_to_all.11.sums, bf16[1,4,4,16,1024]{4,3,2,1,0:T(8,128)(2,1)S(1)} %copy-done, bf16[80,1024]{1,0:T(8,128)(2,1)S(1)} %collective-permute-done.1.parcel, ...), custom_call_target="tpu_custom_call" | custom-call | tf_op jit(solution)/shard_map/deltas/pallas_call | solution.py:386
Async XLA Ops:
  0.6 9.2 %collective-permute-start = (bf16[8,1024]{1,0:T(8,128)(2,1)}, bf16[8,1024]{1,0:T(8,128)(2,1)S(1)}, u32[]{:S(2)}, u32[]{:S(2)}) collective-permute-start(bf16[8,1024]{1,0:T(8,128)(2,1)} %bitcast.9), channel_id=1, source_target_pairs={{0,256},{8,264},{16,272},{24,280},{32,288},{40,296},{48,304},{56,3... | collective-permute-start | bytes 49160 | tf_op jit(solution)/shard_map/ppermute | solution.py:345
  7.9 17.3 %collective-permute-start.1 = (bf16[80,1024]{1,0:T(8,128)(2,1)S(1)}, bf16[80,1024]{1,0:T(8,128)(2,1)S(1)}, u32[]{:S(2)}, u32[]{:S(2)}) collective-permute-start(bf16[80,1024]{1,0:T(8,128)(2,1)S(1)} %get-tuple-element.24), channel_id=1, source_target_pairs={{0,256},{8,264},{16,272},{24,280},{32,288},{40,296},{48,304},{56,3... | collective-permute-start | bytes 491528 | tf_op jit(solution)/shard_map/ppermute | solution.py:344
  9.8 15.4 %copy-start = (bf16[1,4,4,16,1024]{4,3,2,1,0:T(8,128)(2,1)S(1)}, bf16[1,4,4,16,1024]{4,3,2,1,0:T(8,128)(2,1)}, u32[]{:S(2)}) copy-start(bf16[1,4,4,16,1024]{4,3,2,1,0:T(8,128)(2,1)} %tables.3) | copy-start | bytes 1572868
  9.8 15.4 %copy-start.1 = (bf16[1,8,2,1024,128]{4,3,2,1,0:T(8,128)(2,1)S(1)}, bf16[1,8,2,1024,128]{4,3,2,1,0:T(8,128)(2,1)}, u32[]{:S(2)}) copy-start(bf16[1,8,2,1024,128]{4,3,2,1,0:T(8,128)(2,1)} %kv.1) | copy-start | bytes 12582916
  9.9 15.3 %copy-start.2 = (bf16[1,8,1024]{2,1,0:T(8,128)(2,1)S(1)}, bf16[1,8,1024]{2,1,0:T(8,128)(2,1)}, u32[]{:S(2)}) copy-start(bf16[1,8,1024]{2,1,0:T(8,128)(2,1)} %base1.1) | copy-start | bytes 49156
  9.9 15.3 %copy-start.3 = (bf16[1,8,2,128]{3,2,1,0:T(2,128)(2,1)S(1)}, bf16[1,8,2,128]{3,2,1,0:T(2,128)(2,1)}, u32[]{:S(2)}) copy-start(bf16[1,8,2,128]{3,2,1,0:T(2,128)(2,1)} %fresh1.1) | copy-start | bytes 12292
